TPU v7x, 32 devices: a whole 2x2x4 slice. The times are simulated.
32 devices in a mesh: dp: 8 (over z, y), mp: 4 (over x, core).
Axes of the slice: x: 2, y: 2, z: 4, core: 2. Of those that a mesh axis runs over, the one named last changes fastest.
Arguments:
- states: bfloat16 [8, 1024, 1024], P(None, 'dp', 'mp'), may hold values from -6 to 6
- memory: bfloat16 [8, 1024, 1024], P(None, 'dp', 'mp'), may hold values from -6 to 6
- cotangent: bfloat16 [8, 1024, 1024], P('dp', 'mp'), may hold values from -6 to 6
- lengths: int32 [8], replicated, may hold values from 512 to 1024, as said below
- memory_lengths: int32 [8], replicated, may hold values from 64 to 1024, as said below
- regroup_order: int32 [8], replicated, may hold values from 0 to 7, as said below
- attn_weights: float32 [8, 1024, 1024], P(None, 'dp', 'mp')
- ffn_weights: float32 [2, 1024, 4096], P(None, 'dp', 'mp')
- norm_params: float32 [8, 1024], P(None, 'dp')
- attn_mean: float32 [8, 1024, 1024], P(None, 'dp', 'mp'), may hold values from -0.00015258789 to 0.00015258789
- ffn_mean: float32 [2, 1024, 4096], P(None, 'dp', 'mp'), may hold values from -0.00015258789 to 0.00015258789
- norm_mean: float32 [8, 1024], P(None, 'dp'), may hold values from -0.00048828125 to 0.00048828125
- attn_square: float32 [8, 1024, 1024], P(None, 'dp', 'mp'), may hold values from 5.960465e-11 to 2.384186e-10
- ffn_square: float32 [2, 1024, 4096], P(None, 'dp', 'mp'), may hold values from 5.960465e-11 to 2.384186e-10
- norm_square: float32 [8, 1024], P(None, 'dp'), may hold values from 5.364418e-10 to 2.1457671e-09
- attn_average: float32 [8, 1024, 1024], P(None, 'dp', 'mp'), may hold values from -0.1875 to 0.1875
- ffn_average: float32 [2, 1024, 4096], P(None, 'dp', 'mp'), may hold values from -0.1875 to 0.1875
- norm_average: float32 [8, 1024], P(None, 'dp'), may hold values from -0.5 to 1.5
Outputs:
- layer_output: bfloat16 [8, 1024, 1024], P('dp', 'mp')
- states_grad: float32 [8, 1024, 1024], P(None, 'dp', 'mp')
- memory_grad: float32 [8, 1024, 1024], P(None, 'dp', 'mp')
- attn_updated: float32 [8, 1024, 1024], P(None, 'dp', 'mp')
- ffn_updated: float32 [2, 1024, 4096], P(None, 'dp', 'mp')
- norm_updated: float32 [8, 1024], P(None, 'dp')
- mean_attn: float32 [8, 1024, 1024], P(None, 'dp', 'mp')
- mean_ffn: float32 [2, 1024, 4096], P(None, 'dp', 'mp')
- mean_norm: float32 [8, 1024], P(None, 'dp')
- square_attn: float32 [8, 1024, 1024], P(None, 'dp', 'mp')
- square_ffn: float32 [2, 1024, 4096], P(None, 'dp', 'mp')
- square_norm: float32 [8, 1024], P(None, 'dp')
- average_attn: float32 [8, 1024, 1024], P(None, 'dp', 'mp')
- average_ffn: float32 [2, 1024, 4096], P(None, 'dp', 'mp')
- average_norm: float32 [8, 1024], P(None, 'dp')
- grad_norm: float32 [], replicated
Inputs may be any that keep to these rules, and one draw needn't show every extreme that they name: `lengths`: some utterance has exactly 1024 units. `memory_lengths`: some memory has exactly 1024 frames. `regroup_order`: every number from 0 to 7 appears once.
All inputs are finite; a program needn't handle non-finite values.
Results may differ from a plain program's by a relative error of at most 0.03.
The roundings to bfloat16 on the way count: a program that leaves them out, or rounds other values in their place, can miss the bound.
Values may be sent and summed in bfloat16 or wider, within the bound.
A program may use at most 192 MiB of HBM per device.

v0:
```python
import jax
import jax.numpy as jnp
from jax import lax
from jax.sharding import PartitionSpec as P

HD = 64
STEP = 10


EPSILON = 1e-05
NEGATIVE = -1000000000.0
BETA_FIRST = 0.9
BETA_SECOND = 0.999
ADAM_EPSILON = 1e-08
MATRIX_RATE = 0.05
NORM_RATE = 1.0
MATRIX_DECAY = 0.1
AVERAGING = 0.7
THRESHOLD = 1.0


def layer_norm(values, gains, biases):
    centered = values - jnp.mean(values, axis=-1, keepdims=True)
    variance = jnp.mean(centered * centered, axis=-1, keepdims=True)
    return centered * lax.rsqrt(variance + EPSILON) * gains + biases


def norm_back(values, gains, biases, upstream):
    result, pullback = jax.vjp(layer_norm, values, gains, biases)
    return pullback(upstream)


def gather_rows(values):
    return lax.all_gather(values, "mp", axis=1, tiled=True)


def scatter_rows(values):
    return lax.psum_scatter(values, "mp", scatter_dimension=1, tiled=True)


def usable_keys(offset, block_rows, key_total, limits, causal):
    key_pos = jnp.arange(key_total, dtype=jnp.int32)
    allowed = key_pos[None, None, :] < limits[:, None, None]
    if causal:
        query_pos = offset + jnp.arange(block_rows, dtype=jnp.int32)
        allowed = allowed & (key_pos[None, None, :] <= query_pos[None, :, None])
    return allowed


def block_scores(query_block, key_heads, allowed):
    scores = jnp.einsum(
        "uqhd,ukhd->uhqk", query_block, key_heads, preferred_element_type=jnp.float32
    ) * HD ** (-0.5)
    return jnp.where(allowed[:, None], scores, NEGATIVE)


def attend_forward(queries, key_set, value_set, limits, causal):
    utterances, query_total, local_width = queries.shape
    key_total = key_set.shape[1]
    local_heads = local_width // HD
    block_rows = min(512, query_total)
    blocks = query_total // block_rows
    key_heads = key_set.reshape(utterances, key_total, local_heads, HD)
    value_heads = value_set.reshape(utterances, key_total, local_heads, HD)

    def one_block(block_index):
        offset = block_index * block_rows
        query_block = lax.dynamic_slice_in_dim(queries, offset, block_rows, 1).reshape(
            utterances, block_rows, local_heads, HD
        )
        allowed = usable_keys(offset, block_rows, key_total, limits, causal)
        scores = block_scores(query_block, key_heads, allowed)
        row_max = jnp.max(scores, axis=-1, keepdims=True)
        raised = jnp.exp(scores - row_max)
        row_total = jnp.sum(raised, axis=-1, keepdims=True)
        weights = (raised / row_total).astype(jnp.bfloat16)
        mixed_rows = jnp.einsum(
            "uhqk,ukhd->uqhd", weights, value_heads, preferred_element_type=jnp.float32
        )
        return (
            mixed_rows.astype(jnp.bfloat16).reshape(utterances, block_rows, local_width),
            (row_max + jnp.log(row_total))[..., 0],
        )

    mixed_rows, logsum = lax.map(one_block, jnp.arange(blocks))
    return (jnp.moveaxis(mixed_rows, 0, 1).reshape(utterances, query_total, local_width), logsum)


def attend_backward(queries, key_set, value_set, limits, causal, logsum, upstream):
    utterances, query_total, local_width = queries.shape
    key_total = key_set.shape[1]
    local_heads = local_width // HD
    block_rows = min(512, query_total)
    blocks = query_total // block_rows
    key_heads = key_set.reshape(utterances, key_total, local_heads, HD)
    value_heads = value_set.reshape(utterances, key_total, local_heads, HD)

    def one_block(running, block_index):
        key_acc, value_acc = running
        offset = block_index * block_rows
        query_block = lax.dynamic_slice_in_dim(queries, offset, block_rows, 1).reshape(
            utterances, block_rows, local_heads, HD
        )
        grad_block = lax.dynamic_slice_in_dim(upstream, offset, block_rows, 1).reshape(
            utterances, block_rows, local_heads, HD
        )
        allowed = usable_keys(offset, block_rows, key_total, limits, causal)
        scores = block_scores(query_block, key_heads, allowed)
        weights = jnp.exp(scores - logsum[block_index][..., None])
        value_acc = value_acc + jnp.einsum(
            "uhqk,uqhd->ukhd",
            weights.astype(jnp.bfloat16),
            grad_block,
            preferred_element_type=jnp.float32,
        )
        grad_weights = jnp.einsum(
            "uqhd,ukhd->uhqk", grad_block, value_heads, preferred_element_type=jnp.float32
        )
        grad_scores = (
            weights * (grad_weights - jnp.sum(weights * grad_weights, axis=-1, keepdims=True))
        ).astype(jnp.bfloat16)
        grad_query = jnp.einsum(
            "uhqk,ukhd->uqhd", grad_scores, key_heads, preferred_element_type=jnp.float32
        ) * HD ** (-0.5)
        key_acc = key_acc + jnp.einsum(
            "uhqk,uqhd->ukhd", grad_scores, query_block, preferred_element_type=jnp.float32
        ) * HD ** (-0.5)
        return (
            (key_acc, value_acc),
            grad_query.astype(jnp.bfloat16).reshape(utterances, block_rows, local_width),
        )

    empty = jnp.zeros((utterances, key_total, local_heads, HD), jnp.float32)
    (key_acc, value_acc), grad_query = lax.scan(one_block, (empty, empty), jnp.arange(blocks))
    grad_query = jnp.moveaxis(grad_query, 0, 1).reshape(utterances, query_total, local_width)
    grad_key = key_acc.reshape(utterances, key_total, local_width).astype(jnp.bfloat16)
    grad_value = value_acc.reshape(utterances, key_total, local_width).astype(jnp.bfloat16)
    return (grad_query, grad_key, grad_value)


def adam_step(weight, moment, square, gradient, step_rate, weight_decay):
    moment_new = BETA_FIRST * moment + (1.0 - BETA_FIRST) * gradient
    square_new = BETA_SECOND * square + (1.0 - BETA_SECOND) * gradient * gradient
    moment_hat = moment_new / (1.0 - BETA_FIRST**STEP)
    square_hat = square_new / (1.0 - BETA_SECOND**STEP)
    updated = weight - step_rate * (
        moment_hat / (jnp.sqrt(square_hat) + ADAM_EPSILON) + weight_decay * weight
    )
    return (updated, moment_new, square_new)


def per_device(
    states,
    memory,
    cotangent,
    lengths,
    memory_lengths,
    regroup_order,
    attn_weights,
    ffn_weights,
    norm_params,
    attn_mean,
    ffn_mean,
    norm_mean,
    attn_square,
    ffn_square,
    norm_square,
    attn_average,
    ffn_average,
    norm_average,
):
    attn_full, ffn_full, norm_full = (
        lax.all_gather(attn_weights.astype(jnp.bfloat16), "dp", axis=1, tiled=True),
        lax.all_gather(ffn_weights.astype(jnp.bfloat16), "dp", axis=1, tiled=True),
        lax.all_gather(norm_params.astype(jnp.bfloat16), "dp", axis=1, tiled=True),
    )
    norm_values = norm_full.astype(jnp.float32)
    ordered_states = jnp.take(states, regroup_order, axis=0)
    ordered_memory = jnp.take(memory, regroup_order, axis=0)
    own_states, own_memory = (
        lax.all_to_all(
            lax.all_to_all(ordered_states, "dp", split_axis=0, concat_axis=1, tiled=True),
            "mp",
            split_axis=1,
            concat_axis=2,
            tiled=True,
        ),
        lax.all_to_all(
            lax.all_to_all(ordered_memory, "dp", split_axis=0, concat_axis=1, tiled=True),
            "mp",
            split_axis=1,
            concat_axis=2,
            tiled=True,
        ),
    )
    utterances = cotangent.shape[0]
    part_rows = cotangent.shape[1]
    data_index = lax.axis_index("dp")
    model_index = lax.axis_index("mp")
    owned = lax.dynamic_slice_in_dim(regroup_order, data_index * utterances, utterances)
    own_lengths = jnp.take(lengths, owned, axis=0)
    own_reach = jnp.take(memory_lengths, owned, axis=0)
    memory_all = lax.all_gather(own_memory, "mp", axis=1, tiled=True)
    resid_zero = own_states.astype(jnp.float32)
    inputs_first = gather_rows(
        layer_norm(resid_zero, norm_values[0], norm_values[4]).astype(jnp.bfloat16)
    )
    heads_first = jnp.einsum(
        "usd,jde->juse", inputs_first, attn_full[0:3], preferred_element_type=jnp.float32
    ).astype(jnp.bfloat16)
    mixed_self, logsum_self = attend_forward(
        heads_first[0], heads_first[1], heads_first[2], own_lengths, True
    )
    resid_one = resid_zero + scatter_rows(
        jnp.einsum("use,de->usd", mixed_self, attn_full[3], preferred_element_type=jnp.float32)
    )
    inputs_second = gather_rows(
        layer_norm(resid_one, norm_values[1], norm_values[5]).astype(jnp.bfloat16)
    )
    query_cross = jnp.einsum(
        "usd,de->use", inputs_second, attn_full[4], preferred_element_type=jnp.float32
    ).astype(jnp.bfloat16)
    memory_heads = jnp.einsum(
        "usd,jde->juse", memory_all, attn_full[5:7], preferred_element_type=jnp.float32
    ).astype(jnp.bfloat16)
    mixed_cross, logsum_cross = attend_forward(
        query_cross, memory_heads[0], memory_heads[1], own_reach, False
    )
    resid_two = resid_one + scatter_rows(
        jnp.einsum("use,de->usd", mixed_cross, attn_full[7], preferred_element_type=jnp.float32)
    )
    inputs_third = gather_rows(
        layer_norm(resid_two, norm_values[2], norm_values[6]).astype(jnp.bfloat16)
    )
    hidden = jnp.einsum(
        "usd,df->usf", inputs_third, ffn_full[0], preferred_element_type=jnp.float32
    )
    active = jax.nn.gelu(hidden).astype(jnp.bfloat16)
    resid_three = resid_two + scatter_rows(
        jnp.einsum("usf,df->usd", active, ffn_full[1], preferred_element_type=jnp.float32)
    )
    layer_output = layer_norm(resid_three, norm_values[3], norm_values[7]).astype(jnp.bfloat16)
    positions = model_index * part_rows + jnp.arange(part_rows, dtype=jnp.int32)
    live = positions[None, :] < own_lengths[:, None]
    seed_grad = jnp.where(live[:, :, None], cotangent.astype(jnp.float32), 0.0)
    grad_three, gain_final, bias_final = norm_back(
        resid_three, norm_values[3], norm_values[7], seed_grad
    )
    down_rows = gather_rows(grad_three.astype(jnp.bfloat16))
    grad_down = jnp.einsum("usd,usf->df", down_rows, active, preferred_element_type=jnp.float32)
    grad_active = jnp.einsum(
        "usd,df->usf", down_rows, ffn_full[1], preferred_element_type=jnp.float32
    )
    result, gelu_pull = jax.vjp(jax.nn.gelu, hidden)
    grad_hidden = gelu_pull(grad_active)[0].astype(jnp.bfloat16)
    grad_up = jnp.einsum(
        "usd,usf->df", inputs_third, grad_hidden, preferred_element_type=jnp.float32
    )
    grad_normed = scatter_rows(
        jnp.einsum("usf,df->usd", grad_hidden, ffn_full[0], preferred_element_type=jnp.float32)
    )
    step_back, gain_third, bias_third = norm_back(
        resid_two, norm_values[2], norm_values[6], grad_normed
    )
    grad_two = grad_three + step_back
    ffn_grad = jnp.stack([grad_up, grad_down])
    cross_rows = gather_rows(grad_two.astype(jnp.bfloat16))
    grad_out_cross = jnp.einsum(
        "usd,use->de", cross_rows, mixed_cross, preferred_element_type=jnp.float32
    )
    grad_mixed_cross = jnp.einsum(
        "usd,de->use", cross_rows, attn_full[7], preferred_element_type=jnp.float32
    ).astype(jnp.bfloat16)
    query_grad_cross, key_grad_cross, value_grad_cross = attend_backward(
        query_cross,
        memory_heads[0],
        memory_heads[1],
        own_reach,
        False,
        logsum_cross,
        grad_mixed_cross,
    )
    grad_query_map = jnp.einsum(
        "usd,use->de", inputs_second, query_grad_cross, preferred_element_type=jnp.float32
    )
    memory_heads_grad = jnp.stack([key_grad_cross, value_grad_cross])
    grad_memory_maps = jnp.einsum(
        "usd,juse->jde", memory_all, memory_heads_grad, preferred_element_type=jnp.float32
    )
    normed_part = jnp.einsum(
        "use,de->usd", query_grad_cross, attn_full[4], preferred_element_type=jnp.float32
    )
    memory_part = jnp.einsum(
        "juse,jde->usd", memory_heads_grad, attn_full[5:7], preferred_element_type=jnp.float32
    )
    grad_normed_cross, memory_rows_grad = (
        lax.psum_scatter(
            normed_part.astype(jnp.bfloat16), "mp", scatter_dimension=1, tiled=True
        ).astype(jnp.float32),
        lax.psum_scatter(
            memory_part.astype(jnp.bfloat16), "mp", scatter_dimension=1, tiled=True
        ).astype(jnp.float32),
    )
    step_back, gain_second, bias_second = norm_back(
        resid_one, norm_values[1], norm_values[5], grad_normed_cross
    )
    grad_one = grad_two + step_back
    cross_grad = jnp.concatenate(
        [grad_query_map[None], grad_memory_maps, grad_out_cross[None]], axis=0
    )
    self_rows = gather_rows(grad_one.astype(jnp.bfloat16))
    grad_out_self = jnp.einsum(
        "usd,use->de", self_rows, mixed_self, preferred_element_type=jnp.float32
    )
    grad_mixed_self = jnp.einsum(
        "usd,de->use", self_rows, attn_full[3], preferred_element_type=jnp.float32
    ).astype(jnp.bfloat16)
    query_grad, key_grad, value_grad = attend_backward(
        heads_first[0],
        heads_first[1],
        heads_first[2],
        own_lengths,
        True,
        logsum_self,
        grad_mixed_self,
    )
    heads_grad = jnp.stack([query_grad, key_grad, value_grad])
    grad_in_maps = jnp.einsum(
        "usd,juse->jde", inputs_first, heads_grad, preferred_element_type=jnp.float32
    )
    grad_normed_self = scatter_rows(
        jnp.einsum("juse,jde->usd", heads_grad, attn_full[0:3], preferred_element_type=jnp.float32)
    )
    step_back, gain_first, bias_first = norm_back(
        resid_zero, norm_values[0], norm_values[4], grad_normed_self
    )
    grad_zero = grad_one + step_back
    self_grad = jnp.concatenate([grad_in_maps, grad_out_self[None]], axis=0)
    norm_grad = jnp.stack(
        [
            gain_first,
            gain_second,
            gain_third,
            gain_final,
            bias_first,
            bias_second,
            bias_third,
            bias_final,
        ]
    )
    norm_grad = lax.psum(norm_grad.astype(jnp.bfloat16), "mp").astype(jnp.float32)
    attn_shard, ffn_shard, norm_shard = (
        lax.psum_scatter(
            jnp.concatenate([self_grad, cross_grad], axis=0).astype(jnp.bfloat16),
            "dp",
            scatter_dimension=1,
            tiled=True,
        ).astype(jnp.float32),
        lax.psum_scatter(
            ffn_grad.astype(jnp.bfloat16), "dp", scatter_dimension=1, tiled=True
        ).astype(jnp.float32),
        lax.psum_scatter(
            norm_grad.astype(jnp.bfloat16), "dp", scatter_dimension=1, tiled=True
        ).astype(jnp.float32),
    )
    back_states, back_memory = (
        lax.all_to_all(
            lax.all_to_all(
                grad_zero.astype(jnp.bfloat16), "mp", split_axis=2, concat_axis=1, tiled=True
            ),
            "dp",
            split_axis=1,
            concat_axis=0,
            tiled=True,
        ).astype(grad_zero.dtype),
        lax.all_to_all(
            lax.all_to_all(
                memory_rows_grad.astype(jnp.bfloat16), "mp", split_axis=2, concat_axis=1, tiled=True
            ),
            "dp",
            split_axis=1,
            concat_axis=0,
            tiled=True,
        ).astype(memory_rows_grad.dtype),
    )
    inverse = jnp.argsort(regroup_order)
    states_grad = jnp.take(back_states, inverse, axis=0)
    memory_grad = jnp.take(back_memory, inverse, axis=0)
    local_squares = (
        jnp.sum(attn_shard * attn_shard)
        + jnp.sum(ffn_shard * ffn_shard)
        + jnp.sum(norm_shard * norm_shard) / lax.axis_size("mp")
    )
    grad_norm = jnp.sqrt(lax.psum(local_squares, ("dp", "mp")))
    clip_scale = jnp.minimum(1.0, THRESHOLD / (grad_norm + 1e-06))
    attn_updated, mean_attn, square_attn = adam_step(
        attn_weights, attn_mean, attn_square, clip_scale * attn_shard, MATRIX_RATE, MATRIX_DECAY
    )
    ffn_updated, mean_ffn, square_ffn = adam_step(
        ffn_weights, ffn_mean, ffn_square, clip_scale * ffn_shard, MATRIX_RATE, MATRIX_DECAY
    )
    norm_updated, mean_norm, square_norm = adam_step(
        norm_params, norm_mean, norm_square, clip_scale * norm_shard, NORM_RATE, 0.0
    )
    average_attn = AVERAGING * attn_average + (1.0 - AVERAGING) * attn_updated
    average_ffn = AVERAGING * ffn_average + (1.0 - AVERAGING) * ffn_updated
    average_norm = AVERAGING * norm_average + (1.0 - AVERAGING) * norm_updated
    return (
        layer_output,
        states_grad,
        memory_grad,
        attn_updated,
        ffn_updated,
        norm_updated,
        mean_attn,
        mean_ffn,
        mean_norm,
        square_attn,
        square_ffn,
        square_norm,
        average_attn,
        average_ffn,
        average_norm,
        grad_norm,
    )


def solution(mesh):
    return jax.shard_map(
        per_device,
        mesh=mesh,
        in_specs=(
            P(None, "dp", "mp"),
            P(None, "dp", "mp"),
            P("dp", "mp", None),
            P(),
            P(),
            P(),
            P(None, "dp", "mp"),
            P(None, "dp", "mp"),
            P(None, "dp"),
            P(None, "dp", "mp"),
            P(None, "dp", "mp"),
            P(None, "dp"),
            P(None, "dp", "mp"),
            P(None, "dp", "mp"),
            P(None, "dp"),
            P(None, "dp", "mp"),
            P(None, "dp", "mp"),
            P(None, "dp"),
        ),
        out_specs=(
            P("dp", "mp", None),
            P(None, "dp", "mp"),
            P(None, "dp", "mp"),
            P(None, "dp", "mp"),
            P(None, "dp", "mp"),
            P(None, "dp"),
            P(None, "dp", "mp"),
            P(None, "dp", "mp"),
            P(None, "dp"),
            P(None, "dp", "mp"),
            P(None, "dp", "mp"),
            P(None, "dp"),
            P(None, "dp", "mp"),
            P(None, "dp", "mp"),
            P(None, "dp"),
            P(),
        ),
        check_vma=False,
    )
```

profile of v0, /device:TPU:0, one launch (start us, length us, event | category | flops | bytes accessed | tf_op | source)
XLA Modules:
  0.0 1193.1 jit_solution(12054989271595000062)
XLA Ops:
  14.0 21.6 %all_to_all.105 = bf16[8,128,256]{2,1,0:T(8,128)(2,1)S(1)} all-to-all(bf16[8,128,256]{2,1,0:T(8,128)(2,1)S(1)} %get-tuple-element.698), channel_id=1, replica_groups=mesh['dp'=8,'mp'=4] {'dp'}, dimensions={0} | all-to-all | bytes 1048576 | tf_op jit(solution)/shard_map/all_to_all | solution.py:182
  45.3 26.0 %all_gather.30 = bf16[8,1024]{1,0:T(8,128)(2,1)S(1)} all-gather(bf16[8,128]{1,0:T(8,128)(2,1)S(1)} %convert_element_type.322), channel_id=1, replica_groups=mesh['dp'=8,'mp'=4] {'dp'}, dimensions={1}, use_global_device_ids=true | all-gather | bytes 18432 | tf_op jit(solution)/shard_map/all_gather | solution.py:175
  81.1 14.0 %all-gather.10.cloned.1.call-done = bf16[1,1024,1024]{2,1,0:T(8,128)(2,1)} async-done(((bf16[1,256,1024]{2,1,0:T(8,128)(2,1)}), bf16[1,1024,1024]{2,1,0:T(8,128)(2,1)}) %all-gather.10.cloned.1.call-update) | async-done | bytes 2097168 | tf_op jit(solution)/shard_map/all_gather | solution.py:34
  95.0 77.7 %all-gather.12.cloned.1.call-done = bf16[8,1024,256]{1,2,0:T(8,128)(2,1)} async-done(((bf16[8,128,256]{1,2,0:T(8,128)(2,1)}), bf16[8,1024,256]{1,2,0:T(8,128)(2,1)}) %all-gather.12.cloned.1.call-update) | async-done | bytes 4194320 | tf_op jit(solution)/shard_map/all_gather | solution.py:173
  172.7 3.9 fusion.110
  177.6 19.1 %while.56 = (s32[]{:T(128)}, bf16[2,1,512,256]{3,2,0,1:T(8,128)(2,1)}, f32[2,1,4,512]{3,2,1,0:T(4,128)S(1)}, s32[1]{0:T(128)}, s32[2]{0:T(128)S(1)}, /*index=5*/...) while((s32[]{:T(128)}, ...), condition=%wide.region_6.8_spmd, body=%wide.region_3.7_spmd.sunk | while | flops 563215872 | bytes 30480588 | solution.py:85
  197.3 3.9 convolution_bitcast_fusion.4
  201.3 17.2 %all_to_all.106 = bf16[8,128,256]{2,1,0:T(8,128)(2,1)S(1)} all-to-all(bf16[8,128,256]{2,1,0:T(8,128)(2,1)S(1)} %copy-done.26), channel_id=1, replica_groups=mesh['dp'=8,'mp'=4] {'dp'}, dimensions={0} | all-to-all | bytes 1048576 | tf_op jit(solution)/shard_map/all_to_all | solution.py:189
  223.3 17.3 %all_to_all.107 = bf16[4,2,32768]{2,1,0:T(2,128)(2,1)S(1)} all-to-all(bf16[4,2,32768]{2,1,0:T(2,128)(2,1)S(1)} %reshape.1288), channel_id=1, replica_groups=mesh['dp'=8,'mp'=4] {'mp'}, dimensions={0} | all-to-all | bytes 1048576 | tf_op jit(solution)/shard_map/all_to_all | solution.py:188
  242.4 7.3 reduce-scatter.15.cloned.1.call-done
  253.8 20.6 %all-gather.16.cloned.1.call-done = bf16[1,1024,1024]{2,1,0:T(8,128)(2,1)} async-done(((bf16[1,256,1024]{2,1,0:T(8,128)(2,1)}), bf16[1,1024,1024]{2,1,0:T(8,128)(2,1)}) %all-gather.16.cloned.1.call-update) | async-done | bytes 2097168 | tf_op jit(solution)/shard_map/all_gather | solution.py:203
  277.6 21.5 %all-gather.14.cloned.1.call-done = bf16[1,1024,1024]{2,1,0:T(8,128)(2,1)} async-done(((bf16[1,256,1024]{2,1,0:T(8,128)(2,1)}), bf16[1,1024,1024]{2,1,0:T(8,128)(2,1)}) %all-gather.14.cloned.1.call-update) | async-done | bytes 2097168 | tf_op jit(solution)/shard_map/all_gather | solution.py:34
  304.4 16.2 %while.57 = (s32[]{:T(128)}, bf16[2,1,512,256]{3,2,0,1:T(8,128)(2,1)}, f32[2,1,4,512]{3,2,1,0:T(4,128)S(1)}, s32[1]{0:T(128)}, s32[2]{0:T(128)S(1)}, /*index=5*/...) while((s32[]{:T(128)}, ...), condition=%wide.region_13.15_spmd, body=%wide.region_10.14_spmd.sunk | while | flops 562166784 | bytes 28381384 | solution.py:85
  320.6 4.1 convolution_bitcast_fusion.3
  326.9 42.4 %reduce-scatter.17.cloned.1.call-done = f32[1,256,1024]{2,1,0:T(8,128)} async-done(((f32[1,1024,1024]{2,1,0:T(8,128)}), f32[1,256,1024]{2,1,0:T(8,128)}) %reduce-scatter.17.cloned.1.call-update) | async-done | bytes 1048592 | tf_op jit(solution)/shard_map/reduce_scatter | solution.py:38
  372.2 73.3 %all-gather.20.cloned.1.call-done = bf16[2,1024,1024]{2,1,0:T(8,128)(2,1)} async-done(((bf16[2,128,1024]{2,1,0:T(8,128)(2,1)}), bf16[2,1024,1024]{2,1,0:T(8,128)(2,1)}) %all-gather.20.cloned.1.call-update) | async-done | bytes 4194320 | tf_op jit(solution)/shard_map/all_gather | solution.py:174
  445.5 23.0 %all-gather.18.cloned.1.call-done = bf16[1,1024,1024]{2,1,0:T(8,128)(2,1)} async-done(((bf16[1,256,1024]{2,1,0:T(8,128)(2,1)}), bf16[1,1024,1024]{2,1,0:T(8,128)(2,1)}) %all-gather.18.cloned.1.call-update) | async-done | bytes 2097168 | tf_op jit(solution)/shard_map/all_gather | solution.py:34
  468.6 4.7 fusion.83
  475.2 4.6 convolution_bitcast_fusion.2
  480.3 44.2 %reduce-scatter.19.cloned.1.call-done = f32[1,256,1024]{2,1,0:T(8,128)} async-done(((f32[1,1024,1024]{2,1,0:T(8,128)}), f32[1,256,1024]{2,1,0:T(8,128)}) %reduce-scatter.19.cloned.1.call-update) | async-done | bytes 1048592 | tf_op jit(solution)/shard_map/reduce_scatter | solution.py:38
  532.7 22.7 %all-gather.22.cloned.1.call-done = bf16[1,1024,1024]{2,1,0:T(8,128)(2,1)} async-done(((bf16[1,256,1024]{2,1,0:T(8,128)(2,1)}), bf16[1,1024,1024]{2,1,0:T(8,128)(2,1)}) %all-gather.22.cloned.1.call-update) | async-done | bytes 2097168 | tf_op jit(solution)/shard_map/all_gather | solution.py:34
  555.4 8.0 fusion.66
  564.7 4.3 convolution_bitcast_fusion.1
  569.2 44.6 %reduce-scatter.21.cloned.1.call-done = f32[1,256,1024]{2,1,0:T(8,128)} async-done(((f32[1,1024,1024]{2,1,0:T(8,128)}), f32[1,256,1024]{2,1,0:T(8,128)}) %reduce-scatter.21.cloned.1.call-update) | async-done | bytes 1048592 | tf_op jit(solution)/shard_map/reduce_scatter | solution.py:38
  619.2 22.5 %all-gather.24.cloned.1.call-done = bf16[1,1024,1024]{2,1,0:T(8,128)(2,1)} async-done(((bf16[1,256,1024]{2,1,0:T(8,128)(2,1)}), bf16[1,1024,1024]{2,1,0:T(8,128)(2,1)}) %all-gather.24.cloned.1.call-update) | async-done | bytes 2097168 | tf_op jit(solution)/shard_map/all_gather | solution.py:34
  645.7 31.8 %while.58 = (s32[]{:T(128)}, f32[1,1024,4,64]{1,3,2,0:T(8,128)S(1)}, f32[1,1024,4,64]{1,3,2,0:T(8,128)}, bf16[2,1,512,256]{3,2,0,1:T(8,128)(2,1)}, s32[2]{0:T(12...) while((s32[]{:T(128)}, ...), condition=%wide.region_27.29_spmd.clone, body=%wide.region_25.28_spmd.clone.sunk | while | flops 1375206400 | bytes 81064280 | solution.py:134
  681.0 31.6 %reduce-scatter.23.cloned.1.call-done = bf16[1,256,1024]{2,1,0:T(8,128)(2,1)} async-done(((bf16[1,1024,1024]{2,1,0:T(8,128)(2,1)}), bf16[1,256,1024]{2,1,0:T(8,128)(2,1)}) %reduce-scatter.23.cloned.1.call-update) | async-done | bytes 524304 | tf_op jit(solution)/shard_map/reduce_scatter | solution.py:297
  721.4 4.1 fusion.107
  725.6 16.5 %all-gather.26.cloned.1.call-done = bf16[1,1024,1024]{2,1,0:T(8,128)(2,1)} async-done(((bf16[1,256,1024]{2,1,0:T(8,128)(2,1)}), bf16[1,1024,1024]{2,1,0:T(8,128)(2,1)}) %all-gather.26.cloned.1.call-update) | async-done | bytes 2097168 | tf_op jit(solution)/shard_map/all_gather | solution.py:34
  746.2 35.5 %while.59 = (s32[]{:T(128)}, f32[1,1024,4,64]{1,3,2,0:T(8,128)S(1)}, f32[1,1024,4,64]{1,3,2,0:T(8,128)}, bf16[2,1,512,256]{3,2,0,1:T(8,128)(2,1)}, s32[2]{0:T(12...) while((s32[]{:T(128)}, ...), condition=%wide.region_33.35_spmd.clone, body=%wide.region_31.34_spmd.clone.sunk | while | flops 1376255488 | bytes 83163480 | solution.py:134
  783.4 5.2 convolution_bitcast_fusion
  788.9 4.8 convert_bitcast_fusion.1
  798.8 4.9 bitcast_dynamic-update-slice_fusion.2
  811.6 7.0 copy.216
  818.5 5.7 copy.238
  831.5 4.0 all-to-all-start.6
  847.0 5.7 reduce.45
  854.7 5.6 all-to-all-start.7
  871.9 16.7 %all-to-all-done.7 = bf16[8,2,16384]{2,1,0:T(2,128)(2,1)} async-done(((bf16[8,2,16384]{2,1,0:T(2,128)(2,1)}), bf16[8,2,16384]{2,1,0:T(2,128)(2,1)}, u32[]{:S(2)}, u32[]{:S(2)}) %all-to-all-start.7) | async-done | bytes 524320 | tf_op jit(solution)/shard_map/all_to_all | solution.py:376
  892.1 44.3 %reduce-scatter.29.cloned.1.call-done = bf16[2,128,1024]{2,1,0:T(8,128)(2,1)} async-done(((bf16[2,1024,1024]{2,1,0:T(8,128)(2,1)}), bf16[2,128,1024]{2,1,0:T(8,128)(2,1)}) %reduce-scatter.29.cloned.1.call-update) | async-done | bytes 524304 | tf_op jit(solution)/shard_map/reduce_scatter | solution.py:359
  941.7 85.8 %reduce-scatter.31.cloned.1.call-done = bf16[128,2048]{1,0:T(8,128)(2,1)} async-done(((bf16[1024,2048]{1,0:T(8,128)(2,1)}), bf16[128,2048]{1,0:T(8,128)(2,1)}) %reduce-scatter.31.cloned.1.call-update) | async-done | bytes 524304
  1031.3 61.6 %reduce-scatter.33.cloned.1.call-done = bf16[128,8]{1,0:T(8,128)(2,1)} async-done(((bf16[1024,8]{1,0:T(8,128)(2,1)}), bf16[128,8]{1,0:T(8,128)(2,1)}) %reduce-scatter.33.cloned.1.call-update) | async-done | bytes 2064
  1093.7 5.7 psum.16
  1101.4 40.6 %psum.15 = f32[]{:T(128)} all-reduce(f32[]{:T(128)S(6)} %add.360), channel_id=1, replica_groups=mesh['dp'=8,'mp'=4] {'dp','mp'}, use_global_device_ids=true, to_apply=%region_54.57 | all-reduce | flops 1 | bytes 8 | tf_op jit(solution)/shard_map/psum | solution.py:394
  1149.7 4.8 reduce.47
  1155.4 4.7 all-to-all-start.5
  1160.1 4.5 multiply_add_fusion.1
  1175.5 4.6 multiply_add_fusion
  (487 shorter events, 259.3 us)
Async XLA Ops:
  13.0 32.2 %copy-start.57 = (f32[8,128]{1,0:T(8,128)S(1)}, f32[8,128]{1,0:T(8,128)}, u32[]{:S(2)}) copy-start(f32[8,128]{1,0:T(8,128)} %param.38) | copy-start | bytes 12292
  41.7 30.2 %all-to-all-start.1 = ((bf16[4,2,32768]{2,1,0:T(2,128)(2,1)}), bf16[4,2,32768]{2,1,0:T(2,128)(2,1)S(1)}, u32[]{:S(2)}, u32[]{:S(2)}) async-start(bf16[4,2,32768]{2,1,0:T(2,128)(2,1)} %reshape.1286), calls=%async_computation.1 | async-start | bytes 1048576 | tf_op jit(solution)/shard_map/all_to_all | solution.py:181
  45.2 49.8 %all-gather.10.cloned.1.call-start = ((), (), s32[]{:S(2)}) async-start(), calls=%async_computation.18 | async-start | bytes 2621440 | tf_op jit(solution)/shard_map/all_gather | solution.py:34
  71.9 179.5 %copy-start.43 = (f32[1,1024]{1,0:T(1,128)}, f32[1,1024]{1,0:T(1,128)S(1)}, u32[]{:S(2)}) copy-start(f32[1,1024]{1,0:T(1,128)S(1)} %get-tuple-element.691) | copy-start | bytes 12292
  72.9 176.8 %copy-start.4 = (f32[1,4,32,8,256]{4,3,1,2,0:T(8,128)}, f32[1,4,32,8,256]{4,3,1,2,0:T(8,128)S(1)}, u32[]{:S(2)}) copy-start(f32[1,4,32,8,256]{4,3,1,2,0:T(8,128)S(1)} %copy.236) | copy-start | bytes 3145732
  74.3 98.4 %all-gather.12.cloned.1.call-start = ((), (), s32[]{:S(2)}) async-start(), calls=%async_computation.19 | async-start | bytes 4718592 | tf_op jit(solution)/shard_map/all_gather | solution.py:173
  76.0 96.7 %copy-start.17 = (f32[8,128,256]{1,2,0:T(8,128)}, f32[8,128,256]{1,2,0:T(8,128)S(1)}, u32[]{:S(2)}) copy-start(f32[8,128,256]{1,2,0:T(8,128)S(1)} %copy.172) | copy-start | bytes 3145732
  77.0 172.7 %reduce-scatter.15.cloned.1.call-start = ((), (), s32[]{:S(2)}) async-start(), calls=%async_computation.20 | async-start | bytes 5242880 | tf_op jit(solution)/shard_map/reduce_scatter | solution.py:38
  201.3 73.1 %all-gather.16.cloned.1.call-start = ((), (), s32[]{:S(2)}) async-start(), calls=%async_computation.22 | async-start | bytes 2621440 | tf_op jit(solution)/shard_map/all_gather | solution.py:203
  242.2 56.9 %all-gather.14.cloned.1.call-start = ((), (), s32[]{:S(2)}) async-start(), calls=%async_computation.21 | async-start | bytes 2621440 | tf_op jit(solution)/shard_map/all_gather | solution.py:34
  251.1 118.2 %copy-start.6 = (f32[1,256,1024]{2,1,0:T(8,128)}, f32[1,256,1024]{2,1,0:T(8,128)S(1)}, u32[]{:S(2)}) copy-start(f32[1,256,1024]{2,1,0:T(8,128)S(1)} %get-tuple-element.672) | copy-start | bytes 3145732
  251.1 23.3 %copy-start.47 = (f32[256]{0:T(256)}, f32[256]{0:T(256)S(1)}, u32[]{:S(2)}) copy-start(f32[256]{0:T(256)S(1)} %broadcast_multiply_fusion.2) | copy-start | bytes 3076
  251.4 23.0 %copy-start.63 = (f32[256]{0:T(256)}, f32[256]{0:T(256)S(1)}, u32[]{:S(2)}) copy-start(f32[256]{0:T(256)S(1)} %multiply_reduce_fusion.10) | copy-start | bytes 3076
  251.4 23.0 %copy-start.51 = (f32[256]{0:T(256)}, f32[256]{0:T(256)S(1)}, u32[]{:S(2)}) copy-start(f32[256]{0:T(256)S(1)} %fusion.197) | copy-start | bytes 3076
  252.5 116.8 %reduce-scatter.17.cloned.1.call-start = ((), (), s32[]{:S(2)}) async-start(), calls=%async_computation.23 | async-start | bytes 5242880 | tf_op jit(solution)/shard_map/reduce_scatter | solution.py:38
  324.7 46.4 %copy-start.45 = (f32[1,1024]{1,0:T(1,128)S(1)}, f32[1,1024]{1,0:T(1,128)}, u32[]{:S(2)}) copy-start(f32[1,1024]{1,0:T(1,128)} %get-tuple-element.689) | copy-start | bytes 12292
  324.7 46.4 %copy-start.56 = (f32[1,1024]{1,0:T(1,128)S(1)}, f32[1,1024]{1,0:T(1,128)}, u32[]{:S(2)}) copy-start(f32[1,1024]{1,0:T(1,128)} %get-tuple-element.690) | copy-start | bytes 12292
  324.7 120.8 %all-gather.20.cloned.1.call-start = ((), (), s32[]{:S(2)}) async-start(), calls=%async_computation.25 | async-start | bytes 4718592 | tf_op jit(solution)/shard_map/all_gather | solution.py:174
  326.9 141.7 %all-gather.18.cloned.1.call-start = ((), (), s32[]{:S(2)}) async-start(), calls=%async_computation.24 | async-start | bytes 2621440 | tf_op jit(solution)/shard_map/all_gather | solution.py:34
  372.1 152.4 %reduce-scatter.19.cloned.1.call-start = ((), (), s32[]{:S(2)}) async-start(), calls=%async_computation.26 | async-start | bytes 5242880 | tf_op jit(solution)/shard_map/reduce_scatter | solution.py:38
  479.8 46.4 %copy-start.46 = (f32[1,1024]{1,0:T(1,128)S(1)}, f32[1,1024]{1,0:T(1,128)}, u32[]{:S(2)}) copy-start(f32[1,1024]{1,0:T(1,128)} %get-tuple-element.687) | copy-start | bytes 12292
  479.8 48.5 %copy-start.55 = (f32[1,1024]{1,0:T(1,128)S(1)}, f32[1,1024]{1,0:T(1,128)}, u32[]{:S(2)}) copy-start(f32[1,1024]{1,0:T(1,128)} %get-tuple-element.688) | copy-start | bytes 12292
  479.8 75.5 %all-gather.22.cloned.1.call-start = ((), (), s32[]{:S(2)}) async-start(), calls=%async_computation.27 | async-start | bytes 2621440 | tf_op jit(solution)/shard_map/all_gather | solution.py:34
  532.6 81.1 %reduce-scatter.21.cloned.1.call-start = ((), (), s32[]{:S(2)}) async-start(), calls=%async_computation.28 | async-start | bytes 5242880 | tf_op jit(solution)/shard_map/reduce_scatter | solution.py:38
  569.1 48.5 %copy-start.20 = (f32[1,256,1024]{2,1,0:T(8,128)S(1)}, f32[1,256,1024]{2,1,0:T(8,128)}, u32[]{:S(2)}) copy-start(f32[1,256,1024]{2,1,0:T(8,128)} %copy-done.19) | copy-start | bytes 3145732
  569.1 72.6 %all-gather.24.cloned.1.call-start = ((), (), s32[]{:S(2)}) async-start(), calls=%async_computation.29 | async-start | bytes 2621440 | tf_op jit(solution)/shard_map/all_gather | solution.py:34
  618.9 26.8 %copy-start.13 = (bf16[1,1024,256]{1,2,0:T(8,128)(2,1)S(1)}, bf16[1,1024,256]{1,2,0:T(8,128)(2,1)}, u32[]{:S(2)}) copy-start(bf16[1,1024,256]{1,2,0:T(8,128)(2,1)} %copy-done.12) | copy-start | bytes 1572868
  619.0 93.6 %reduce-scatter.23.cloned.1.call-start = ((), (), s32[]{:S(2)}) async-start(), calls=%async_computation.30 | async-start | bytes 2621440 | tf_op jit(solution)/shard_map/reduce_scatter | solution.py:297
  677.5 35.0 %copy-start.7 = (f32[1,256,1024]{2,1,0:T(8,128)S(1)}, f32[1,256,1024]{2,1,0:T(8,128)}, u32[]{:S(2)}) copy-start(f32[1,256,1024]{2,1,0:T(8,128)} %copy-done.6) | copy-start | bytes 3145732
  677.5 35.0 %copy-start.44 = (f32[1,1024]{1,0:T(1,128)S(1)}, f32[1,1024]{1,0:T(1,128)}, u32[]{:S(2)}) copy-start(f32[1,1024]{1,0:T(1,128)} %copy-done.43) | copy-start | bytes 12292
  677.5 35.0 %copy-start.48 = (f32[256]{0:T(256)S(1)}, f32[256]{0:T(256)}, u32[]{:S(2)}) copy-start(f32[256]{0:T(256)} %copy-done.47) | copy-start | bytes 3076
  677.5 35.0 %copy-start.52 = (f32[256]{0:T(256)S(1)}, f32[256]{0:T(256)}, u32[]{:S(2)}) copy-start(f32[256]{0:T(256)} %copy-done.51) | copy-start | bytes 3076
  677.5 37.1 %copy-start.64 = (f32[256]{0:T(256)S(1)}, f32[256]{0:T(256)}, u32[]{:S(2)}) copy-start(f32[256]{0:T(256)} %copy-done.63) | copy-start | bytes 3076
  681.0 61.1 %all-gather.26.cloned.1.call-start = ((), (), s32[]{:S(2)}) async-start(), calls=%async_computation.31 | async-start | bytes 2621440 | tf_op jit(solution)/shard_map/all_gather | solution.py:34
  719.4 104.9 %reduce-scatter.27.cloned.1.call-start = ((), (), s32[]{:S(2)}) async-start(), calls=%async_computation.33 | async-start | bytes 2621440 | tf_op jit(solution)/shard_map/reduce_scatter | solution.py:300
  725.5 20.7 %copy-start.3 = (bf16[1,1024,4,64]{1,3,2,0:T(8,128)(2,1)S(1)}, bf16[1,1024,4,64]{1,3,2,0:T(8,128)(2,1)}, u32[]{:S(2)}) copy-start(bf16[1,1024,4,64]{1,3,2,0:T(8,128)(2,1)} %copy-done.2) | copy-start | bytes 1572868
  725.5 20.7 %copy-start.9 = (bf16[1,1024,4,64]{1,3,2,0:T(8,128)(2,1)S(1)}, bf16[1,1024,4,64]{1,3,2,0:T(8,128)(2,1)}, u32[]{:S(2)}) copy-start(bf16[1,1024,4,64]{1,3,2,0:T(8,128)(2,1)} %copy-done.8) | copy-start | bytes 1572868
  725.5 20.7 %copy-start.11 = (bf16[1,1024,256]{1,2,0:T(8,128)(2,1)S(1)}, bf16[1,1024,256]{1,2,0:T(8,128)(2,1)}, u32[]{:S(2)}) copy-start(bf16[1,1024,256]{1,2,0:T(8,128)(2,1)} %copy-done.10) | copy-start | bytes 1572868
  725.5 134.7 %reduce-scatter.25.cloned.1.call-start = ((), (), s32[]{:S(2)}) async-start(), calls=%async_computation.32 | async-start | bytes 5242880 | tf_op jit(solution)/shard_map/reduce_scatter | solution.py:38
  788.6 147.8 %reduce-scatter.29.cloned.1.call-start = ((), (), s32[]{:S(2)}) async-start(), calls=%async_computation.34 | async-start | bytes 4718592 | tf_op jit(solution)/shard_map/reduce_scatter | solution.py:359
  798.7 228.8 %reduce-scatter.31.cloned.1.call-start = ((), (), s32[]{:S(2)}) async-start(), calls=%async_computation.35 | async-start | bytes 4718592
  831.5 12.8 %all-to-all-start.6 = ((bf16[4,2,32768]{2,1,0:T(2,128)(2,1)}), bf16[4,2,32768]{2,1,0:T(2,128)(2,1)S(1)}, u32[]{:S(2)}, u32[]{:S(2)}) async-start(bf16[4,2,32768]{2,1,0:T(2,128)(2,1)} %reshape.1294), calls=%async_computation.13 | async-start | bytes 1048576 | tf_op jit(solution)/shard_map/all_to_all | solution.py:377
  854.7 34.0 %all-to-all-start.7 = ((bf16[8,2,16384]{2,1,0:T(2,128)(2,1)}), bf16[8,2,16384]{2,1,0:T(2,128)(2,1)}, u32[]{:S(2)}, u32[]{:S(2)}) async-start(bf16[8,2,16384]{2,1,0:T(2,128)(2,1)} %reshape.1296), calls=%async_computation.14 | async-start | bytes 1048576 | tf_op jit(solution)/shard_map/all_to_all | solution.py:376
  863.7 74.7 %copy-start.21 = (bf16[1,256,1024]{2,1,0:T(8,128)(2,1)S(1)}, bf16[1,256,1024]{2,1,0:T(8,128)(2,1)}, u32[]{:S(2)}) copy-start(bf16[1,256,1024]{2,1,0:T(8,128)(2,1)} %reduce-scatter.23.cloned.1.call-done) | copy-start | bytes 1572868
  863.7 74.8 %copy-start.69 = (bf16[1024]{0:T(1024)(128)(2,1)S(1)}, bf16[1024]{0:T(1024)(128)(2,1)}, u32[]{:S(2)}) copy-start(bf16[1024]{0:T(1024)(128)(2,1)} %get-tuple-element.564) | copy-start | bytes 6148
  888.6 254.1 %all-to-all-start.4 = ((bf16[4,2,32768]{2,1,0:T(2,128)(2,1)}), bf16[4,2,32768]{2,1,0:T(2,128)(2,1)S(1)}, u32[]{:S(2)}, u32[]{:S(2)}) async-start(bf16[4,2,32768]{2,1,0:T(2,128)(2,1)} %reshape.1290), calls=%async_computation.10 | async-start | bytes 1048576 | tf_op jit(solution)/shard_map/all_to_all | solution.py:368
  892.1 200.8 %reduce-scatter.33.cloned.1.call-start = ((), (), s32[]{:S(2)}) async-start(), calls=%async_computation.36 | async-start | bytes 294912
  1155.4 24.7 %all-to-all-start.5 = ((bf16[8,2,16384]{2,1,0:T(2,128)(2,1)}), bf16[8,2,16384]{2,1,0:T(2,128)(2,1)S(1)}, u32[]{:S(2)}, u32[]{:S(2)}) async-start(bf16[8,2,16384]{2,1,0:T(2,128)(2,1)} %reshape.1292), calls=%async_computation.11 | async-start | bytes 1048576 | tf_op jit(solution)/shard_map/all_to_all | solution.py:367
  (68 other events, 441.4 us)
Sparse Core Ops, SparseCore 0:
  74.4 20.5 all-gather.9
  97.6 75.0 all-gather.11
  201.4 48.3 reduce-scatter.14
  251.8 22.5 all-gather.15
  276.5 22.5 all-gather.13
  324.8 44.5 reduce-scatter.16
  372.1 73.3 all-gather.19
  447.7 20.8 all-gather.17
  480.0 44.4 reduce-scatter.18
  532.7 22.5 all-gather.21
  569.2 44.4 reduce-scatter.20
  619.1 22.5 all-gather.23
  681.1 31.4 reduce-scatter.22
  719.5 22.5 all-gather.25
  744.6 31.4 reduce-scatter.26
  788.8 44.4 reduce-scatter.24
  837.2 99.1 reduce-scatter.28
  939.9 87.6 reduce-scatter.30
  1031.8 61.0 reduce-scatter.32
where the time goes:
time: 1200 us; the launch traced here: 1190 us
  waiting for transfers between devices  674 us (56%)
  matrix products  131 us (11%)
  blocking collectives  128 us (11%)
  other arithmetic  103 us (9%)
  local copies, waits for them, and re-layouts  97.7 us (8%)
  starting transfers between devices  23.2 us (2%)
  between operations  22.6 us (2%)
  loops' own time  13.8 us (1%)
    unnamed x21, waiting for transfers between devices  148 us
    reduce_scatter x5, waiting for transfers between devices, scatter_rows(): return lax.psum_scatter(values, 'mp', scatter_dimension=1, tiled=True)  138 us
    all_gather x6, waiting for transfers between devices, gather_rows(): return lax.all_gather(values, 'mp', axis=1, tiled=True)  120 us
    all_gather x1, waiting for transfers between devices, per_device(): lax.all_gather(attn_weights.astype(jnp.bfloat16), 'dp', axis=1, tiled=True)  77.7 us
    all_gather x1, waiting for transfers between devices, per_device(): lax.all_gather(ffn_weights.astype(jnp.bfloat16), 'dp', axis=1, tiled=True)  73.3 us
    unnamed x200, local copies, waits for them, and re-layouts  54.9 us
    reduce_scatter x1, waiting for transfers between devices, per_device(): lax.psum_scatter(ffn_grad.astype(jnp.bfloat16), 'dp', scatter_dimension=1...  44.3 us
    psum x1, blocking collectives, per_device(): grad_norm = jnp.sqrt(lax.psum(local_squares, ('dp', 'mp')))  40.6 us
  transfers between devices with their start and end apart: 24, of which 19 were waited for; matrix products, arithmetic and copies ran while one was open for 14% of the time, Pallas kernels for 0%

commit v1 on v0

v1 whole, which is shorter than its diff:
```python
import functools

import jax
import jax.numpy as jnp
from jax import lax
from jax.experimental import pallas as pl
from jax.experimental.pallas import tpu as pltpu
from jax.sharding import PartitionSpec as P

HD = 64
STEP = 10


EPSILON = 1e-05
NEGATIVE = -1000000000.0
BETA_FIRST = 0.9
BETA_SECOND = 0.999
ADAM_EPSILON = 1e-08
MATRIX_RATE = 0.05
NORM_RATE = 1.0
MATRIX_DECAY = 0.1
AVERAGING = 0.7
THRESHOLD = 1.0
BF = jnp.bfloat16
F32 = jnp.float32


def grid_sizes():
    dp = lax.axis_size("dp")
    mp = lax.axis_size("mp")
    ny = 1 << ((dp.bit_length() - 1) // 2)
    return {"z": dp // ny, "y": ny, "x": mp // 2, "c": 2}


def grid_place():
    n = grid_sizes()
    dp = lax.axis_index("dp")
    mp = lax.axis_index("mp")
    return {"z": dp // n["y"], "y": dp % n["y"], "x": mp // 2, "c": mp % 2}


def hop(value, axis, step=1):
    n = grid_sizes()
    pairs = []
    for z in range(n["z"]):
        for y in range(n["y"]):
            for x in range(n["x"]):
                for c in range(2):
                    at = {"z": z, "y": y, "x": x, "c": c}
                    to = dict(at)
                    to[axis] = (at[axis] + step) % n[axis]
                    number = lambda p: ((p["z"] * n["y"] + p["y"]) * n["x"] + p["x"]) * 2 + p["c"]
                    pairs.append((number(at), number(to)))
    return lax.ppermute(value, ("dp", "mp"), pairs)


def pick(value, index, dim):
    return lax.dynamic_index_in_dim(value, index, dim, keepdims=False)


def gather_along(value, axis, dim):
    n = grid_sizes()[axis]
    me = grid_place()[axis]
    pieces = [value] + [hop(value, axis, s) for s in range(1, n)]
    if n == 2:
        low = jnp.where(me == 0, pieces[0], pieces[1])
        high = jnp.where(me == 0, pieces[1], pieces[0])
        return jnp.stack([low, high], dim)
    shape = value.shape[:dim] + (n,) + value.shape[dim:]
    out = jnp.zeros(shape, value.dtype)
    for s, piece in enumerate(pieces):
        out = lax.dynamic_update_index_in_dim(out, piece, (me - s) % n, dim)
    return out


def reduce_along(value, axis, dim):
    n = grid_sizes()[axis]
    me = grid_place()[axis]
    total = pick(value, me, dim).astype(F32)
    for s in range(1, n):
        total = total + hop(pick(value, (me + s) % n, dim).astype(BF), axis, s).astype(F32)
    return total


def dot(left, right, left_dim, right_dim):
    return lax.dot_general(
        left, right, (((left_dim,), (right_dim,)), ((), ())), preferred_element_type=F32
    )


def layer_norm(values, gains, biases):
    centered = values - jnp.mean(values, axis=-1, keepdims=True)
    variance = jnp.mean(centered * centered, axis=-1, keepdims=True)
    return centered * lax.rsqrt(variance + EPSILON) * gains + biases


def norm_back(values, gains, biases, upstream):
    result, pullback = jax.vjp(layer_norm, values, gains, biases)
    return pullback(upstream)


PAIR = 2 * HD


def key_bound(scalars, width, causal):
    limit = scalars[0]
    if not causal:
        return jnp.full((1, width), limit, jnp.int32)
    reach = lax.broadcasted_iota(jnp.int32, (1, width), 1) + scalars[1] + 1
    return jnp.minimum(reach, limit)


def only_head(value, head):
    lane = lax.broadcasted_iota(jnp.int32, value.shape, 1)
    keep = (lane < HD) if head == 0 else (lane >= HD)
    return jnp.where(keep, value, jnp.zeros_like(value))


def attend_forward_kernel(
    causal, chunk, scalars, q_ref, k_ref, v_ref, o_ref, sum_ref, score_ref, weight_ref
):
    rows, keys = q_ref.shape[0], k_ref.shape[0]
    bound = key_bound(scalars, rows, causal)
    queries = q_ref[...] * BF(HD**-0.5)
    values = v_ref[...]
    mixed = []
    for head in range(2):
        masked = only_head(queries, head)
        top = None
        for start in range(0, keys, chunk):
            block = slice(start, start + chunk)
            scores = dot(k_ref[block, :], masked, 1, 1)
            position = lax.broadcasted_iota(jnp.int32, scores.shape, 0) + start
            scores = jnp.where(position < bound, scores, NEGATIVE)
            score_ref[head, block, :] = scores
            highest = jnp.max(scores, axis=0, keepdims=True)
            top = highest if top is None else jnp.maximum(top, highest)
        total = None
        for start in range(0, keys, chunk):
            block = slice(start, start + chunk)
            raised = jnp.exp(score_ref[head, block, :] - top)
            part = jnp.sum(raised, axis=0, keepdims=True)
            total = part if total is None else total + part
            score_ref[head, block, :] = raised
        inverse = 1.0 / total
        for start in range(0, keys, chunk):
            block = slice(start, start + chunk)
            weight_ref[head, block, :] = (score_ref[head, block, :] * inverse).astype(BF)
        mixed.append(dot(values, weight_ref[head], 0, 0)[head * HD : (head + 1) * HD])
        sum_ref[head : head + 1, :] = top + jnp.log(total)
    o_ref[...] = jnp.concatenate(mixed, axis=0).T.astype(BF)


def attend_forward(scalars, queries, keys, values, causal):
    rows, width = queries.shape
    count = keys.shape[0]
    pairs = width // PAIR
    q_spec = pl.BlockSpec((rows, PAIR), lambda p: (0, p))
    k_spec = pl.BlockSpec((count, PAIR), lambda p: (0, p))
    return pl.pallas_call(
        functools.partial(attend_forward_kernel, causal, 256),
        grid=(pairs,),
        in_specs=[pl.BlockSpec(memory_space=pltpu.SMEM), q_spec, k_spec, k_spec],
        out_specs=[q_spec, pl.BlockSpec((None, 2, rows), lambda p: (p, 0, 0))],
        out_shape=[
            jax.ShapeDtypeStruct((rows, width), BF),
            jax.ShapeDtypeStruct((pairs, 2, rows), F32),
        ],
        scratch_shapes=[pltpu.VMEM((2, count, rows), F32), pltpu.VMEM((2, count, rows), BF)],
        compiler_params=pltpu.CompilerParams(vmem_limit_bytes=24 * 2**20),
        name="attend_forward",
        cost_estimate=pl.CostEstimate(
            flops=4 * rows * count * width,
            bytes_accessed=4 * width * (rows + count),
            transcendentals=rows * count * width // HD,
        ),
    )(scalars, queries, keys, values)


def attend_backward_kernel(
    causal, chunk, scalars, q_ref, k_ref, v_ref, o_ref, sum_ref, g_ref, dq_ref, dk_ref, dv_ref, ds_ref
):
    rows, keys = q_ref.shape[0], k_ref.shape[0]
    bound = key_bound(scalars, rows, causal)
    queries = q_ref[...] * BF(HD**-0.5)
    grads = g_ref[...]
    product = (grads.astype(F32) * o_ref[...].astype(F32)).T
    head_q = [only_head(queries, head) for head in range(2)]
    head_g = [only_head(grads, head) for head in range(2)]
    shift = [
        jnp.sum(product[head * HD : (head + 1) * HD], axis=0, keepdims=True) for head in range(2)
    ]
    for start in range(0, keys, chunk):
        block = slice(start, start + chunk)
        key_block, value_block = k_ref[block, :], v_ref[block, :]
        grad_value, grad_key = 0.0, 0.0
        for head in range(2):
            scores = dot(key_block, head_q[head], 1, 1)
            position = lax.broadcasted_iota(jnp.int32, scores.shape, 0) + start
            scores = jnp.where(position < bound, scores, NEGATIVE)
            weights = jnp.exp(scores - sum_ref[head : head + 1, :])
            grad_weights = dot(value_block, head_g[head], 1, 1)
            grad_scores = (weights * (grad_weights - shift[head])).astype(BF)
            ds_ref[head, block, :] = grad_scores
            grad_value = grad_value + dot(weights.astype(BF), head_g[head], 1, 0)
            grad_key = grad_key + dot(grad_scores, head_q[head], 1, 0)
        dv_ref[block, :] = grad_value.astype(BF)
        dk_ref[block, :] = grad_key.astype(BF)
    key_all = k_ref[...]
    parts = [dot(key_all, ds_ref[h], 0, 0)[h * HD : (h + 1) * HD] for h in range(2)]
    dq_ref[...] = (jnp.concatenate(parts, axis=0).T * HD**-0.5).astype(BF)


def attend_backward(scalars, queries, keys, values, mixed, logsum, grads, causal):
    rows, width = queries.shape
    count = keys.shape[0]
    pairs = width // PAIR
    q_spec = pl.BlockSpec((rows, PAIR), lambda p: (0, p))
    k_spec = pl.BlockSpec((count, PAIR), lambda p: (0, p))
    sum_spec = pl.BlockSpec((None, 2, rows), lambda p: (p, 0, 0))
    return pl.pallas_call(
        functools.partial(attend_backward_kernel, causal, 256),
        grid=(pairs,),
        in_specs=[
            pl.BlockSpec(memory_space=pltpu.SMEM), q_spec, k_spec, k_spec, q_spec, sum_spec, q_spec
        ],
        out_specs=[q_spec, k_spec, k_spec],
        out_shape=[jax.ShapeDtypeStruct((rows, width), BF)]
        + [jax.ShapeDtypeStruct((count, width), BF)] * 2,
        scratch_shapes=[pltpu.VMEM((2, count, rows), BF)],
        compiler_params=pltpu.CompilerParams(vmem_limit_bytes=24 * 2**20),
        name="attend_backward",
        cost_estimate=pl.CostEstimate(
            flops=10 * rows * count * width,
            bytes_accessed=8 * width * (rows + count),
            transcendentals=rows * count * width // HD,
        ),
    )(scalars, queries, keys, values, mixed, logsum, grads)


class Wires:
    def __init__(self, sizes, place, send_sem, recv_sem):
        self.sizes, self.place = sizes, place
        self.send_sem, self.recv_sem = send_sem, recv_sem
        self.count = 0
        self.started = []

    def peer(self, z=0, y=0, x=0, c=0):
        n, at = self.sizes, self.place
        pz, py = (at["z"] + z) % n["z"], (at["y"] + y) % n["y"]
        px, pc = (at["x"] + x) % n["x"], (at["c"] + c) % 2
        return (pz * n["y"] + py, px * 2 + pc)

    def send(self, src, dst, **shift):
        copy = pltpu.make_async_remote_copy(
            src_ref=src,
            dst_ref=dst,
            send_sem=self.send_sem.at[self.count],
            recv_sem=self.recv_sem.at[self.count],
            device_id=self.peer(**shift),
            device_id_type=pl.DeviceIdType.MESH,
        )
        self.count += 1
        copy.start()
        self.started.append(copy)
        return copy

    def greet(self, shifts):
        barrier = pltpu.get_barrier_semaphore()
        for shift in shifts:
            pl.semaphore_signal(
                barrier, inc=1, device_id=self.peer(**shift), device_id_type=pl.DeviceIdType.MESH
            )
        pl.semaphore_wait(barrier, len(shifts))

    def close(self):
        for copy in self.started:
            copy.wait_send()


def dp_shifts(n):
    return [{"z": z, "y": y} for z in range(n["z"]) for y in range(n["y"]) if z or y]


def mp_shifts(n):
    return [{"x": x, "c": c} for x in range(n["x"]) for c in range(2) if x or c]


def entry_kernel(
    n, w_ref, p_ref, s_ref, m_ref, ow_ref, op_ref, os_ref, om_ref, send_sem, recv_sem, local_sem
):
    at = grid_place()
    z, y, x, c = at["z"], at["y"], at["x"], at["c"]
    data = z * n["y"] + y
    wires = Wires(n, at, send_sem, recv_sem)
    wires.greet(
        dp_shifts(n) + [{"x": s} for s in range(1, n["x"])] + [{"c": 1}]
    )
    rows, wide = w_ref.shape[1], w_ref.shape[2]
    lines, deep = s_ref.shape[1], s_ref.shape[2]

    def spot(sz, sy, sx, mats=slice(None)):
        block = ((z - sz) % n["z"]) * n["y"] + (y - sy) % n["y"]
        column = (x - sx) % n["x"]
        return ow_ref.at[
            mats,
            pl.ds(pl.multiple_of(block * rows, rows), rows),
            pl.ds(pl.multiple_of(column * wide, wide), wide),
        ]

    def column(ref, sx, sc):
        index = ((x - sx) % n["x"]) * 2 + (c - sc) % 2
        return ref.at[:, pl.ds(pl.multiple_of(index * deep, deep), deep)]

    def patch(ref):
        index = x * 2 + c
        return ref.at[
            pl.ds(pl.multiple_of(data * lines, lines), lines),
            pl.ds(pl.multiple_of(index * deep, deep), deep),
        ]

    def stripe(ref):
        return ref.at[data]

    own = [
        pltpu.make_async_copy(w_ref, spot(0, 0, 0), local_sem.at[0]),
        pltpu.make_async_copy(p_ref, stripe(op_ref), local_sem.at[1]),
        pltpu.make_async_copy(s_ref.at[data], patch(os_ref), local_sem.at[2]),
        pltpu.make_async_copy(m_ref.at[data], patch(om_ref), local_sem.at[3]),
    ]
    for copy in own:
        copy.start()

    def spread(ref, out):
        copies = []
        for shift in dp_shifts(n):
            target = wires.peer(**shift)[0]
            copies.append(wires.send(ref.at[target], patch(out), **shift))
        return copies

    def forward_columns(out, copies):
        for copy in copies:
            copy.wait_recv()
        near = [wires.send(column(out, 0, 0), column(out, 0, 0), x=s) for s in range(1, n["x"])]
        pair = [wires.send(column(out, 0, 0), column(out, 0, 0), c=1)]
        return near, pair

    def finish_columns(out, near, pair):
        for s in range(1, n["x"]):
            near[s - 1].wait_recv()
            pair.append(wires.send(column(out, s, 0), column(out, s, 0), c=1))
        for copy in pair:
            copy.wait_recv()

    to_z = {s: wires.send(w_ref, spot(0, 0, 0), z=s) for s in range(1, n["z"])}
    to_y = {(0, s): wires.send(w_ref, spot(0, 0, 0), y=s) for s in range(1, n["y"])}
    to_x = {(0, s): wires.send(w_ref, spot(0, 0, 0), x=s) for s in range(1, n["x"])}
    params = [wires.send(p_ref, stripe(op_ref), **shift) for shift in dp_shifts(n)]
    states = spread(s_ref, os_ref)
    memory = spread(m_ref, om_ref)

    for sz in range(1, n["z"]):
        to_z[sz].wait_recv()
        for s in range(1, n["y"]):
            to_y[sz, s] = wires.send(spot(sz, 0, 0), spot(sz, 0, 0), y=s)
        for s in range(1, n["x"]):
            to_x[sz, s] = wires.send(spot(sz, 0, 0), spot(sz, 0, 0), x=s)
    for copy in own:
        copy.wait()
    states = forward_columns(os_ref, states)
    last = []
    cut = max(1, w_ref.shape[0] // 4)
    for sz in range(n["z"]):
        for sy in range(1, n["y"]):
            to_y[sz, sy].wait_recv()
            part = spot(sz, sy, 0, slice(0, cut))
            for s in range(1, n["x"]):
                last.append(wires.send(part, part, x=s))
        for sx in range(1, n["x"]):
            to_x[sz, sx].wait_recv()
            part = spot(sz, 0, sx, slice(cut, w_ref.shape[0]))
            for s in range(1, n["y"]):
                last.append(wires.send(part, part, y=s))
    memory = forward_columns(om_ref, memory)
    finish_columns(os_ref, *states)
    finish_columns(om_ref, *memory)
    for copy in params + last:
        copy.wait_recv()
    wires.close()


def entry(weights, params, states, memory):
    n = grid_sizes()
    count, rows, wide = weights.shape
    utterances, lines, deep = states.shape
    nz, ny, nx = n["z"], n["y"], n["x"]
    data = nz * ny
    copies = (
        (nz - 1)
        + nz * (ny - 1 + nx - 1)
        + 2 * nz * (ny - 1) * (nx - 1)
        + 3 * (data - 1)
        + 2 * (2 * (nx - 1) + 1)
    )
    hbm = pl.BlockSpec(memory_space=pl.ANY)
    return pl.pallas_call(
        functools.partial(entry_kernel, n),
        out_shape=[
            jax.ShapeDtypeStruct((count, data * rows, nx * wide), BF),
            jax.ShapeDtypeStruct((data,) + params.shape, F32),
            jax.ShapeDtypeStruct((data * lines, 2 * nx * deep), BF),
            jax.ShapeDtypeStruct((data * lines, 2 * nx * deep), BF),
        ],
        in_specs=[pl.BlockSpec(memory_space=pltpu.VMEM)] * 4,
        out_specs=[hbm] * 4,
        scratch_shapes=[
            pltpu.SemaphoreType.DMA((copies,)),
            pltpu.SemaphoreType.DMA((copies,)),
            pltpu.SemaphoreType.DMA((4,)),
        ],
        compiler_params=pltpu.CompilerParams(
            collective_id=0, has_side_effects=True, vmem_limit_bytes=16 * 2**20
        ),
        name="entry",
    )(weights, params, states, memory)


def closing_kernel(
    n,
    g0_ref,
    g1_ref,
    g2_ref,
    g3_ref,
    h_ref,
    x_ref,
    d_ref,
    gain_ref,
    m_ref,
    p_ref,
    og_ref,
    os_ref,
    om_ref,
    op_ref,
    ra1_ref,
    rb1_ref,
    sa2_ref,
    sb2_ref,
    ra2_ref,
    rb2_ref,
    acc_ref,
    s3_ref,
    r3_ref,
    rc_ref,
    sx_ref,
    rx_ref,
    dx_ref,
    np_ref,
    nn_ref,
    nf_ref,
    send_sem,
    recv_sem,
    move_send_sem,
    move_recv_sem,
    local_sem,
):
    at = grid_place()
    z, y, x, c = at["z"], at["y"], at["x"], at["c"]
    nz, ny, nx = n["z"], n["y"], n["x"]
    data, model = z * ny + y, x * 2 + c
    wires = Wires(n, at, send_sem, recv_sem)
    everyone = [
        dict(z=sz, y=sy, x=sx, c=sc)
        for sz in range(nz)
        for sy in range(ny)
        for sx in range(nx)
        for sc in range(2)
        if sz or sy or sx or sc
    ]
    wires.greet(everyone)
    first, second = (g0_ref, g1_ref), (g2_ref, g3_ref)
    rows, wide = og_ref.shape[1], og_ref.shape[2]

    def bands(ref, band, count, col):
        return ref.at[
            pl.ds(pl.multiple_of(band * rows, rows), count * rows),
            pl.ds(pl.multiple_of(col * wide, wide), wide),
        ]

    def full_band(ref, band):
        return ref.at[pl.ds(pl.multiple_of(band * rows, rows), rows)]

    order = list(range(1, nz)) + [0]
    to_c = wires.send(h_ref.at[:, 1 - c], rc_ref, c=1)
    by_x, by_y = {}, {}
    for s in order:
        zone = ((z + s) % nz) * ny
        for t in range(1, nx):
            col = (x + t) % nx
            by_x[s, t] = [
                wires.send(bands(ref, zone, ny, col), ra1_ref.at[t - 1, s, i], x=t)
                for i, ref in enumerate(first)
            ]
        for t in range(1, ny):
            band = zone + (y + t) % ny
            by_y[s, t] = [
                wires.send(full_band(ref, band), rb1_ref.at[t - 1, s, i], y=t)
                for i, ref in enumerate(second)
            ]
    spread = []
    for i, shift in enumerate(dp_shifts(n)):
        target = wires.peer(**shift)[0]
        spread.append(wires.send(m_ref.at[target], om_ref.at[data], **shift))
    keep = pltpu.make_async_copy(m_ref.at[data], om_ref.at[data], local_sem)
    keep.start()

    to_c.wait_recv()
    near = []
    for t in range(1, nx):
        index = (x + t) % nx
        sx_ref[t - 1] = (h_ref[index, c].astype(F32) + rc_ref[index].astype(F32)).astype(BF)
        near.append(wires.send(sx_ref.at[t - 1], rx_ref.at[t - 1], x=t))

    next_y, next_x = {}, {}
    for s in order:
        zone = ((z + s) % nz) * ny
        for t in range(1, nx):
            for copy in by_x[s, t]:
                copy.wait_recv()
        for i, ref in enumerate(first):
            for b in range(ny):
                band = (y + b) % ny
                total = bands(ref, zone + band, 1, x)[...].astype(F32)
                for t in range(1, nx):
                    part = ra1_ref.at[
                        t - 1, s, i, pl.ds(pl.multiple_of(band * rows, rows), rows)
                    ]
                    total = total + part[...].astype(F32)
                if b == 0:
                    acc_ref[s, i] = total
                else:
                    sa2_ref[b - 1, s, i] = total.astype(BF)
        for t in range(1, ny):
            next_y[s, t] = wires.send(sa2_ref.at[t - 1, s], ra2_ref.at[t - 1, s], y=t)
        for t in range(1, ny):
            for copy in by_y[s, t]:
                copy.wait_recv()
        for i, ref in enumerate(second):
            for b in range(nx):
                col = pl.ds(pl.multiple_of(((x + b) % nx) * wide, wide), wide)
                total = bands(ref, zone + y, 1, (x + b) % nx)[...].astype(F32)
                for t in range(1, ny):
                    total = total + rb1_ref[t - 1, s, i, :, col].astype(F32)
                if b == 0:
                    acc_ref[s, 2 + i] = total
                else:
                    sb2_ref[b - 1, s, i] = total.astype(BF)
        for t in range(1, nx):
            next_x[s, t] = wires.send(sb2_ref.at[t - 1, s], rb2_ref.at[t - 1, s], x=t)

    grad = h_ref[x, c].astype(F32) + rc_ref[x].astype(F32)
    for t in range(1, nx):
        near[t - 1].wait_recv()
        grad = grad + rx_ref[t - 1].astype(F32)
    values = x_ref[...].astype(F32)
    centered = values - jnp.mean(values, axis=-1, keepdims=True)
    scale = lax.rsqrt(jnp.mean(centered * centered, axis=-1, keepdims=True) + EPSILON)
    normed = centered * scale
    up = grad * gain_ref[...]
    back = scale * (
        up
        - jnp.mean(up, axis=-1, keepdims=True)
        - normed * jnp.mean(up * normed, axis=-1, keepdims=True)
    )
    dx_ref[...] = (d_ref[...] + back).astype(BF)
    lines, deep = os_ref.shape[1], os_ref.shape[2]
    blocks = dx_ref.shape[0] // lines

    def moves():
        for b in range(blocks):
            for m in range(2 * nx):
                target = (model * blocks + b, m)
                src = dx_ref.at[b * lines : (b + 1) * lines, m * deep : (m + 1) * deep]
                mine = jnp.logical_and(target[0] == data, model == m)
                remote = pltpu.make_async_remote_copy(
                    src_ref=src,
                    dst_ref=os_ref.at[data],
                    send_sem=move_send_sem.at[b * 2 * nx + m],
                    recv_sem=move_recv_sem.at[data],
                    device_id=target,
                    device_id_type=pl.DeviceIdType.MESH,
                )
                yield mine, remote, pltpu.make_async_copy(src, os_ref.at[data], move_recv_sem.at[data])

    for mine, remote, here in moves():
        pl.when(mine)(lambda: here.start())
        pl.when(jnp.logical_not(mine))(lambda: remote.start())

    line = lax.broadcasted_iota(jnp.int32, p_ref.shape, 0)
    gain_grad = jnp.sum(grad * normed, axis=0, keepdims=True)
    bias_grad = jnp.sum(grad, axis=0, keepdims=True)
    params = p_ref[...] + jnp.where(line == 0, gain_grad, 0.0) + jnp.where(line == 4, bias_grad, 0.0)
    columns = op_ref.shape[1]
    for k in range(nz * ny):
        np_ref[0, k] = params[:, k * columns : (k + 1) * columns]
    norm_near = [wires.send(np_ref.at[0], nn_ref.at[i], **s) for i, s in enumerate(mp_shifts(n))]

    to_z = {}
    for s in order:
        for t in range(1, ny):
            next_y[s, t].wait_recv()
        for t in range(1, nx):
            next_x[s, t].wait_recv()
        for i in range(4):
            total = acc_ref[s, i]
            if i < 2:
                for t in range(1, ny):
                    total = total + ra2_ref[t - 1, s, i].astype(F32)
            else:
                for t in range(1, nx):
                    total = total + rb2_ref[t - 1, s, i - 2].astype(F32)
            if s == 0:
                acc_ref[s, i] = total
            else:
                s3_ref[s - 1, i] = total.astype(BF)
        if s:
            to_z[s] = wires.send(s3_ref.at[s - 1], r3_ref.at[s - 1], z=s)

    total = np_ref[0]
    for i, copy in enumerate(norm_near):
        copy.wait_recv()
        total = total + nn_ref[i]
    np_ref[1] = total
    norm_far = []
    for i, shift in enumerate(dp_shifts(n)):
        target = wires.peer(**shift)[0]
        norm_far.append(wires.send(np_ref.at[1, target], nf_ref.at[i], **shift))
    for s in range(1, nz):
        to_z[s].wait_recv()
    for i in range(4):
        total = acc_ref[0, i]
        for s in range(1, nz):
            total = total + r3_ref[s - 1, i].astype(F32)
        og_ref[i] = total
    total = np_ref[1, data]
    for i, copy in enumerate(norm_far):
        copy.wait_recv()
        total = total + nf_ref[i]
    op_ref[...] = total
    for copy in spread:
        copy.wait_recv()
    keep.wait()
    for mine, remote, here in moves():
        pl.when(jnp.logical_not(mine))(lambda: remote.wait_send())
    for r in range(nz * ny):
        pltpu.make_async_copy(os_ref.at[r], os_ref.at[r], move_recv_sem.at[r]).wait()
    wires.close()


def closing(grads, partial, inputs, upstream, gain, memory, params):
    n = grid_sizes()
    nz, ny, nx = n["z"], n["y"], n["x"]
    data, model = nz * ny, 2 * nx
    width, local = grads[0].shape
    rows, wide = width // data, local // nx
    own = inputs.shape[0]
    utterances, lines, deep = memory.shape
    columns = width // data
    copies = (
        1
        + nz * 2 * (nx - 1 + ny - 1)
        + (data - 1)
        + (nx - 1)
        + nz * (ny - 1 + nx - 1)
        + (model - 1)
        + (nz - 1)
        + (data - 1)
    )
    vmem = pl.BlockSpec(memory_space=pltpu.VMEM)
    hbm = pl.BlockSpec(memory_space=pl.ANY)
    return pl.pallas_call(
        functools.partial(closing_kernel, n),
        out_shape=[
            jax.ShapeDtypeStruct((4, rows, wide), F32),
            jax.ShapeDtypeStruct((data, lines, deep), BF),
            jax.ShapeDtypeStruct((data, lines, deep), BF),
            jax.ShapeDtypeStruct((params.shape[0], columns), F32),
        ],
        in_specs=[vmem] * 8 + [hbm, vmem],
        out_specs=[vmem, hbm, hbm, vmem],
        scratch_shapes=[
            pltpu.VMEM((nx - 1, nz, 2, ny * rows, wide), BF),
            pltpu.VMEM((ny - 1, nz, 2, rows, nx * wide), BF),
            pltpu.VMEM((ny - 1, nz, 2, rows, wide), BF),
            pltpu.VMEM((nx - 1, nz, 2, rows, wide), BF),
            pltpu.VMEM((ny - 1, nz, 2, rows, wide), BF),
            pltpu.VMEM((nx - 1, nz, 2, rows, wide), BF),
            pltpu.VMEM((nz, 4, rows, wide), F32),
            pltpu.VMEM((nz - 1, 4, rows, wide), BF),
            pltpu.VMEM((nz - 1, 4, rows, wide), BF),
            pltpu.VMEM((nx, own, width), BF),
            pltpu.VMEM((nx - 1, own, width), BF),
            pltpu.VMEM((nx - 1, own, width), BF),
            pltpu.VMEM((own, width), BF),
            pltpu.VMEM((2, data, params.shape[0], columns), F32),
            pltpu.VMEM((model - 1, data, params.shape[0], columns), F32),
            pltpu.VMEM((data - 1, params.shape[0], columns), F32),
            pltpu.SemaphoreType.DMA((copies,)),
            pltpu.SemaphoreType.DMA((copies,)),
            pltpu.SemaphoreType.DMA((data,)),
            pltpu.SemaphoreType.DMA((data,)),
            pltpu.SemaphoreType.DMA,
        ],
        compiler_params=pltpu.CompilerParams(
            collective_id=1, has_side_effects=True, vmem_limit_bytes=48 * 2**20
        ),
        name="closing",
    )(*grads, partial, inputs, upstream, gain, memory, params)


def place_kernel(n, plan, by_x, *refs):
    at = grid_place()
    out, sem = refs[-2], refs[-1]
    rows, wide = refs[0].shape[2], refs[0].shape[3]
    copies = []
    for ref, (sy, sx) in zip(refs[:-2], plan):
        for sz in range(n["z"]):
            block = ((at["z"] - sz) % n["z"]) * n["y"] + (at["y"] - sy) % n["y"]
            column = (at["x"] - sx) % n["x"] if by_x else 0
            target = out.at[
                :,
                pl.ds(pl.multiple_of(block * rows, rows), rows),
                pl.ds(pl.multiple_of(column * wide, wide), wide),
            ]
            copy = pltpu.make_async_copy(ref.at[sz], target, sem.at[len(copies)])
            copy.start()
            copies.append(copy)
    for copy in copies:
        copy.wait()


def gather_weights(group, by_x):
    n = grid_sizes()
    zone = jnp.stack([group] + [hop(group, "z", s) for s in range(1, n["z"])])
    blocks, plan = [zone], [(0, 0)]
    for s in range(1, n["y"]):
        blocks.append(hop(zone, "y", s))
        plan.append((s, 0))
    if by_x:
        for s in range(1, n["x"]):
            for block, (sy, _) in list(zip(blocks, plan))[: n["y"]]:
                blocks.append(hop(block, "x", s))
                plan.append((sy, s))
    count, rows, wide = group.shape
    hbm = pl.BlockSpec(memory_space=pl.ANY)
    columns = wide * (n["x"] if by_x else 1)
    return pl.pallas_call(
        functools.partial(place_kernel, n, tuple(plan), by_x),
        out_shape=jax.ShapeDtypeStruct((count, n["z"] * n["y"] * rows, columns), BF),
        in_specs=[hbm] * len(blocks),
        out_specs=pl.BlockSpec(memory_space=pltpu.VMEM),
        scratch_shapes=[pltpu.SemaphoreType.DMA((len(blocks) * n["z"],))],
        compiler_params=pltpu.CompilerParams(vmem_limit_bytes=16 * 2**20),
        name="place",
    )(*blocks)


def after(value, *others):
    return lax.optimization_barrier((value,) + others)[0]


def square_sum_kernel(n, g_ref, o_ref, near_ref, sum_ref, far_ref, send_sem, recv_sem):
    wires = Wires(n, grid_place(), send_sem, recv_sem)
    wires.greet(dp_shifts(n) + mp_shifts(n))
    copies = [wires.send(g_ref, near_ref.at[i], **shift) for i, shift in enumerate(mp_shifts(n))]
    total = g_ref[...]
    for i, copy in enumerate(copies):
        copy.wait_recv()
        total = total + near_ref[i]
    sum_ref[...] = total
    copies = [wires.send(sum_ref, far_ref.at[i], **shift) for i, shift in enumerate(dp_shifts(n))]
    for i, copy in enumerate(copies):
        copy.wait_recv()
        total = total + far_ref[i]
    o_ref[...] = total
    wires.close()


def square_sum(partial):
    n = grid_sizes()
    data = n["z"] * n["y"]
    model = 2 * n["x"]
    vmem = pl.BlockSpec(memory_space=pltpu.VMEM)
    copies = data - 1 + model - 1
    return pl.pallas_call(
        functools.partial(square_sum_kernel, n),
        out_shape=jax.ShapeDtypeStruct(partial.shape, F32),
        in_specs=[vmem],
        out_specs=vmem,
        scratch_shapes=[
            pltpu.VMEM((model - 1,) + partial.shape, F32),
            pltpu.VMEM(partial.shape, F32),
            pltpu.VMEM((data - 1,) + partial.shape, F32),
            pltpu.SemaphoreType.DMA((copies,)),
            pltpu.SemaphoreType.DMA((copies,)),
        ],
        compiler_params=pltpu.CompilerParams(collective_id=2, has_side_effects=True),
        name="square_sum",
    )(partial)


def adam_step(weight, moment, square, gradient, step_rate, weight_decay):
    moment_new = BETA_FIRST * moment + (1.0 - BETA_FIRST) * gradient
    square_new = BETA_SECOND * square + (1.0 - BETA_SECOND) * gradient * gradient
    moment_hat = moment_new / (1.0 - BETA_FIRST**STEP)
    square_hat = square_new / (1.0 - BETA_SECOND**STEP)
    updated = weight - step_rate * (
        moment_hat / (jnp.sqrt(square_hat) + ADAM_EPSILON) + weight_decay * weight
    )
    return (updated, moment_new, square_new)


def per_device(
    states,
    memory,
    cotangent,
    lengths,
    memory_lengths,
    regroup_order,
    attn_weights,
    ffn_weights,
    norm_params,
    attn_mean,
    ffn_mean,
    norm_mean,
    attn_square,
    ffn_square,
    norm_square,
    attn_average,
    ffn_average,
    norm_average,
):
    n = grid_sizes()
    at = grid_place()
    nz, ny, nx = n["z"], n["y"], n["x"]
    data_index = lax.axis_index("dp")
    model_index = lax.axis_index("mp")
    data_size = lax.axis_size("dp")
    width = states.shape[2] * lax.axis_size("mp")
    slot = states.shape[1] * data_size
    own_rows = cotangent.shape[1]
    chip_rows = 2 * own_rows
    chip_start = at["x"] * chip_rows

    def own_of(value):
        return lax.dynamic_slice_in_dim(value, at["c"] * own_rows, own_rows, 0)

    def other_of(value):
        return lax.dynamic_slice_in_dim(value, (1 - at["c"]) * own_rows, own_rows, 0)

    def pair_rows(value):
        other = hop(value, "c")
        first = at["c"] == 0
        return jnp.concatenate(
            [jnp.where(first, value, other), jnp.where(first, other, value)], axis=0
        )

    def chip_of(value):
        return lax.dynamic_slice_in_dim(value, chip_start, chip_rows, 0)

    attn_low = attn_weights.astype(BF)
    ffn_low = ffn_weights.astype(BF)

    weights_self, norm_values, inputs, frames = entry(
        attn_low[0:4],
        norm_params.astype(BF).astype(F32),
        jnp.take(states, regroup_order, axis=0),
        jnp.take(memory, regroup_order, axis=0),
    )
    norm_values = jnp.swapaxes(norm_values, 0, 1).reshape(norm_params.shape[0], width)
    length = lengths[regroup_order[data_index]]
    reach = memory_lengths[regroup_order[data_index]]

    self_scalars = jnp.stack([length, chip_start]).astype(jnp.int32)
    cross_scalars = jnp.stack([reach, chip_start]).astype(jnp.int32)

    weights_cross = gather_weights(after(attn_low[4:8], weights_self), True)
    ffn_maps = gather_weights(after(ffn_low, weights_self), False)
    up_map, down_map = ffn_maps[0], ffn_maps[1]

    resid_zero_full = inputs.astype(F32)
    normed_first = layer_norm(resid_zero_full, norm_values[0], norm_values[4]).astype(BF)
    normed_first_chip = chip_of(normed_first)
    resid_zero = chip_of(resid_zero_full)
    query_self = dot(normed_first_chip, weights_self[0], 1, 0).astype(BF)
    key_self = dot(normed_first, weights_self[1], 1, 0).astype(BF)
    value_self = dot(normed_first, weights_self[2], 1, 0).astype(BF)
    mixed_self, logsum_self = attend_forward(
        self_scalars, query_self, key_self, value_self, True
    )

    def core_sum(partial):
        partial = partial.astype(BF)
        return partial.astype(F32) + hop(partial, "c").astype(F32)

    resid_one = resid_zero + core_sum(dot(mixed_self, weights_self[3], 1, 1))
    normed_second = layer_norm(resid_one, norm_values[1], norm_values[5]).astype(BF)

    query_cross = dot(normed_second, weights_cross[0], 1, 0).astype(BF)
    key_cross = dot(frames, weights_cross[1], 1, 0).astype(BF)
    value_cross = dot(frames, weights_cross[2], 1, 0).astype(BF)
    mixed_cross, logsum_cross = attend_forward(
        cross_scalars, query_cross, key_cross, value_cross, False
    )
    resid_two = resid_one + core_sum(dot(mixed_cross, weights_cross[3], 1, 1))
    normed_third = layer_norm(resid_two, norm_values[2], norm_values[6]).astype(BF)

    def far_rows(own):
        near = [hop(own, "x", s) for s in range(1, nx)]
        cross = hop(jnp.stack(near), "c")
        return jnp.concatenate([v for s in range(nx - 1) for v in (near[s], cross[s])], axis=0)

    def scatter_rows(partial_chip, partial_far):
        total = own_of(partial_chip) + hop(other_of(partial_chip).astype(BF), "c").astype(F32)
        far = partial_far.reshape(nx - 1, 2, own_rows, width)
        far = far[:, 0] + hop(far[:, 1].astype(BF), "c").astype(F32)
        for s in range(1, nx):
            total = total + hop(far[s - 1].astype(BF), "x", nx - s).astype(F32)
        return total

    normed_far = far_rows(own_of(normed_third))
    hidden_chip = dot(normed_third, up_map, 1, 0)
    hidden_far = dot(normed_far, up_map, 1, 0)
    active_chip = jax.nn.gelu(hidden_chip).astype(BF)
    active_far = jax.nn.gelu(hidden_far).astype(BF)
    resid_two_own = own_of(resid_two)
    resid_three = resid_two_own + scatter_rows(
        dot(active_chip, down_map, 1, 1), dot(active_far, down_map, 1, 1)
    )
    layer_output = layer_norm(resid_three, norm_values[3], norm_values[7]).astype(BF)

    positions = model_index * own_rows + jnp.arange(own_rows, dtype=jnp.int32)
    seed_grad = jnp.where((positions < length)[:, None], cotangent[0].astype(F32), 0.0)
    grad_three, gain_final, bias_final = norm_back(
        resid_three, norm_values[3], norm_values[7], seed_grad
    )
    down_own = grad_three.astype(BF)
    down_far = far_rows(down_own)
    down_chip = pair_rows(down_own)

    def hidden_back(rows, hidden):
        grad_active = dot(rows, down_map, 1, 0)
        result, pull = jax.vjp(jax.nn.gelu, hidden)
        return pull(grad_active)[0].astype(BF)

    grad_hidden_chip = hidden_back(down_chip, hidden_chip)
    grad_hidden_far = hidden_back(down_far, hidden_far)
    grad_normed = scatter_rows(
        dot(grad_hidden_chip, up_map, 1, 1), dot(grad_hidden_far, up_map, 1, 1)
    )

    def band_of(value, band):
        return pick(value.reshape(value.shape[0], nz, ny, -1), band, 2).reshape(value.shape[0], -1)

    def scatter_ffn(lefts, rights):
        def part(step):
            band = (at["y"] + step) % ny
            total = sum(dot(band_of(l, band), r, 0, 0) for l, r in zip(lefts, rights))
            return total.reshape(nz, -1, rights[0].shape[1])

        others = [hop(part(s).astype(BF), "y", s) for s in range(1, ny)]
        total = part(0)

        def finish(*ready):
            value = total
            for piece in others:
                value = value + after(piece, *ready).astype(F32)
            return reduce_along(value, "z", 0)

        return finish

    finish_down = scatter_ffn((down_chip, down_far), (active_chip, active_far))
    finish_up = scatter_ffn((normed_third, normed_far), (grad_hidden_chip, grad_hidden_far))

    def columns_of(value, index):
        return pick(value.reshape(value.shape[0], nx, -1), index, 1)

    def scatter_attn(lefts, rights):
        def part(step):
            return [dot(l, columns_of(r, (at["x"] + step) % nx), 0, 0) for l, r in zip(lefts, rights)]

        others = [
            hop(jnp.stack([v.astype(BF) for v in part(s)]), "x", s) for s in range(1, nx)
        ]
        own = part(0)

        def finish(*ready):
            total = jnp.stack(own)
            for piece in others:
                total = total + after(piece, *ready).astype(F32)
            total = total.reshape(len(own), nz, ny, -1, total.shape[2])
            return reduce_along(reduce_along(total, "y", 2), "z", 1)

        return finish

    step_back, gain_third, bias_third = norm_back(
        resid_two_own, norm_values[2], norm_values[6], grad_normed
    )
    grad_two = grad_three + step_back

    cross_rows = pair_rows(grad_two.astype(BF))
    grad_mixed_cross = dot(cross_rows, weights_cross[3], 1, 0).astype(BF)
    query_grad_cross, key_grad_cross, value_grad_cross = attend_backward(
        cross_scalars,
        query_cross,
        key_cross,
        value_cross,
        mixed_cross,
        logsum_cross,
        grad_mixed_cross,
        False,
    )

    def core_scatter(partial):
        return own_of(partial) + hop(other_of(partial).astype(BF), "c").astype(F32)

    grad_normed_cross = core_scatter(dot(query_grad_cross, weights_cross[0], 1, 1))
    step_back, gain_second, bias_second = norm_back(
        own_of(resid_one), norm_values[1], norm_values[5], grad_normed_cross
    )
    grad_one = grad_two + step_back
    finish_cross = scatter_attn(
        (normed_second, frames, frames, cross_rows),
        (query_grad_cross, key_grad_cross, value_grad_cross, mixed_cross),
    )
    shard_down = finish_down(query_grad_cross)
    shard_up = finish_up(query_grad_cross)
    memory_part = dot(key_grad_cross, weights_cross[1], 1, 1) + dot(
        value_grad_cross, weights_cross[2], 1, 1
    )
    memory_part = memory_part.reshape(slot, nx, 2, -1)
    memory_part = reduce_along(reduce_along(memory_part, "c", 2), "x", 1)
    self_rows = pair_rows(grad_one.astype(BF))
    grad_mixed_self = dot(self_rows, weights_self[3], 1, 0).astype(BF)
    query_grad, key_grad, value_grad = attend_backward(
        self_scalars,
        query_self,
        key_self,
        value_self,
        mixed_self,
        logsum_self,
        grad_mixed_self,
        True,
    )
    shard_cross = finish_cross(query_grad)
    self_grads = [
        dot(normed_first_chip, query_grad, 0, 0).astype(BF),
        dot(normed_first, key_grad, 0, 0).astype(BF),
        dot(normed_first, value_grad, 0, 0).astype(BF),
        dot(self_rows, mixed_self, 0, 0).astype(BF),
    ]
    part = dot(key_grad, weights_self[1], 1, 1) + dot(value_grad, weights_self[2], 1, 1)
    query_part = dot(query_grad, weights_self[0], 1, 1)
    part = lax.dynamic_update_slice_in_dim(part, chip_of(part) + query_part, chip_start, 0)
    empty = jnp.zeros_like(gain_third)
    norm_grad = jnp.stack(
        [empty, gain_second, gain_third, gain_final, empty, bias_second, bias_third, bias_final]
    )
    shard_self, back_states, back_memory, norm_shard = closing(
        self_grads,
        part.astype(BF).reshape(nx, 2, own_rows, width),
        own_of(chip_of(inputs)),
        grad_one,
        norm_values[0:1],
        memory_part.astype(BF).reshape(data_size, -1, memory_part.shape[1]),
        norm_grad,
    )
    attn_shard = jnp.concatenate([shard_self, shard_cross], axis=0)
    ffn_shard = jnp.stack([shard_up, shard_down])

    inverse = jnp.argsort(regroup_order)
    states_grad = jnp.take(back_states, inverse, axis=0).astype(F32)
    memory_grad = jnp.take(back_memory, inverse, axis=0).astype(F32)
    def squares(value):
        return jnp.sum((value * value).reshape(-1, 8, 128), axis=0)

    norm_squares = jnp.sum(norm_shard * norm_shard) / lax.axis_size("mp")
    local_squares = squares(attn_shard) + squares(ffn_shard) + norm_squares / 1024.0
    grad_norm = jnp.sqrt(jnp.sum(square_sum(local_squares)))
    clip_scale = jnp.minimum(1.0, THRESHOLD / (grad_norm + 1e-06))
    attn_updated, mean_attn, square_attn = adam_step(
        attn_weights, attn_mean, attn_square, clip_scale * attn_shard, MATRIX_RATE, MATRIX_DECAY
    )
    ffn_updated, mean_ffn, square_ffn = adam_step(
        ffn_weights, ffn_mean, ffn_square, clip_scale * ffn_shard, MATRIX_RATE, MATRIX_DECAY
    )
    norm_updated, mean_norm, square_norm = adam_step(
        norm_params, norm_mean, norm_square, clip_scale * norm_shard, NORM_RATE, 0.0
    )
    average_attn = AVERAGING * attn_average + (1.0 - AVERAGING) * attn_updated
    average_ffn = AVERAGING * ffn_average + (1.0 - AVERAGING) * ffn_updated
    average_norm = AVERAGING * norm_average + (1.0 - AVERAGING) * norm_updated
    return (
        layer_output[None],
        states_grad,
        memory_grad,
        attn_updated,
        ffn_updated,
        norm_updated,
        mean_attn,
        mean_ffn,
        mean_norm,
        square_attn,
        square_ffn,
        square_norm,
        average_attn,
        average_ffn,
        average_norm,
        grad_norm,
    )


def solution(mesh):
    rows = P(None, "dp", "mp")
    line = P(None, "dp")
    return jax.shard_map(
        per_device,
        mesh=mesh,
        in_specs=(rows, rows, P("dp", "mp", None), P(), P(), P())
        + (rows, rows, line) * 4,
        out_specs=(P("dp", "mp", None), rows, rows) + (rows, rows, line) * 4 + (P(),),
        check_vma=False,
    )
```

time: 1200 us -> 717 us (0.60)
  waiting for transfers between devices: 674 us -> 200 us
  Pallas kernels: 0 us -> 229 us
  blocking collectives: 128 us -> 0 us
  matrix products: 131 us -> 79.4 us
  other arithmetic: 103 us -> 69.3 us
  between operations: 22.6 us -> 7.32 us
  loops' own time: 13.8 us -> 0 us
    all_gather x9 -> x0, waiting for transfers between devices: 292 us -> none  [the longest x6 120 us: gather_rows(): return lax.all_gather(values, 'mp', axis=1, tiled=True)]
    pallas_call x0 -> x9, Pallas kernels: none -> 229 us  [the longest x1 92.7 us: closing(): pl.pallas_call(functools.partial(closing_kernel, n), out_shape=[jax.Shape...]
    reduce_scatter x8 -> x0, waiting for transfers between devices: 214 us -> none  [the longest x5 138 us: scatter_rows(): return lax.psum_scatter(values, 'mp', scatter_dimension=1, tiled=True)]
    ppermute x0 -> x41, waiting for transfers between devices: none -> 200 us  [hop(): return lax.ppermute(value, ('dp', 'mp'), pairs)]
    unnamed x21 -> x0, waiting for transfers between devices: 148 us -> none
    all_to_all x3 -> x0, blocking collectives: 56.2 us -> none  [the longest x1 21.6 us: per_device(): lax.all_to_all(ordered_states, 'dp', split_axis=0, concat_axis=1, tiled=T...]
    dot_general x49 -> x44, matrix products: 131 us -> 79.4 us  [dot(): lax.dot_general(left, right, (((left_dim,), (right_dim,)), ((), ())), pre...]
    psum x2 -> x0, blocking collectives: 46.3 us -> none  [the longest x1 40.6 us: per_device(): grad_norm = jnp.sqrt(lax.psum(local_squares, ('dp', 'mp')))]
  transfers between devices with their start and end apart: 24 -> 41, of which waited for: 19 -> 15; matrix products, arithmetic and copies ran while one was open for 14% -> 26% of each run, Pallas kernels for 0% -> 18%
where the time goes in v1:
time: 717 us; the launch traced here: 711 us
  Pallas kernels  229 us (32%)
  waiting for transfers between devices  200 us (28%)
  local copies, waits for them, and re-layouts  96.8 us (14%)
  matrix products  79.4 us (11%)
  other arithmetic  69.3 us (10%)
  starting transfers between devices  29.2 us (4%)
  between operations  7.32 us (1%)
    ppermute x41, waiting for transfers between devices, hop(): return lax.ppermute(value, ('dp', 'mp'), pairs)  200 us
    pallas_call x1, Pallas kernels, closing(): pl.pallas_call(functools.partial(closing_kernel, n), out_shape=[jax.Shape...  92.7 us
    dot_general x44, matrix products, dot(): lax.dot_general(left, right, (((left_dim,), (right_dim,)), ((), ())), pre...  79.4 us
    pallas_call x1, Pallas kernels, entry(): pl.pallas_call(functools.partial(entry_kernel, n), out_shape=[jax.ShapeDt...  76.8 us
    unnamed x215, local copies, waits for them, and re-layouts  36.9 us
    ppermute x41, starting transfers between devices, hop(): return lax.ppermute(value, ('dp', 'mp'), pairs)  29.2 us
    pallas_call x2, Pallas kernels, attend_backward(): pl.pallas_call(functools.partial(attend_backward_kernel, causal, 256), gr...  26.6 us
    dynamic_slice x9, local copies, waits for them, and re-layouts, pick(): return lax.dynamic_index_in_dim(value, index, dim, keepdims=False)  23.3 us
  transfers between devices with their start and end apart: 41, of which 15 were waited for; matrix products, arithmetic and copies ran while one was open for 26% of the time, Pallas kernels for 18%

profile of v1, /device:TPU:0, one launch (start us, length us, event | category | flops | bytes accessed | tf_op | source)
XLA Modules:
  0.0 710.6 jit_solution(18425110838511672369)
XLA Ops:
  7.0 76.8 %entry.1 = (bf16[4,1024,512]{2,1,0:T(8,128)(2,1)S(1)}, f32[8,8,128]{2,1,0:T(8,128)S(1)}, bf16[1024,1024]{1,0:T(8,128)(2,1)S(1)}, bf16[1024,1024]{1,0:T(8,128)(2,1)S(1)}) custom-call(bf16[4,128,256]{2,1,0:T(8,128)(2,1)S(1)} %get-tuple-element.135.w_ref, f32[8,128]{1,0:T(8,128)S(1)} %convert_convert_fusion.p_ref, ...), custom_call_target="tpu_custom_call" | custom-call | tf_op jit(solution)/shard_map/entry/pallas_call | solution.py:406
  87.1 4.1 collective-permute-start.3
  108.4 9.8 %attend_forward.2 = (bf16[512,512]{1,0:T(8,128)(2,1)S(1)}, f32[4,2,512]{2,1,0:T(2,128)S(1)}) custom-call(s32[2]{0:T(128)S(1)} %pad_add_fusion.scalars, bf16[512,512]{1,0:T(8,128)(2,1)S(1)} %convolution_convert_fusion.17.q_ref, bf16[1024,512]{1,0:T(8,128)(2,1)S(1)} %copy-done.20, bf16[1024,512]{1,0:T(8,128)(2,1)S(1)} %copy-done.22), custom_call_target="tpu_custom_call" | custom-call | flops 1073741824 | bytes 3145728 | tf_op jit(solution)/shard_map/attend_forward/pallas_call | solution.py:160
  125.9 18.7 %collective-permute-done.4.refs_1_ = bf16[4,4,128,256]{3,2,1,0:T(8,128)(2,1)S(1)} collective-permute-done((bf16[4,4,128,256]{3,2,1,0:T(8,128)(2,1)S(1)}, bf16[4,4,128,256]{3,2,1,0:T(8,128)(2,1)S(1)}, u32[]{:S(2)}, u32[]{:S(2)}) %collective-permute-start.4) | collective-permute-done | bytes 1048608 | tf_op jit(solution)/shard_map/ppermute | solution.py:54
  147.0 4.4 collective-permute-done.5.refs_2_
  151.3 22.0 %collective-permute-done.6.refs_3_ = bf16[4,4,128,256]{3,2,1,0:T(8,128)(2,1)S(1)} collective-permute-done((bf16[4,4,128,256]{3,2,1,0:T(8,128)(2,1)S(1)}, bf16[4,4,128,256]{3,2,1,0:T(8,128)(2,1)S(1)}, u32[]{:S(2)}, u32[]{:S(2)}) %collective-permute-start.6) | collective-permute-done | bytes 1048608 | tf_op jit(solution)/shard_map/ppermute | solution.py:54
  177.2 9.5 %attend_forward.3 = (bf16[512,512]{1,0:T(8,128)(2,1)S(1)}, f32[4,2,512]{2,1,0:T(2,128)S(1)}) custom-call(s32[2]{0:T(128)S(1)} %pad_add_fusion.1.scalars, bf16[512,512]{1,0:T(8,128)(2,1)S(1)} %convolution_convert_fusion.16.q_ref, bf16[1024,512]{1,0:T(8,128)(2,1)S(1)} %convolution_convert_fusion.3.k_ref, bf16[1024,512]{1,0:T(8,128)(2,1)S(1)} %convolution_convert_fusion.2.v_ref), custom_call_target="tpu_custom_call" | custom-call | flops 1073741824 | bytes 3145728 | tf_op jit(solution)/shard_map/attend_forward/pallas_call | solution.py:160
  188.5 3.9 collective-permute-start.10
  193.3 11.5 %collective-permute-done.10 = bf16[2,128,1024]{2,1,0:T(8,128)(2,1)} collective-permute-done((bf16[2,128,1024]{2,1,0:T(8,128)(2,1)S(1)}, bf16[2,128,1024]{2,1,0:T(8,128)(2,1)}, u32[]{:S(2)}, u32[]{:S(2)}) %collective-permute-start.10) | collective-permute-done | bytes 524320 | tf_op jit(solution)/shard_map/ppermute | solution.py:54
  204.7 33.8 %collective-permute-done.9 = bf16[2,128,1024]{2,1,0:T(8,128)(2,1)} collective-permute-done((bf16[2,128,1024]{2,1,0:T(8,128)(2,1)S(1)}, bf16[2,128,1024]{2,1,0:T(8,128)(2,1)}, u32[]{:S(2)}, u32[]{:S(2)}) %collective-permute-start.9) | collective-permute-done | bytes 524320 | tf_op jit(solution)/shard_map/ppermute | solution.py:54
  238.5 3.1 pad_maximum_fusion.refs_0_
  250.4 9.8 %collective-permute-done.13 = bf16[256,1024]{1,0:T(8,128)(2,1)S(1)} collective-permute-done((bf16[256,1024]{1,0:T(8,128)(2,1)}, bf16[256,1024]{1,0:T(8,128)(2,1)S(1)}, u32[]{:S(2)}, u32[]{:S(2)}) %collective-permute-start.13) | collective-permute-done | bytes 524320 | tf_op jit(solution)/shard_map/ppermute | solution.py:54
  260.4 28.7 %collective-permute-done.11.refs_1_ = bf16[4,2,128,1024]{3,2,1,0:T(8,128)(2,1)} collective-permute-done((bf16[4,2,128,1024]{3,2,1,0:T(8,128)(2,1)}, bf16[4,2,128,1024]{3,2,1,0:T(8,128)(2,1)}, u32[]{:S(2)}, u32[]{:S(2)}) %collective-permute-start.11) | collective-permute-done | bytes 2097184 | tf_op jit(solution)/shard_map/ppermute | solution.py:54
  292.7 2.9 multiply_convert_fusion
  303.7 3.0 reshape.363
  306.9 8.2 %collective-permute-done.16 = bf16[256,1024]{1,0:T(8,128)(2,1)} collective-permute-done((bf16[256,1024]{1,0:T(8,128)(2,1)}, bf16[256,1024]{1,0:T(8,128)(2,1)}, u32[]{:S(2)}, u32[]{:S(2)}) %collective-permute-start.16) | collective-permute-done | bytes 524320 | tf_op jit(solution)/shard_map/ppermute | solution.py:54
  321.2 3.5 constant_dynamic-slice_fusion.2
  324.7 3.5 copy.66
  328.2 2.3 copy.67
  338.9 2.3 fusion.103
  344.2 3.9 fusion.6
  348.1 7.8 %collective-permute-done.19 = bf16[256,1024]{1,0:T(8,128)(2,1)} collective-permute-done((bf16[256,1024]{1,0:T(8,128)(2,1)}, bf16[256,1024]{1,0:T(8,128)(2,1)}, u32[]{:S(2)}, u32[]{:S(2)}) %collective-permute-start.19) | collective-permute-done | bytes 524320 | tf_op jit(solution)/shard_map/ppermute | solution.py:54
  359.2 2.7 reshape.369
  361.9 5.2 constant_dynamic-slice_fusion
  367.1 3.5 copy.68
  370.6 3.6 fusion.151
  374.2 2.4 fusion.139
  377.8 3.5 fusion.13
  388.9 2.3 copy.69
  391.2 4.0 fusion.138
  407.4 7.8 %collective-permute-done.22 = bf16[256,1024]{1,0:T(8,128)(2,1)S(1)} collective-permute-done((bf16[256,1024]{1,0:T(8,128)(2,1)S(1)}, bf16[256,1024]{1,0:T(8,128)(2,1)S(1)}, u32[]{:S(2)}, u32[]{:S(2)}) %collective-permute-start.22) | collective-permute-done | bytes 524320 | tf_op jit(solution)/shard_map/ppermute | solution.py:54
  426.0 12.9 %attend_backward.2 = (bf16[512,512]{1,0:T(8,128)(2,1)S(1)}, bf16[1024,512]{1,0:T(8,128)(2,1)S(1)}, bf16[1024,512]{1,0:T(8,128)(2,1)S(1)}) custom-call(s32[2]{0:T(128)S(1)} %pad_add_fusion.1.scalars, bf16[512,512]{1,0:T(8,128)(2,1)S(1)} %copy-done.19, bf16[1024,512]{1,0:T(8,128)(2,1)S(1)} %copy-done.25, bf16[1024,512]{1,0:T(8,128)(2,1)S(1)} %copy-done.27, ...), custom_call_target="tpu_custom_call" | custom-call | flops 2684354560 | bytes 6291456 | tf_op jit(solution)/shard_map/attend_backward/pallas_call | solution.py:221
  438.9 3.4 fusion.83
  443.3 3.3 fusion.82
  449.3 3.8 convolution_add_fusion
  456.7 2.9 copy.36
  459.6 2.7 constant_dynamic-slice_fusion.14
  462.3 2.5 copy.56
  490.6 10.1 %collective-permute-done.39 = bf16[128,1024]{1,0:T(8,128)(2,1)S(1)} collective-permute-done((bf16[128,1024]{1,0:T(8,128)(2,1)S(1)}, bf16[128,1024]{1,0:T(8,128)(2,1)S(1)}, u32[]{:S(2)}, u32[]{:S(2)}) %collective-permute-start.39) | collective-permute-done | bytes 262176 | tf_op jit(solution)/shard_map/ppermute | solution.py:54
  509.5 13.6 %collective-permute-done.35 = bf16[128,1024]{1,0:T(8,128)(2,1)S(1)} collective-permute-done((bf16[128,1024]{1,0:T(8,128)(2,1)S(1)}, bf16[128,1024]{1,0:T(8,128)(2,1)S(1)}, u32[]{:S(2)}, u32[]{:S(2)}) %collective-permute-start.35) | collective-permute-done | bytes 262176 | tf_op jit(solution)/shard_map/ppermute | solution.py:54
  529.7 13.6 %attend_backward.3 = (bf16[512,512]{1,0:T(8,128)(2,1)S(1)}, bf16[1024,512]{1,0:T(8,128)(2,1)S(1)}, bf16[1024,512]{1,0:T(8,128)(2,1)S(1)}) custom-call(s32[2]{0:T(128)S(1)} %pad_add_fusion.scalars, bf16[512,512]{1,0:T(8,128)(2,1)S(1)} %copy-done.17, bf16[1024,512]{1,0:T(8,128)(2,1)S(1)} %copy-done.21, bf16[1024,512]{1,0:T(8,128)(2,1)S(1)} %copy-done.23, ...), custom_call_target="tpu_custom_call" | custom-call | flops 2684354560 | bytes 6291456 | tf_op jit(solution)/shard_map/attend_backward/pallas_call | solution.py:221
  559.9 92.7 %closing.1 = (f32[4,128,256]{2,1,0:T(8,128)S(1)}, bf16[8,128,256]{2,1,0:T(8,128)(2,1)S(1)}, bf16[8,128,256]{2,1,0:T(8,128)(2,1)S(1)}, f32[8,128]{1,0:T(8,128)S(1)}) custom-call(bf16[1024,512]{1,0:T(8,128)(2,1)S(1)} %convolution_convert_fusion.7.g0_ref, bf16[1024,512]{1,0:T(8,128)(2,1)S(1)} %convolution_convert_fusion.1.g1_ref, ...), custom_call_target="tpu_custom_call" | custom-call | tf_op jit(solution)/shard_map/closing/pallas_call | solution.py:680
  661.0 4.2 collective-permute-done.32
  665.2 17.0 %collective-permute-done.31 = bf16[4,128,256]{2,1,0:T(8,128)(2,1)S(1)} collective-permute-done((bf16[4,128,256]{2,1,0:T(8,128)(2,1)S(1)}, bf16[4,128,256]{2,1,0:T(8,128)(2,1)S(1)}, u32[]{:S(2)}, u32[]{:S(2)}) %collective-permute-start.31) | collective-permute-done | bytes 262176 | tf_op jit(solution)/shard_map/ppermute | solution.py:54
  683.4 2.4 mul.578
  687.9 10.8 %square_sum.1 = f32[8,128]{1,0:T(8,128)} custom-call(f32[8,128]{1,0:T(8,128)} %fusion.125.g_ref), custom_call_target="tpu_custom_call" | custom-call | tf_op jit(solution)/shard_map/square_sum/pallas_call | solution.py:794
  700.8 4.7 multiply_add_fusion.1
  705.6 2.7 multiply_add_fusion
  (435 shorter events, 191.4 us)
Async XLA Ops:
  87.1 31.1 %collective-permute-start.3 = (bf16[4,128,256]{2,1,0:T(8,128)(2,1)S(1)}, bf16[4,128,256]{2,1,0:T(8,128)(2,1)S(1)}, u32[]{:S(2)}, u32[]{:S(2)}) collective-permute-start(bf16[4,128,256]{2,1,0:T(8,128)(2,1)S(1)} %get-tuple-element.45), channel_id=1, source_target_pairs={{0,24},{1,25},{2,26},{3,27},{4,28},{5,29},{6,30},{7,31},{8,0},{9,1... | collective-permute-start | bytes 786440 | tf_op jit(solution)/shard_map/ppermute | solution.py:54
  91.3 27.0 %collective-permute-start.2 = (bf16[4,128,256]{2,1,0:T(8,128)(2,1)S(1)}, bf16[4,128,256]{2,1,0:T(8,128)(2,1)S(1)}, u32[]{:S(2)}, u32[]{:S(2)}) collective-permute-start(bf16[4,128,256]{2,1,0:T(8,128)(2,1)S(1)} %get-tuple-element.45), channel_id=1, source_target_pairs={{0,16},{1,17},{2,18},{3,19},{4,20},{5,21},{6,22},{7,23},{8,24},{9,... | collective-permute-start | bytes 786440 | tf_op jit(solution)/shard_map/ppermute | solution.py:54
  92.0 26.3 %collective-permute-start.1 = (bf16[4,128,256]{2,1,0:T(8,128)(2,1)S(1)}, bf16[4,128,256]{2,1,0:T(8,128)(2,1)}, u32[]{:S(2)}, u32[]{:S(2)}) collective-permute-start(bf16[4,128,256]{2,1,0:T(8,128)(2,1)S(1)} %get-tuple-element.45), channel_id=1, source_target_pairs={{0,8},{1,9},{2,10},{3,11},{4,12},{5,13},{6,14},{7,15},{8,16},{9,17... | collective-permute-start | bytes 786440 | tf_op jit(solution)/shard_map/ppermute | solution.py:54
  102.0 16.2 %copy-start.16 = (bf16[512,512]{1,0:T(8,128)(2,1)}, bf16[512,512]{1,0:T(8,128)(2,1)S(1)}, u32[]{:S(2)}) copy-start(bf16[512,512]{1,0:T(8,128)(2,1)S(1)} %convolution_convert_fusion.17.q_ref) | copy-start | bytes 1572868
  119.5 25.1 %collective-permute-start.4 = (bf16[4,4,128,256]{3,2,1,0:T(8,128)(2,1)S(1)}, bf16[4,4,128,256]{3,2,1,0:T(8,128)(2,1)S(1)}, u32[]{:S(2)}, u32[]{:S(2)}) collective-permute-start(bf16[4,4,128,256]{3,2,1,0:T(8,128)(2,1)S(1)} %pad_maximum_fusion.2.refs_0_), channel_id=1, source_target_pairs={{0,4},{1,5},{2,6},{3,7},{4,0},{5,1},{6,2},{7,3},{8,12},{9,13},{10,... | collective-permute-start | bytes 3145736 | tf_op jit(solution)/shard_map/ppermute | solution.py:54
  123.4 21.8 %collective-permute-start = (bf16[512,1024]{1,0:T(8,128)(2,1)S(1)}, bf16[512,1024]{1,0:T(8,128)(2,1)S(1)}, u32[]{:S(2)}, u32[]{:S(2)}) collective-permute-start(bf16[512,1024]{1,0:T(8,128)(2,1)S(1)} %convolution_convert_fusion.9), channel_id=1, source_target_pairs={{0,1},{1,0},{2,3},{3,2},{4,5},{5,4},{6,7},{7,6},{8,9},{9,8},{10,11... | collective-permute-start | bytes 3145736 | tf_op jit(solution)/shard_map/ppermute | solution.py:54
  125.4 26.0 %collective-permute-start.5 = (bf16[4,4,128,256]{3,2,1,0:T(8,128)(2,1)S(1)}, bf16[4,4,128,256]{3,2,1,0:T(8,128)(2,1)S(1)}, u32[]{:S(2)}, u32[]{:S(2)}) collective-permute-start(bf16[4,4,128,256]{3,2,1,0:T(8,128)(2,1)S(1)} %pad_maximum_fusion.2.refs_0_), channel_id=1, source_target_pairs={{0,2},{1,3},{2,0},{3,1},{4,6},{5,7},{6,4},{7,5},{8,10},{9,11},{10,... | collective-permute-start | bytes 3145736 | tf_op jit(solution)/shard_map/ppermute | solution.py:54
  144.7 28.7 %collective-permute-start.6 = (bf16[4,4,128,256]{3,2,1,0:T(8,128)(2,1)S(1)}, bf16[4,4,128,256]{3,2,1,0:T(8,128)(2,1)S(1)}, u32[]{:S(2)}, u32[]{:S(2)}) collective-permute-start(bf16[4,4,128,256]{3,2,1,0:T(8,128)(2,1)S(1)} %collective-permute-done.4.refs_1_), channel_id=1, source_target_pairs={{0,2},{1,3},{2,0},{3,1},{4,6},{5,7},{6,4},{7,5},{8,10},{9,11},{10,... | collective-permute-start | bytes 3145736 | tf_op jit(solution)/shard_map/ppermute | solution.py:54
  147.0 29.4 %copy-start.60 = (bf16[512,1024]{1,0:T(8,128)(2,1)}, bf16[512,1024]{1,0:T(8,128)(2,1)S(1)}, u32[]{:S(2)}) copy-start(bf16[512,1024]{1,0:T(8,128)(2,1)S(1)} %add_convert_fusion.4) | copy-start | bytes 3145732
  147.0 26.9 %copy-start.12 = (bf16[1024,1024]{1,0:T(8,128)(2,1)S(1)}, bf16[1024,1024]{1,0:T(8,128)(2,1)}, u32[]{:S(2)}) copy-start(bf16[1024,1024]{1,0:T(8,128)(2,1)} %copy-done.11) | copy-start | bytes 6291460
  188.4 53.7 %collective-permute-start.7 = (bf16[512,1024]{1,0:T(8,128)(2,1)}, bf16[512,1024]{1,0:T(8,128)(2,1)}, u32[]{:S(2)}, u32[]{:S(2)}) collective-permute-start(bf16[512,1024]{1,0:T(8,128)(2,1)} %convolution_convert_fusion.8), channel_id=1, source_target_pairs={{0,1},{1,0},{2,3},{3,2},{4,5},{5,4},{6,7},{7,6},{8,9},{9,8},{10,11... | collective-permute-start | bytes 3145736 | tf_op jit(solution)/shard_map/ppermute | solution.py:54
  188.5 16.2 %collective-permute-start.10 = (bf16[2,128,1024]{2,1,0:T(8,128)(2,1)S(1)}, bf16[2,128,1024]{2,1,0:T(8,128)(2,1)}, u32[]{:S(2)}, u32[]{:S(2)}) collective-permute-start(bf16[2,128,1024]{2,1,0:T(8,128)(2,1)S(1)} %convert_element_type.346), channel_id=1, source_target_pairs={{0,24},{1,25},{2,26},{3,27},{4,28},{5,29},{6,30},{7,31},{8,0},{9,1... | collective-permute-start | bytes 1572872 | tf_op jit(solution)/shard_map/ppermute | solution.py:54
  192.4 46.1 %collective-permute-start.9 = (bf16[2,128,1024]{2,1,0:T(8,128)(2,1)S(1)}, bf16[2,128,1024]{2,1,0:T(8,128)(2,1)}, u32[]{:S(2)}, u32[]{:S(2)}) collective-permute-start(bf16[2,128,1024]{2,1,0:T(8,128)(2,1)S(1)} %convert_element_type.346), channel_id=1, source_target_pairs={{0,16},{1,17},{2,18},{3,19},{4,20},{5,21},{6,22},{7,23},{8,24},{9,... | collective-permute-start | bytes 1572872 | tf_op jit(solution)/shard_map/ppermute | solution.py:54
  192.4 46.1 %collective-permute-start.8 = (bf16[2,128,1024]{2,1,0:T(8,128)(2,1)S(1)}, bf16[2,128,1024]{2,1,0:T(8,128)(2,1)}, u32[]{:S(2)}, u32[]{:S(2)}) collective-permute-start(bf16[2,128,1024]{2,1,0:T(8,128)(2,1)S(1)} %convert_element_type.346), channel_id=1, source_target_pairs={{0,8},{1,9},{2,10},{3,11},{4,12},{5,13},{6,14},{7,15},{8,16},{9,17... | collective-permute-start | bytes 1572872 | tf_op jit(solution)/shard_map/ppermute | solution.py:54
  241.6 47.6 %collective-permute-start.11 = (bf16[4,2,128,1024]{3,2,1,0:T(8,128)(2,1)}, bf16[4,2,128,1024]{3,2,1,0:T(8,128)(2,1)}, u32[]{:S(2)}, u32[]{:S(2)}) collective-permute-start(bf16[4,2,128,1024]{3,2,1,0:T(8,128)(2,1)} %pad_maximum_fusion.refs_0_), channel_id=1, source_target_pairs={{0,4},{1,5},{2,6},{3,7},{4,0},{5,1},{6,2},{7,3},{8,12},{9,13},{10,... | collective-permute-start | bytes 6291464 | tf_op jit(solution)/shard_map/ppermute | solution.py:54
  246.7 13.5 %collective-permute-start.13 = (bf16[256,1024]{1,0:T(8,128)(2,1)}, bf16[256,1024]{1,0:T(8,128)(2,1)S(1)}, u32[]{:S(2)}, u32[]{:S(2)}) collective-permute-start(bf16[256,1024]{1,0:T(8,128)(2,1)} %constant_dynamic-slice_fusion.17), channel_id=1, source_target_pairs={{0,2},{1,3},{2,0},{3,1},{4,6},{5,7},{6,4},{7,5},{8,10},{9,11},{10,... | collective-permute-start | bytes 1572872 | tf_op jit(solution)/shard_map/ppermute | solution.py:54
  260.2 32.6 %copy-start.88 = (bf16[256,1024]{1,0:T(8,128)(2,1)}, bf16[256,1024]{1,0:T(8,128)(2,1)S(1)}, u32[]{:S(2)}) copy-start(bf16[256,1024]{1,0:T(8,128)(2,1)S(1)} %collective-permute-done.13) | copy-start | bytes 1572868
  260.2 32.6 %collective-permute-start.14 = (bf16[1,256,1024]{2,1,0:T(8,128)(2,1)S(1)}, bf16[1,256,1024]{2,1,0:T(8,128)(2,1)S(1)}, u32[]{:S(2)}, u32[]{:S(2)}) collective-permute-start(bf16[1,256,1024]{2,1,0:T(8,128)(2,1)S(1)} %bitcast.321), channel_id=1, source_target_pairs={{0,1},{1,0},{2,3},{3,2},{4,5},{5,4},{6,7},{7,6},{8,9},{9,8},{10,11... | collective-permute-start | bytes 1572872 | tf_op jit(solution)/shard_map/ppermute | solution.py:54
  260.4 31.0 %copy-start.51 = (bf16[512,1024]{1,0:T(8,128)(2,1)S(1)}, bf16[512,1024]{1,0:T(8,128)(2,1)}, u32[]{:S(2)}) copy-start(bf16[512,1024]{1,0:T(8,128)(2,1)} %copy-done.50) | copy-start | bytes 3145732
  297.0 3.0 collective-permute-start.15
  299.5 7.4 %collective-permute-start.12 = (bf16[256,1024]{1,0:T(8,128)(2,1)}, bf16[256,1024]{1,0:T(8,128)(2,1)}, u32[]{:S(2)}, u32[]{:S(2)}) collective-permute-start(bf16[256,1024]{1,0:T(8,128)(2,1)} %dynamic-slice_convert_fusion.3), channel_id=1, source_target_pairs={{0,1},{1,0},{2,3},{3,2},{4,5},{5,4},{6,7},{7,6},{8,9},{9,8},{10,11... | collective-permute-start | bytes 1572872 | tf_op jit(solution)/shard_map/ppermute | solution.py:54
  300.9 14.2 %collective-permute-start.16 = (bf16[256,1024]{1,0:T(8,128)(2,1)}, bf16[256,1024]{1,0:T(8,128)(2,1)}, u32[]{:S(2)}, u32[]{:S(2)}) collective-permute-start(bf16[256,1024]{1,0:T(8,128)(2,1)} %fusion.97), channel_id=1, source_target_pairs={{0,2},{1,3},{2,0},{3,1},{4,6},{5,7},{6,4},{7,5},{8,10},{9,11},{10,... | collective-permute-start | bytes 1572872 | tf_op jit(solution)/shard_map/ppermute | solution.py:54
  321.2 20.6 %collective-permute-start.17 = (bf16[256,1024]{1,0:T(8,128)(2,1)}, bf16[256,1024]{1,0:T(8,128)(2,1)}, u32[]{:S(2)}, u32[]{:S(2)}) collective-permute-start(bf16[256,1024]{1,0:T(8,128)(2,1)} %add_convert_fusion.6), channel_id=1, source_target_pairs={{0,1},{1,0},{2,3},{3,2},{4,5},{5,4},{6,7},{7,6},{8,9},{9,8},{10,11... | collective-permute-start | bytes 1572872 | tf_op jit(solution)/shard_map/ppermute | solution.py:54
  341.2 14.7 %collective-permute-start.19 = (bf16[256,1024]{1,0:T(8,128)(2,1)}, bf16[256,1024]{1,0:T(8,128)(2,1)}, u32[]{:S(2)}, u32[]{:S(2)}) collective-permute-start(bf16[256,1024]{1,0:T(8,128)(2,1)} %add_convert_fusion.6), channel_id=1, source_target_pairs={{0,2},{1,3},{2,0},{3,1},{4,6},{5,7},{6,4},{7,5},{8,10},{9,11},{10,... | collective-permute-start | bytes 1572872 | tf_op jit(solution)/shard_map/ppermute | solution.py:54
  355.9 20.8 %collective-permute-start.20 = (bf16[1,256,1024]{2,1,0:T(8,128)(2,1)}, bf16[1,256,1024]{2,1,0:T(8,128)(2,1)}, u32[]{:S(2)}, u32[]{:S(2)}) collective-permute-start(bf16[1,256,1024]{2,1,0:T(8,128)(2,1)} %bitcast.40), channel_id=1, source_target_pairs={{0,1},{1,0},{2,3},{3,2},{4,5},{5,4},{6,7},{7,6},{8,9},{9,8},{10,11... | collective-permute-start | bytes 1572872 | tf_op jit(solution)/shard_map/ppermute | solution.py:54
  358.7 48.7 %collective-permute-start.18 = (bf16[256,1024]{1,0:T(8,128)(2,1)}, bf16[256,1024]{1,0:T(8,128)(2,1)}, u32[]{:S(2)}, u32[]{:S(2)}) collective-permute-start(bf16[256,1024]{1,0:T(8,128)(2,1)} %dynamic-slice_convert_fusion.2), channel_id=1, source_target_pairs={{0,1},{1,0},{2,3},{3,2},{4,5},{5,4},{6,7},{7,6},{8,9},{9,8},{10,11... | collective-permute-start | bytes 1572872 | tf_op jit(solution)/shard_map/ppermute | solution.py:54
  383.7 16.1 %collective-permute-start.21 = (bf16[1,256,1024]{2,1,0:T(8,128)(2,1)}, bf16[1,256,1024]{2,1,0:T(8,128)(2,1)}, u32[]{:S(2)}, u32[]{:S(2)}) collective-permute-start(bf16[1,256,1024]{2,1,0:T(8,128)(2,1)} %fusion.100), channel_id=1, source_target_pairs={{0,1},{1,0},{2,3},{3,2},{4,5},{5,4},{6,7},{7,6},{8,9},{9,8},{10,11... | collective-permute-start | bytes 1572872 | tf_op jit(solution)/shard_map/ppermute | solution.py:54
  401.3 13.9 %collective-permute-start.22 = (bf16[256,1024]{1,0:T(8,128)(2,1)S(1)}, bf16[256,1024]{1,0:T(8,128)(2,1)S(1)}, u32[]{:S(2)}, u32[]{:S(2)}) collective-permute-start(bf16[256,1024]{1,0:T(8,128)(2,1)S(1)} %fusion.99), channel_id=1, source_target_pairs={{0,2},{1,3},{2,0},{3,1},{4,6},{5,7},{6,4},{7,5},{8,10},{9,11},{10,... | collective-permute-start | bytes 1572872 | tf_op jit(solution)/shard_map/ppermute | solution.py:54
  403.6 69.8 %collective-permute-start.37 = (bf16[4,128,1024]{2,1,0:T(8,128)(2,1)}, bf16[4,128,1024]{2,1,0:T(8,128)(2,1)}, u32[]{:S(2)}, u32[]{:S(2)}) collective-permute-start(bf16[4,128,1024]{2,1,0:T(8,128)(2,1)} %bitcast.101), channel_id=1, source_target_pairs={{0,4},{1,5},{2,6},{3,7},{4,0},{5,1},{6,2},{7,3},{8,12},{9,13},{10,... | collective-permute-start | bytes 3145736 | tf_op jit(solution)/shard_map/ppermute | solution.py:54
  406.0 76.8 %collective-permute-start.33 = (bf16[4,128,1024]{2,1,0:T(8,128)(2,1)}, bf16[4,128,1024]{2,1,0:T(8,128)(2,1)}, u32[]{:S(2)}, u32[]{:S(2)}) collective-permute-start(bf16[4,128,1024]{2,1,0:T(8,128)(2,1)} %bitcast.90), channel_id=1, source_target_pairs={{0,4},{1,5},{2,6},{3,7},{4,0},{5,1},{6,2},{7,3},{8,12},{9,13},{10,... | collective-permute-start | bytes 3145736 | tf_op jit(solution)/shard_map/ppermute | solution.py:54
  418.2 5.2 collective-permute-start.23
  449.0 52.6 %collective-permute-start.24 = (bf16[256,1024]{1,0:T(8,128)(2,1)}, bf16[256,1024]{1,0:T(8,128)(2,1)}, u32[]{:S(2)}, u32[]{:S(2)}) collective-permute-start(bf16[256,1024]{1,0:T(8,128)(2,1)} %dynamic-slice_convert_fusion.1), channel_id=1, source_target_pairs={{0,1},{1,0},{2,3},{3,2},{4,5},{5,4},{6,7},{7,6},{8,9},{9,8},{10,11... | collective-permute-start | bytes 1572872 | tf_op jit(solution)/shard_map/ppermute | solution.py:54
  464.8 59.4 %collective-permute-start.26 = (bf16[1024,2,256]{2,0,1:T(8,128)(2,1)}, bf16[1024,2,256]{2,0,1:T(8,128)(2,1)}, u32[]{:S(2)}, u32[]{:S(2)}) collective-permute-start(bf16[1024,2,256]{2,0,1:T(8,128)(2,1)} %bitcast.317), channel_id=1, source_target_pairs={{0,1},{1,0},{2,3},{3,2},{4,5},{5,4},{6,7},{7,6},{8,9},{9,8},{10,11... | collective-permute-start | bytes 3145736 | tf_op jit(solution)/shard_map/ppermute | solution.py:54
  475.1 14.9 %collective-permute-start.40 = (bf16[128,1024]{1,0:T(8,128)(2,1)S(1)}, bf16[128,1024]{1,0:T(8,128)(2,1)S(1)}, u32[]{:S(2)}, u32[]{:S(2)}) collective-permute-start(bf16[128,1024]{1,0:T(8,128)(2,1)S(1)} %get-tuple-element.105), channel_id=1, source_target_pairs={{0,24},{1,25},{2,26},{3,27},{4,28},{5,29},{6,30},{7,31},{8,0},{9,1... | collective-permute-start | bytes 786440 | tf_op jit(solution)/shard_map/ppermute | solution.py:54
  475.2 25.5 %collective-permute-start.39 = (bf16[128,1024]{1,0:T(8,128)(2,1)S(1)}, bf16[128,1024]{1,0:T(8,128)(2,1)S(1)}, u32[]{:S(2)}, u32[]{:S(2)}) collective-permute-start(bf16[128,1024]{1,0:T(8,128)(2,1)S(1)} %get-tuple-element.106), channel_id=1, source_target_pairs={{0,16},{1,17},{2,18},{3,19},{4,20},{5,21},{6,22},{7,23},{8,24},{9,... | collective-permute-start | bytes 786440 | tf_op jit(solution)/shard_map/ppermute | solution.py:54
  482.8 17.8 %collective-permute-start.38 = (bf16[128,1024]{1,0:T(8,128)(2,1)S(1)}, bf16[128,1024]{1,0:T(8,128)(2,1)S(1)}, u32[]{:S(2)}, u32[]{:S(2)}) collective-permute-start(bf16[128,1024]{1,0:T(8,128)(2,1)S(1)} %get-tuple-element.104), channel_id=1, source_target_pairs={{0,8},{1,9},{2,10},{3,11},{4,12},{5,13},{6,14},{7,15},{8,16},{9,17... | collective-permute-start | bytes 786440 | tf_op jit(solution)/shard_map/ppermute | solution.py:54
  490.0 58.9 %collective-permute-start.28 = (bf16[4,1024,256]{2,1,0:T(8,128)(2,1)}, bf16[4,1024,256]{2,1,0:T(8,128)(2,1)}, u32[]{:S(2)}, u32[]{:S(2)}) collective-permute-start(bf16[4,1024,256]{2,1,0:T(8,128)(2,1)} %pad_maximum_fusion.1), channel_id=1, source_target_pairs={{0,2},{1,3},{2,0},{3,1},{4,6},{5,7},{6,4},{7,5},{8,10},{9,11},{10,... | collective-permute-start | bytes 6291464 | tf_op jit(solution)/shard_map/ppermute | solution.py:54
  500.7 8.9 %collective-permute-start.36 = (bf16[128,1024]{1,0:T(8,128)(2,1)S(1)}, bf16[128,1024]{1,0:T(8,128)(2,1)S(1)}, u32[]{:S(2)}, u32[]{:S(2)}) collective-permute-start(bf16[128,1024]{1,0:T(8,128)(2,1)S(1)} %get-tuple-element.102), channel_id=1, source_target_pairs={{0,24},{1,25},{2,26},{3,27},{4,28},{5,29},{6,30},{7,31},{8,0},{9,1... | collective-permute-start | bytes 786440 | tf_op jit(solution)/shard_map/ppermute | solution.py:54
  500.7 22.4 %collective-permute-start.35 = (bf16[128,1024]{1,0:T(8,128)(2,1)S(1)}, bf16[128,1024]{1,0:T(8,128)(2,1)S(1)}, u32[]{:S(2)}, u32[]{:S(2)}) collective-permute-start(bf16[128,1024]{1,0:T(8,128)(2,1)S(1)} %get-tuple-element.103), channel_id=1, source_target_pairs={{0,16},{1,17},{2,18},{3,19},{4,20},{5,21},{6,22},{7,23},{8,24},{9,... | collective-permute-start | bytes 786440 | tf_op jit(solution)/shard_map/ppermute | solution.py:54
  501.6 21.5 %collective-permute-start.34 = (bf16[128,1024]{1,0:T(8,128)(2,1)S(1)}, bf16[128,1024]{1,0:T(8,128)(2,1)S(1)}, u32[]{:S(2)}, u32[]{:S(2)}) collective-permute-start(bf16[128,1024]{1,0:T(8,128)(2,1)S(1)} %get-tuple-element.101), channel_id=1, source_target_pairs={{0,8},{1,9},{2,10},{3,11},{4,12},{5,13},{6,14},{7,15},{8,16},{9,17... | collective-permute-start | bytes 786440 | tf_op jit(solution)/shard_map/ppermute | solution.py:54
  507.6 16.6 %copy-start.46 = (f32[1024,2,1,256]{3,0,1,2:T(8,128)S(1)}, f32[1024,2,1,256]{3,0,1,2:T(8,128)}, u32[]{:S(2)}) copy-start(f32[1024,2,1,256]{3,0,1,2:T(8,128)} %copy.36) | copy-start | bytes 6291460
  509.5 17.0 %collective-permute-start.25 = (bf16[256,1024]{1,0:T(8,128)(2,1)}, bf16[256,1024]{1,0:T(8,128)(2,1)}, u32[]{:S(2)}, u32[]{:S(2)}) collective-permute-start(bf16[256,1024]{1,0:T(8,128)(2,1)} %get-tuple-element.86), channel_id=1, source_target_pairs={{0,1},{1,0},{2,3},{3,2},{4,5},{5,4},{6,7},{7,6},{8,9},{9,8},{10,11... | collective-permute-start | bytes 1572872 | tf_op jit(solution)/shard_map/ppermute | solution.py:54
  525.9 32.9 %collective-permute-start.27 = (bf16[1024,256]{1,0:T(8,128)(2,1)S(1)}, bf16[1024,256]{1,0:T(8,128)(2,1)S(1)}, u32[]{:S(2)}, u32[]{:S(2)}) collective-permute-start(bf16[1024,256]{1,0:T(8,128)(2,1)S(1)} %fusion.96), channel_id=1, source_target_pairs={{0,2},{1,3},{2,0},{3,1},{4,6},{5,7},{6,4},{7,5},{8,10},{9,11},{10,... | collective-permute-start | bytes 1572872 | tf_op jit(solution)/shard_map/ppermute | solution.py:54
  553.1 101.9 %collective-permute-start.29 = (bf16[4,4,128,256]{3,2,0,1:T(8,128)(2,1)}, bf16[4,4,128,256]{3,2,0,1:T(8,128)(2,1)}, u32[]{:S(2)}, u32[]{:S(2)}) collective-permute-start(bf16[4,4,128,256]{3,2,0,1:T(8,128)(2,1)} %fusion.54), channel_id=1, source_target_pairs={{0,4},{1,5},{2,6},{3,7},{4,0},{5,1},{6,2},{7,3},{8,12},{9,13},{10,... | collective-permute-start | bytes 3145736 | tf_op jit(solution)/shard_map/ppermute | solution.py:54
  657.3 7.9 %collective-permute-start.32 = (bf16[4,128,256]{2,1,0:T(8,128)(2,1)S(1)}, bf16[4,128,256]{2,1,0:T(8,128)(2,1)S(1)}, u32[]{:S(2)}, u32[]{:S(2)}) collective-permute-start(bf16[4,128,256]{2,1,0:T(8,128)(2,1)S(1)} %get-tuple-element.108), channel_id=1, source_target_pairs={{0,24},{1,25},{2,26},{3,27},{4,28},{5,29},{6,30},{7,31},{8,0},{9,1... | collective-permute-start | bytes 786440 | tf_op jit(solution)/shard_map/ppermute | solution.py:54
  657.4 24.9 %collective-permute-start.31 = (bf16[4,128,256]{2,1,0:T(8,128)(2,1)S(1)}, bf16[4,128,256]{2,1,0:T(8,128)(2,1)S(1)}, u32[]{:S(2)}, u32[]{:S(2)}) collective-permute-start(bf16[4,128,256]{2,1,0:T(8,128)(2,1)S(1)} %get-tuple-element.109), channel_id=1, source_target_pairs={{0,16},{1,17},{2,18},{3,19},{4,20},{5,21},{6,22},{7,23},{8,24},{9,... | collective-permute-start | bytes 786440 | tf_op jit(solution)/shard_map/ppermute | solution.py:54
  659.5 22.8 %collective-permute-start.30 = (bf16[4,128,256]{2,1,0:T(8,128)(2,1)S(1)}, bf16[4,128,256]{2,1,0:T(8,128)(2,1)S(1)}, u32[]{:S(2)}, u32[]{:S(2)}) collective-permute-start(bf16[4,128,256]{2,1,0:T(8,128)(2,1)S(1)} %get-tuple-element.107), channel_id=1, source_target_pairs={{0,8},{1,9},{2,10},{3,11},{4,12},{5,13},{6,14},{7,15},{8,16},{9,17... | collective-permute-start | bytes 786440 | tf_op jit(solution)/shard_map/ppermute | solution.py:54
  683.4 17.3 %copy-start.56 = (f32[8,128,256]{2,1,0:T(8,128)S(1)}, f32[8,128,256]{2,1,0:T(8,128)}, u32[]{:S(2)}) copy-start(f32[8,128,256]{2,1,0:T(8,128)} %param.26) | copy-start | bytes 3145732
  (98 other events, 336.3 us)

commit v2 on v1

v2 whole, which is shorter than its diff:
```python
import functools

import jax
import jax.numpy as jnp
from jax import lax
from jax.experimental import pallas as pl
from jax.experimental.pallas import tpu as pltpu
from jax.sharding import PartitionSpec as P

HD = 64
STEP = 10


EPSILON = 1e-05
NEGATIVE = -1000000000.0
BETA_FIRST = 0.9
BETA_SECOND = 0.999
ADAM_EPSILON = 1e-08
MATRIX_RATE = 0.05
NORM_RATE = 1.0
MATRIX_DECAY = 0.1
AVERAGING = 0.7
THRESHOLD = 1.0
BF = jnp.bfloat16
F32 = jnp.float32


def grid_sizes():
    dp = lax.axis_size("dp")
    mp = lax.axis_size("mp")
    ny = 1 << ((dp.bit_length() - 1) // 2)
    return {"z": dp // ny, "y": ny, "x": mp // 2, "c": 2}


def grid_place():
    n = grid_sizes()
    dp = lax.axis_index("dp")
    mp = lax.axis_index("mp")
    return {"z": dp // n["y"], "y": dp % n["y"], "x": mp // 2, "c": mp % 2}


def dot(left, right, left_dim, right_dim):
    return lax.dot_general(
        left, right, (((left_dim,), (right_dim,)), ((), ())), preferred_element_type=F32
    )


PAIR = 2 * HD


def only_head(value, head):
    lane = lax.broadcasted_iota(jnp.int32, value.shape, 1)
    keep = (lane < HD) if head == 0 else (lane >= HD)
    return jnp.where(keep, value, jnp.zeros_like(value))


def attend_pair(p, chunk, bound, q_ref, k_ref, v_ref, o_ref, sum_ref, score_ref, weight_ref):
    lanes = pl.ds(pl.multiple_of(p * PAIR, PAIR), PAIR)
    keys = k_ref.shape[0]
    queries = q_ref[:, lanes] * BF(HD**-0.5)
    values = v_ref[:, lanes]
    mixed = []
    for head in range(2):
        masked = only_head(queries, head)
        top = None
        for start in range(0, keys, chunk):
            block = slice(start, start + chunk)
            scores = dot(k_ref[block, lanes], masked, 1, 1)
            position = lax.broadcasted_iota(jnp.int32, scores.shape, 0) + start
            scores = jnp.where(position < bound, scores, NEGATIVE)
            score_ref[head, block, :] = scores
            highest = jnp.max(scores, axis=0, keepdims=True)
            top = highest if top is None else jnp.maximum(top, highest)
        total = None
        for start in range(0, keys, chunk):
            block = slice(start, start + chunk)
            raised = jnp.exp(score_ref[head, block, :] - top)
            part = jnp.sum(raised, axis=0, keepdims=True)
            total = part if total is None else total + part
            weight_ref[head, block, :] = raised.astype(BF)
        out = dot(values, weight_ref[head], 0, 0)[head * HD : (head + 1) * HD]
        mixed.append(out * (1.0 / total))
        sum_ref[p, head : head + 1, :] = top + jnp.log(total)
    o_ref[:, lanes] = jnp.concatenate(mixed, axis=0).T.astype(BF)


def attend_pair_back(
    p, chunk, bound, q_ref, k_ref, v_ref, o_ref, sum_ref, g_ref, dq_ref, dk_ref, dv_ref, ds_ref
):
    lanes = pl.ds(pl.multiple_of(p * PAIR, PAIR), PAIR)
    keys = k_ref.shape[0]
    queries = q_ref[:, lanes] * BF(HD**-0.5)
    grads = g_ref[:, lanes]
    product = (grads.astype(F32) * o_ref[:, lanes].astype(F32)).T
    head_q = [only_head(queries, head) for head in range(2)]
    head_g = [only_head(grads, head) for head in range(2)]
    shift = [
        jnp.sum(product[head * HD : (head + 1) * HD], axis=0, keepdims=True) for head in range(2)
    ]
    for start in range(0, keys, chunk):
        block = slice(start, start + chunk)
        key_block, value_block = k_ref[block, lanes], v_ref[block, lanes]
        grad_value, grad_key = 0.0, 0.0
        for head in range(2):
            scores = dot(key_block, head_q[head], 1, 1)
            position = lax.broadcasted_iota(jnp.int32, scores.shape, 0) + start
            scores = jnp.where(position < bound, scores, NEGATIVE)
            weights = jnp.exp(scores - sum_ref[p, head : head + 1, :])
            grad_weights = dot(value_block, head_g[head], 1, 1)
            grad_scores = (weights * (grad_weights - shift[head])).astype(BF)
            ds_ref[head, block, :] = grad_scores
            grad_value = grad_value + dot(weights.astype(BF), head_g[head], 1, 0)
            grad_key = grad_key + dot(grad_scores, head_q[head], 1, 0)
        dv_ref[block, lanes] = grad_value.astype(BF)
        dk_ref[block, lanes] = grad_key.astype(BF)
    key_all = k_ref[:, lanes]
    parts = [dot(key_all, ds_ref[h], 0, 0)[h * HD : (h + 1) * HD] for h in range(2)]
    dq_ref[:, lanes] = (jnp.concatenate(parts, axis=0).T * HD**-0.5).astype(BF)


class Wires:
    def __init__(self, sizes, place, send_sem, recv_sem):
        self.sizes, self.place = sizes, place
        self.send_sem, self.recv_sem = send_sem, recv_sem
        self.count = 0
        self.started = []

    def peer(self, z=0, y=0, x=0, c=0):
        n, at = self.sizes, self.place
        pz, py = (at["z"] + z) % n["z"], (at["y"] + y) % n["y"]
        px, pc = (at["x"] + x) % n["x"], (at["c"] + c) % 2
        return (pz * n["y"] + py, px * 2 + pc)

    def send(self, src, dst, **shift):
        copy = pltpu.make_async_remote_copy(
            src_ref=src,
            dst_ref=dst,
            send_sem=self.send_sem.at[self.count],
            recv_sem=self.recv_sem.at[self.count],
            device_id=self.peer(**shift),
            device_id_type=pl.DeviceIdType.MESH,
        )
        self.count += 1
        copy.start()
        self.started.append(copy)
        return copy

    def greet(self, shifts):
        barrier = pltpu.get_barrier_semaphore()
        for shift in shifts:
            pl.semaphore_signal(
                barrier, inc=1, device_id=self.peer(**shift), device_id_type=pl.DeviceIdType.MESH
            )
        pl.semaphore_wait(barrier, len(shifts))

    def close(self):
        for copy in self.started:
            copy.wait_send()


def dp_shifts(n):
    return [{"z": z, "y": y} for z in range(n["z"]) for y in range(n["y"]) if z or y]


def mp_shifts(n):
    return [{"x": x, "c": c} for x in range(n["x"]) for c in range(2) if x or c]


def entry_kernel(
    n, w_ref, p_ref, s_ref, m_ref, ow_ref, op_ref, os_ref, om_ref, send_sem, recv_sem, local_sem
):
    at = grid_place()
    z, y, x, c = at["z"], at["y"], at["x"], at["c"]
    data = z * n["y"] + y
    wires = Wires(n, at, send_sem, recv_sem)
    wires.greet(
        dp_shifts(n) + [{"x": s} for s in range(1, n["x"])] + [{"c": 1}]
    )
    rows, wide = w_ref.shape[1], w_ref.shape[2]
    lines, deep = s_ref.shape[1], s_ref.shape[2]

    def spot(sz, sy, sx, mats=slice(None)):
        block = ((z - sz) % n["z"]) * n["y"] + (y - sy) % n["y"]
        column = (x - sx) % n["x"]
        return ow_ref.at[
            mats,
            pl.ds(pl.multiple_of(block * rows, rows), rows),
            pl.ds(pl.multiple_of(column * wide, wide), wide),
        ]

    def column(ref, sx, sc):
        index = ((x - sx) % n["x"]) * 2 + (c - sc) % 2
        return ref.at[:, pl.ds(pl.multiple_of(index * deep, deep), deep)]

    def patch(ref):
        index = x * 2 + c
        return ref.at[
            pl.ds(pl.multiple_of(data * lines, lines), lines),
            pl.ds(pl.multiple_of(index * deep, deep), deep),
        ]

    def stripe(ref):
        return ref.at[data]

    own = [
        pltpu.make_async_copy(w_ref, spot(0, 0, 0), local_sem.at[0]),
        pltpu.make_async_copy(p_ref, stripe(op_ref), local_sem.at[1]),
        pltpu.make_async_copy(s_ref.at[data], patch(os_ref), local_sem.at[2]),
        pltpu.make_async_copy(m_ref.at[data], patch(om_ref), local_sem.at[3]),
    ]
    for copy in own:
        copy.start()

    def spread(ref, out):
        copies = []
        for shift in dp_shifts(n):
            target = wires.peer(**shift)[0]
            copies.append(wires.send(ref.at[target], patch(out), **shift))
        return copies

    def forward_columns(out, copies):
        for copy in copies:
            copy.wait_recv()
        near = [wires.send(column(out, 0, 0), column(out, 0, 0), x=s) for s in range(1, n["x"])]
        pair = [wires.send(column(out, 0, 0), column(out, 0, 0), c=1)]
        return near, pair

    def finish_columns(out, near, pair):
        for s in range(1, n["x"]):
            near[s - 1].wait_recv()
            pair.append(wires.send(column(out, s, 0), column(out, s, 0), c=1))
        for copy in pair:
            copy.wait_recv()

    to_z = {s: wires.send(w_ref, spot(0, 0, 0), z=s) for s in range(1, n["z"])}
    to_y = {(0, s): wires.send(w_ref, spot(0, 0, 0), y=s) for s in range(1, n["y"])}
    to_x = {(0, s): wires.send(w_ref, spot(0, 0, 0), x=s) for s in range(1, n["x"])}
    params = [wires.send(p_ref, stripe(op_ref), **shift) for shift in dp_shifts(n)]
    states = spread(s_ref, os_ref)
    memory = spread(m_ref, om_ref)

    for sz in range(1, n["z"]):
        to_z[sz].wait_recv()
        for s in range(1, n["y"]):
            to_y[sz, s] = wires.send(spot(sz, 0, 0), spot(sz, 0, 0), y=s)
        for s in range(1, n["x"]):
            to_x[sz, s] = wires.send(spot(sz, 0, 0), spot(sz, 0, 0), x=s)
    for copy in own:
        copy.wait()
    states = forward_columns(os_ref, states)
    last = []
    cut = max(1, w_ref.shape[0] // 4)
    for sz in range(n["z"]):
        for sy in range(1, n["y"]):
            to_y[sz, sy].wait_recv()
            part = spot(sz, sy, 0, slice(0, cut))
            for s in range(1, n["x"]):
                last.append(wires.send(part, part, x=s))
        for sx in range(1, n["x"]):
            to_x[sz, sx].wait_recv()
            part = spot(sz, 0, sx, slice(cut, w_ref.shape[0]))
            for s in range(1, n["y"]):
                last.append(wires.send(part, part, y=s))
    memory = forward_columns(om_ref, memory)
    finish_columns(os_ref, *states)
    finish_columns(om_ref, *memory)
    for copy in params + last:
        copy.wait_recv()
    wires.close()


def entry(weights, params, states, memory):
    n = grid_sizes()
    count, rows, wide = weights.shape
    utterances, lines, deep = states.shape
    nz, ny, nx = n["z"], n["y"], n["x"]
    data = nz * ny
    copies = (
        (nz - 1)
        + nz * (ny - 1 + nx - 1)
        + 2 * nz * (ny - 1) * (nx - 1)
        + 3 * (data - 1)
        + 2 * (2 * (nx - 1) + 1)
    )
    hbm = pl.BlockSpec(memory_space=pl.ANY)
    return pl.pallas_call(
        functools.partial(entry_kernel, n),
        out_shape=[
            jax.ShapeDtypeStruct((count, data * rows, nx * wide), BF),
            jax.ShapeDtypeStruct((data,) + params.shape, F32),
            jax.ShapeDtypeStruct((data * lines, 2 * nx * deep), BF),
            jax.ShapeDtypeStruct((data * lines, 2 * nx * deep), BF),
        ],
        in_specs=[pl.BlockSpec(memory_space=pltpu.VMEM)] * 4,
        out_specs=[hbm] * 4,
        scratch_shapes=[
            pltpu.SemaphoreType.DMA((copies,)),
            pltpu.SemaphoreType.DMA((copies,)),
            pltpu.SemaphoreType.DMA((4,)),
        ],
        compiler_params=pltpu.CompilerParams(
            collective_id=0, has_side_effects=True, vmem_limit_bytes=16 * 2**20
        ),
        name="entry",
    )(weights, params, states, memory)


def loop_rows(total, step, body):
    def one(i, carry):
        body(pl.ds(pl.multiple_of(i * step, step), step))
        return carry

    lax.fori_loop(0, total // step, one, 0)


def shifted(rows, offset):
    return pl.ds(pl.multiple_of(rows.start + offset, rows.size), rows.size)


def mat_rows(out_ref, left_ref, right_ref, total, step, offset=0):
    def body(rows):
        left = left_ref[shifted(rows, offset), :]
        out_ref[rows, :] = dot(left, right_ref[...], 1, 0).astype(BF)

    loop_rows(total, step, body)


class Moves:
    def __init__(self, sem):
        self.sem = sem
        self.count = 0
        self.open = []

    def start(self, src, dst):
        copy = pltpu.make_async_copy(src, dst, self.sem.at[self.count])
        self.count += 1
        copy.start()
        return copy

    def store(self, src, dst):
        self.open.append(self.start(src, dst))

    def close(self):
        for copy in self.open:
            copy.wait()


class Gather:
    def __init__(self, wires, src, out, by_x, cut):
        self.wires, self.src, self.out = wires, src, out
        self.n, self.at = wires.sizes, wires.place
        self.by_x, self.cut = by_x, cut
        self.to_z, self.to_y, self.to_x = {}, {}, {}
        self.last = []
        nz = self.n["z"]
        self.order = [0] + sorted(range(1, nz), key=lambda s: min(s, nz - s))

    def spot(self, sz, sy, sx, mats=slice(None)):
        rows, wide = self.src.shape[1], self.src.shape[2]
        n, at = self.n, self.at
        block = ((at["z"] - sz) % n["z"]) * n["y"] + (at["y"] - sy) % n["y"]
        column = (at["x"] - sx) % n["x"] if self.by_x else 0
        return self.out.at[
            mats,
            pl.ds(pl.multiple_of(block * rows, rows), rows),
            pl.ds(pl.multiple_of(column * wide, wide), wide),
        ]

    def fan(self, sz):
        src = self.src if sz == 0 else self.spot(sz, 0, 0)
        spot = self.spot(sz, 0, 0)
        for s in range(1, self.n["y"]):
            self.to_y[sz, s] = self.wires.send(src, spot, y=s)
        if self.by_x:
            for s in range(1, self.n["x"]):
                self.to_x[sz, s] = self.wires.send(src, spot, x=s)

    def start_z(self, place):
        if place < len(self.order):
            s = self.order[place]
            self.to_z[s] = self.wires.send(self.src, self.spot(0, 0, 0), z=s)

    def corner(self, sz):
        for sy in range(1, self.n["y"]):
            self.to_y[sz, sy].wait_recv()
            if self.by_x and self.cut:
                part = self.spot(sz, sy, 0, slice(0, self.cut))
                for s in range(1, self.n["x"]):
                    self.last.append(self.wires.send(part, part, x=s))
        if self.by_x:
            for sx in range(1, self.n["x"]):
                self.to_x[sz, sx].wait_recv()
                if self.cut < self.src.shape[0]:
                    part = self.spot(sz, 0, sx, slice(self.cut, self.src.shape[0]))
                    for s in range(1, self.n["y"]):
                        self.last.append(self.wires.send(part, part, y=s))

    def arrive(self, place):
        sz = self.order[place]
        self.to_z[sz].wait_recv()
        self.start_z(place + 1)
        self.fan(sz)

    def begin(self):
        self.start_z(1)
        self.fan(0)

    def steps(self):
        count = len(self.order)
        for place in range(1, count):
            yield functools.partial(self.arrive, place)
            yield functools.partial(self.corner, self.order[place - 1])
        yield functools.partial(self.corner, self.order[count - 1])
        yield self.finish

    def finish(self):
        for copy in self.last:
            copy.wait_recv()

    @staticmethod
    def copies(n, by_x, cut, count):
        nz, ny, nx = n["z"], n["y"], n["x"]
        total = nz - 1 + nz * (ny - 1)
        if by_x:
            total += nz * (nx - 1) + 2 * nz * (ny - 1) * (nx - 1)
        return total


def norm_rows(values, p_ref, index):
    centered = values - jnp.mean(values, axis=-1, keepdims=True)
    variance = jnp.mean(centered * centered, axis=-1, keepdims=True)
    normed = centered * lax.rsqrt(variance + EPSILON)
    return (normed * p_ref[index : index + 1, :] + p_ref[index + 4 : index + 5, :]).astype(BF)


STRIP = 256


def forward_kernel(
    n, own_rows, length, reach, x_hbm, m_hbm, w_hbm, p_ref, wc_ref, wf_ref,
    owc, owf, oh1, oq, ok, ov, oo, ol, ox1, oh2, oq2, ok2, ov2, oo2, ol2, ox2, oh3,
    x_s, m_s, w_s, c_s, h1_s, q_s, k_s, v_s, o_s, l_s, x1_s, h2_s, q2_s, k2_s, v2_s, o2_s, l2_s,
    x2_s, h3_s, give_s, got_s, score_s, weight_s, send_sem, recv_sem, move_sem,
):
    at = grid_place()
    wires = Wires(n, at, send_sem, recv_sem)
    moves = Moves(move_sem)
    get_x = moves.start(x_hbm, x_s)
    get_w = moves.start(w_hbm, w_s)
    get_m = moves.start(m_hbm, m_s)
    wires.greet(
        [{"z": s} for s in range(1, n["z"])]
        + [{"y": s} for s in range(1, n["y"])]
        + [{"x": s} for s in range(1, n["x"])]
        + [{"c": 1}]
    )
    cross = Gather(wires, wc_ref, c_s, True, 3)
    cross.begin()
    own_cross = moves.start(wc_ref, cross.spot(0, 0, 0))
    up_down = Gather(wires, wf_ref, owf, False, 0)
    own_ffn = moves.start(wf_ref, up_down.spot(0, 0, 0))
    first, second = list(cross.steps()), list(up_down.steps())
    zone = 2 * (n["z"] - 1)
    queue = first[:zone] + [up_down.begin] + first[zone:]
    for i, step in enumerate(second):
        queue.insert(min(len(queue), zone + 2 + 2 * i), step)
    needed = queue.index(first[-1]) + 1
    done = [0]

    def advance(limit):
        while done[0] < min(limit, len(queue)):
            queue[done[0]]()
            done[0] += 1

    slot, width = x_s.shape
    chip_rows = 2 * own_rows
    chip_start = at["x"] * chip_rows
    strip = min(STRIP, own_rows)
    pairs = q_s.shape[1] // PAIR
    own = pl.ds(pl.multiple_of(at["c"] * own_rows, own_rows), own_rows)

    get_x.wait()

    def first_norm(rows):
        h1_s[rows, :] = norm_rows(x_s[rows, :].astype(F32), p_ref, 0)

    loop_rows(slot, strip, first_norm)
    get_w.wait()
    advance(1)
    moves.store(h1_s, oh1)
    mat_rows(q_s, h1_s, w_s.at[0], chip_rows, strip, chip_start)
    mat_rows(k_s, h1_s, w_s.at[1], slot, strip)
    advance(2)
    mat_rows(v_s, h1_s, w_s.at[2], slot, strip)
    advance(3)
    for ref, out in ((q_s, oq), (k_s, ok), (v_s, ov)):
        moves.store(ref, out)
    reach_self = lax.broadcasted_iota(jnp.int32, (1, chip_rows), 1) + chip_start + 1
    reach_self = jnp.minimum(reach_self, length[0])
    for p in range(pairs):
        attend_pair(p, 256, reach_self, q_s, k_s, v_s, o_s, l_s, score_s, weight_s)
        advance(4 + p)
    moves.store(o_s, oo)
    moves.store(l_s, ol)

    def give(index, mixed, out_map):
        def body(rows):
            give_s[index, rows, :] = dot(mixed[rows, :], out_map[...], 1, 1).astype(BF)

        loop_rows(chip_rows, strip, body)
        return wires.send(give_s.at[index], got_s.at[index], c=1)

    def total(index, rows):
        return give_s[index, rows, :].astype(F32) + got_s[index, rows, :].astype(F32)

    swap = give(0, o_s, w_s.at[3])
    get_m.wait()
    swap.wait_recv()

    def second_norm(rows):
        values = x_s[shifted(rows, chip_start), :].astype(F32) + total(0, rows)
        x1_s[rows, :] = values
        h2_s[rows, :] = norm_rows(values, p_ref, 1)

    loop_rows(chip_rows, strip, second_norm)
    moves.store(x1_s.at[own], ox1)
    moves.store(h2_s, oh2)
    advance(needed)
    own_cross.wait()
    moves.store(c_s, owc)
    mat_rows(q2_s, h2_s, c_s.at[0], chip_rows, strip)
    mat_rows(k2_s, m_s, c_s.at[1], slot, strip)
    mat_rows(v2_s, m_s, c_s.at[2], slot, strip)
    advance(needed + 1)
    for ref, out in ((q2_s, oq2), (k2_s, ok2), (v2_s, ov2)):
        moves.store(ref, out)
    reach_cross = jnp.full((1, chip_rows), reach[0], jnp.int32)
    for p in range(pairs):
        attend_pair(p, 256, reach_cross, q2_s, k2_s, v2_s, o2_s, l2_s, score_s, weight_s)
        advance(needed + 2 + p)
    moves.store(o2_s, oo2)
    moves.store(l2_s, ol2)
    swap = give(1, o2_s, c_s.at[3])
    advance(needed + 7)
    swap.wait_recv()

    def third_norm(rows):
        values = x1_s[rows, :] + total(1, rows)
        x2_s[rows, :] = values
        h3_s[rows, :] = norm_rows(values, p_ref, 2)

    loop_rows(chip_rows, strip, third_norm)
    moves.store(x2_s.at[own], ox2)
    moves.store(h3_s, oh3)
    advance(len(queue))
    own_ffn.wait()
    moves.close()
    wires.close()


def forward(length, reach, inputs, frames, weights_self, params, cross_shard, ffn_shard, own_rows):
    n = grid_sizes()
    slot, width = inputs.shape
    mats, _, local = weights_self.shape
    hidden = ffn_shard.shape[2]
    chip_rows = 2 * own_rows
    pairs = local // PAIR
    copies = Gather.copies(n, True, 3, 4) + Gather.copies(n, False, 0, 2) + 2
    vmem = pl.BlockSpec(memory_space=pltpu.VMEM)
    smem = pl.BlockSpec(memory_space=pltpu.SMEM)
    hbm = pl.BlockSpec(memory_space=pl.ANY)
    half = lambda *shape: (shape, BF)
    full = lambda *shape: (shape, F32)
    outs = [
        half(mats, width, local),
        half(2, width, hidden),
        half(slot, width),
        half(chip_rows, local),
        half(slot, local),
        half(slot, local),
        half(chip_rows, local),
        full(pairs, 2, chip_rows),
        full(own_rows, width),
        half(chip_rows, width),
        half(chip_rows, local),
        half(slot, local),
        half(slot, local),
        half(chip_rows, local),
        full(pairs, 2, chip_rows),
        full(own_rows, width),
        half(chip_rows, width),
    ]
    scratch = [
        half(slot, width),
        half(slot, width),
        half(mats, width, local),
        half(mats, width, local),
        half(slot, width),
        half(chip_rows, local),
        half(slot, local),
        half(slot, local),
        half(chip_rows, local),
        full(pairs, 2, chip_rows),
        full(chip_rows, width),
        half(chip_rows, width),
        half(chip_rows, local),
        half(slot, local),
        half(slot, local),
        half(chip_rows, local),
        full(pairs, 2, chip_rows),
        full(chip_rows, width),
        half(chip_rows, width),
        half(2, chip_rows, width),
        half(2, chip_rows, width),
        full(2, slot, chip_rows),
        half(2, slot, chip_rows),
    ]
    return pl.pallas_call(
        functools.partial(forward_kernel, n, own_rows),
        out_shape=[jax.ShapeDtypeStruct(s, t) for s, t in outs],
        in_specs=[smem, smem, hbm, hbm, hbm, vmem, vmem, vmem],
        out_specs=[hbm] * len(outs),
        scratch_shapes=[pltpu.VMEM(s, t) for s, t in scratch]
        + [
            pltpu.SemaphoreType.DMA((copies,)),
            pltpu.SemaphoreType.DMA((copies,)),
            pltpu.SemaphoreType.DMA((24,)),
        ],
        compiler_params=pltpu.CompilerParams(
            collective_id=3, has_side_effects=True, vmem_limit_bytes=56 * 2**20
        ),
        name="forward",
    )(length, reach, inputs, frames, weights_self, params, cross_shard, ffn_shard)


def norm_back_rows(values, grad, gain):
    centered = values - jnp.mean(values, axis=-1, keepdims=True)
    scale = lax.rsqrt(jnp.mean(centered * centered, axis=-1, keepdims=True) + EPSILON)
    normed = centered * scale
    up = grad * gain
    back = scale * (
        up
        - jnp.mean(up, axis=-1, keepdims=True)
        - normed * jnp.mean(up * normed, axis=-1, keepdims=True)
    )
    return back, normed


def row_sum(values):
    return jnp.sum(values, axis=0, keepdims=True)


SPLIT = 2


def ffn_kernel(
    n, length, h_hbm, x_ref, w_hbm, ct_ref, p_ref,
    oy_ref, odx_ref, odc, odw, on_ref,
    h_s, f_s, a_s, d_s, u_s, w_s, keep_s, far_s, give_s, got_s, cross_s, crossed_s, back_s, come_s,
    x3_s, dx3_s, dc_s, dw_s, send_sem, recv_sem, move_sem,
):
    at = grid_place()
    wires = Wires(n, at, send_sem, recv_sem)
    moves = Moves(move_sem)
    nx, c = n["x"], at["c"]
    own, width = x_ref.shape
    part = own // SPLIT
    start_own = pl.multiple_of(c * own, own)
    start_other = pl.multiple_of((1 - c) * own, own)
    get_w = moves.start(w_hbm, w_s)
    get_own = moves.start(h_hbm.at[pl.ds(start_own, own)], h_s.at[pl.ds(0, own)])
    get_other = moves.start(h_hbm.at[pl.ds(start_other, own)], h_s.at[pl.ds(own, own)])
    wires.greet([{"x": s} for s in range(1, nx)] + [{"c": 1}])

    def far_at(t, k, j):
        return 2 * own + (((t - 1) * SPLIT + k) * 2 + j) * part

    def spread(src, dst, k):
        return [
            wires.send(src.at[pl.ds(k * part, part)], dst.at[pl.ds(far_at(t, k, 0), part)], x=t)
            for t in range(1, nx)
        ]

    def onward(dst, t, k):
        return wires.send(
            dst.at[pl.ds(far_at(t, k, 0), part)], dst.at[pl.ds(far_at(t, k, 1), part)], c=1
        )

    def up(rows):
        hidden = dot(h_s[rows, :], w_s[0], 1, 0)
        inner = 0.7978845608028654 * (hidden + 0.044715 * (hidden * hidden * hidden))
        bend = jnp.tanh(inner)
        a_s[rows, :] = (0.5 * hidden * (1.0 + bend)).astype(BF)
        slope = 0.7978845608028654 * (1.0 + 0.134145 * (hidden * hidden))
        d_s[rows, :] = 0.5 * (1.0 + bend) + 0.5 * hidden * (1.0 - bend * bend) * slope
        return dot(a_s[rows, :], w_s[1], 1, 1)

    def down(rows):
        grad = dot(f_s[rows, :], w_s[1], 1, 0)
        u_s[rows, :] = (grad * d_s[rows, :]).astype(BF)
        return dot(u_s[rows, :], w_s[0], 1, 1)

    def other_core(phase, work):
        give_s[phase] = work(slice(own, 2 * own)).astype(BF)
        return wires.send(give_s.at[phase], got_s.at[phase], c=1)

    def far_part(phase, work, t, k):
        sums = work(slice(far_at(t, k, 0), far_at(t, k, 0) + 2 * part))
        far_s[t - 1, k] = sums[:part]
        cross_s[phase, t - 1, k] = sums[part:].astype(BF)
        return wires.send(cross_s.at[phase, t - 1, k], crossed_s.at[phase, t - 1, k], c=1)

    def return_part(phase, t, k, crossing):
        crossing.wait_recv()
        back_s[phase, t - 1, k] = (far_s[t - 1, k] + crossed_s[phase, t - 1, k].astype(F32)).astype(
            BF
        )
        return wires.send(back_s.at[phase, t - 1, k], come_s.at[phase, t - 1, k], x=nx - t)

    def far_phase(phase, work, buffer, arriving):
        homing = {}
        for k in range(SPLIT):
            crossed = []
            for t in range(1, nx):
                arriving[k][t - 1].wait_recv()
                crossed.append(onward(buffer, t, k))
            crossing = []
            for t in range(1, nx):
                crossed[t - 1].wait_recv()
                crossing.append(far_part(phase, work, t, k))
            for t in range(1, nx):
                homing[k, t] = return_part(phase, t, k, crossing[t - 1])
        return homing

    def own_part(phase, k, homing):
        rows = slice(k * part, (k + 1) * part)
        total = keep_s[rows, :] + got_s[phase, rows, :].astype(F32)
        for t in range(1, nx):
            homing[k, t].wait_recv()
            total = total + come_s[phase, t - 1, k].astype(F32)
        return total

    get_own.wait()
    arriving = [spread(h_s, h_s, k) for k in range(SPLIT)]
    get_w.wait()
    get_other.wait()
    swap = other_core(0, up)
    keep_s[...] = up(slice(0, own))
    homing = far_phase(0, up, h_s, arriving)
    swap.wait_recv()
    gain_final, bias_final = 0.0, 0.0
    arriving, near = [], []
    first_row = (at["x"] * 2 + c) * own
    for k in range(SPLIT):
        rows = slice(k * part, (k + 1) * part)
        values = x_ref[rows, :] + own_part(0, k, homing)
        x3 = values
        centered = x3 - jnp.mean(x3, axis=-1, keepdims=True)
        variance = jnp.mean(centered * centered, axis=-1, keepdims=True)
        normed = centered * lax.rsqrt(variance + EPSILON)
        oy_ref[rows, :] = (normed * p_ref[3:4, :] + p_ref[7:8, :]).astype(BF)
        position = lax.broadcasted_iota(jnp.int32, (part, 1), 0) + (first_row + k * part)
        seed = jnp.where(position < length[0], ct_ref[rows, :].astype(F32), 0.0)
        grad, normed = norm_back_rows(x3, seed, p_ref[3:4, :])
        gain_final = gain_final + row_sum(seed * normed)
        bias_final = bias_final + row_sum(seed)
        dx3_s[rows, :] = grad
        f_s[rows, :] = grad.astype(BF)
        arriving.append(spread(f_s, f_s, k))
        near.append(
            wires.send(f_s.at[pl.ds(k * part, part)], f_s.at[pl.ds(own + k * part, part)], c=1)
        )
    keep_s[...] = down(slice(0, own))
    for copy in near:
        copy.wait_recv()
    swap = other_core(1, down)
    homing = far_phase(1, down, f_s, arriving)
    step = min(256, width)
    for i, (left, right) in ((1, (f_s, a_s)), (0, (h_s, u_s))):
        for col in range(0, width, step):
            cols = slice(col, col + step)
            dw_s[i, cols, :] = dot(left[:, cols], right[...], 0, 0).astype(BF)
        moves.store(dw_s.at[i], odw.at[i])
    swap.wait_recv()
    gain_third, bias_third = 0.0, 0.0
    near = []
    for k in range(SPLIT):
        rows = slice(k * part, (k + 1) * part)
        upstream = own_part(1, k, homing)
        grad, normed = norm_back_rows(x_ref[rows, :], upstream, p_ref[2:3, :])
        gain_third = gain_third + row_sum(upstream * normed)
        bias_third = bias_third + row_sum(upstream)
        total = dx3_s[rows, :] + grad
        odx_ref[rows, :] = total
        here = pl.ds(start_own + k * part, part)
        dc_s[here, :] = total.astype(BF)
        near.append(wires.send(dc_s.at[here], dc_s.at[here], c=1))
    line = lax.broadcasted_iota(jnp.int32, on_ref.shape, 0)
    sums = jnp.zeros(on_ref.shape, F32)
    for index, value in ((2, gain_third), (3, gain_final), (6, bias_third), (7, bias_final)):
        sums = sums + jnp.where(line == index, value, 0.0)
    on_ref[...] = sums
    for copy in near:
        copy.wait_recv()
    moves.store(dc_s, odc)
    moves.close()
    wires.close()


def feed_forward(length, normed, resid, maps, cotangent, params):
    n = grid_sizes()
    chip_rows, width = normed.shape
    own = chip_rows // 2
    hidden = maps.shape[2]
    nx = n["x"]
    rows = chip_rows * nx
    part = own // SPLIT
    copies = 2 * (SPLIT * (nx - 1) * 4 + 1) + 2 * SPLIT
    vmem = pl.BlockSpec(memory_space=pltpu.VMEM)
    smem = pl.BlockSpec(memory_space=pltpu.SMEM)
    hbm = pl.BlockSpec(memory_space=pl.ANY)
    far = (2, nx - 1, SPLIT, part, width)
    return pl.pallas_call(
        functools.partial(ffn_kernel, n),
        out_shape=[
            jax.ShapeDtypeStruct((own, width), BF),
            jax.ShapeDtypeStruct((own, width), F32),
            jax.ShapeDtypeStruct((chip_rows, width), BF),
            jax.ShapeDtypeStruct((2, width, hidden), BF),
            jax.ShapeDtypeStruct(params.shape, F32),
        ],
        in_specs=[smem, hbm, vmem, hbm, vmem, vmem],
        out_specs=[vmem, vmem, hbm, hbm, vmem],
        scratch_shapes=[
            pltpu.VMEM((rows, width), BF),
            pltpu.VMEM((rows, width), BF),
            pltpu.VMEM((rows, hidden), BF),
            pltpu.VMEM((rows, hidden), F32),
            pltpu.VMEM((rows, hidden), BF),
            pltpu.VMEM((2, width, hidden), BF),
            pltpu.VMEM((own, width), F32),
            pltpu.VMEM((nx - 1, SPLIT, part, width), F32),
            pltpu.VMEM((2, own, width), BF),
            pltpu.VMEM((2, own, width), BF),
            pltpu.VMEM(far, BF),
            pltpu.VMEM(far, BF),
            pltpu.VMEM(far, BF),
            pltpu.VMEM(far, BF),
            pltpu.VMEM((own, width), F32),
            pltpu.VMEM((own, width), F32),
            pltpu.VMEM((chip_rows, width), BF),
            pltpu.VMEM((2, width, hidden), BF),
            pltpu.SemaphoreType.DMA((copies,)),
            pltpu.SemaphoreType.DMA((copies,)),
            pltpu.SemaphoreType.DMA((8,)),
        ],
        compiler_params=pltpu.CompilerParams(
            collective_id=4, has_side_effects=True, vmem_limit_bytes=56 * 2**20
        ),
        name="feed_forward",
    )(length, normed, resid, maps, cotangent, params)


def zone_order(n):
    return list(range(1, n["z"])) + [0]


def cross_back_kernel(
    n, reach, dc_hbm, dx_ref, w_hbm, q_hbm, k_hbm, v_hbm, o_hbm, l_ref, h_hbm, m_hbm, x_ref, p_ref,
    dw_hbm, of_ref, og, odx_ref, odb, om, on_ref,
    dc_s, w_s, q_s, k_s, v_s, o_s, h_s, m_s, g_s, dq_s, dk_s, dv_s, ds_s, gr_s, give_s, got_s,
    db_s, pm_s, rm_s, sm_s, cm_s, om_s, fown_s, fy_s, fkeep_s, fz_s, fr_s,
    send_sem, recv_sem, move_sem,
):
    at = grid_place()
    z, y, x, c = at["z"], at["y"], at["x"], at["c"]
    nz, ny, nx = n["z"], n["y"], n["x"]
    wires = Wires(n, at, send_sem, recv_sem)
    moves = Moves(move_sem)
    loads = [
        moves.start(a, b)
        for a, b in (
            (dc_hbm, dc_s), (w_hbm, w_s), (q_hbm, q_s), (k_hbm, k_s), (v_hbm, v_s), (o_hbm, o_s)
        )
    ]
    later = [moves.start(h_hbm, h_s), moves.start(m_hbm, m_s)]
    rows = of_ref.shape[1]
    order = zone_order(n)

    def band(s, t):
        index = ((z + s) % nz) * ny + (y + t) % ny
        return pl.ds(pl.multiple_of(index * rows, rows), rows)

    owned = [moves.start(dw_hbm.at[:, band(s, 0)], fown_s.at[s]) for s in range(nz)]
    wires.greet(
        [{"z": s} for s in range(1, nz)]
        + [{"y": s} for s in range(1, ny)]
        + [{"x": s} for s in range(1, nx)]
        + [{"c": 1}]
    )
    by_y = {
        (s, t): wires.send(dw_hbm.at[:, band(s, t)], fy_s.at[t - 1, s], y=t)
        for s in order
        for t in range(1, ny)
    }
    by_z = {}

    def ffn_zone(s):
        owned[s].wait()
        for t in range(1, ny):
            by_y[s, t].wait_recv()
        for i in range(2):
            total = fown_s[s, i].astype(F32)
            for t in range(1, ny):
                total = total + fy_s[t - 1, s, i].astype(F32)
            if s:
                fz_s[s - 1, i] = total.astype(BF)
            else:
                fkeep_s[i] = total
        if s:
            by_z[s] = wires.send(fz_s.at[s - 1], fr_s.at[s - 1], z=s)

    def ffn_finish():
        for s in range(1, nz):
            by_z[s].wait_recv()
        for i in range(2):
            total = fkeep_s[i]
            for s in range(1, nz):
                total = total + fr_s[s - 1, i].astype(F32)
            of_ref[i] = total

    queue = [functools.partial(ffn_zone, s) for s in order] + [ffn_finish]
    done = [0]

    def advance(limit):
        while done[0] < min(limit, len(queue)):
            queue[done[0]]()
            done[0] += 1

    chip_rows, width = dc_s.shape
    slot = m_s.shape[0]
    own = chip_rows // 2
    strip = min(STRIP, own)
    pairs = q_s.shape[1] // PAIR
    mine = pl.ds(pl.multiple_of(c * own, own), own)
    other = pl.ds(pl.multiple_of((1 - c) * own, own), own)
    for copy in loads:
        copy.wait()
    mat_rows(g_s, dc_s, w_s.at[3], chip_rows, strip)
    bound = jnp.full((1, chip_rows), reach[0], jnp.int32)
    for p in range(pairs):
        attend_pair_back(
            p, 256, bound, q_s, k_s, v_s, o_s, l_ref, g_s, dq_s, dk_s, dv_s, ds_s
        )
        advance(p)

    def input_part(rows_):
        give_s[rows_, :] = dot(dq_s[rows_, :], w_s[0], 1, 1).astype(BF)

    loop_rows(chip_rows, strip, input_part)
    swap = wires.send(give_s.at[other], got_s, c=1)
    deep = om_s.shape[1]
    piece = min(512, width)

    def memory_part(rows_):
        for col in range(0, width, piece):
            some = slice(col, col + piece)
            sums = dot(dk_s[rows_, :], w_s[1, some, :], 1, 1)
            sums = (sums + dot(dv_s[rows_, :], w_s[2, some, :], 1, 1)).astype(BF)
            for b in range(piece // deep):
                index = col // deep + b
                pm_s[index // 2, index % 2, rows_, :] = sums[:, b * deep : (b + 1) * deep]

    loop_rows(slot, strip, memory_part)
    to_c = wires.send(pm_s.at[:, 1 - c], rm_s, c=1)
    swap.wait_recv()
    upstream = give_s[mine, :].astype(F32) + got_s[...].astype(F32)
    grad, normed = norm_back_rows(x_ref[...], upstream, p_ref[1:2, :])
    total = dx_ref[...] + grad
    odx_ref[...] = total
    db_s[mine, :] = total.astype(BF)
    near = wires.send(db_s.at[mine], db_s.at[mine], c=1)
    line = lax.broadcasted_iota(jnp.int32, on_ref.shape, 0)
    on_ref[...] = jnp.where(line == 1, row_sum(upstream * normed), 0.0) + jnp.where(
        line == 5, row_sum(upstream), 0.0
    )
    to_c.wait_recv()
    to_x = []
    for t in range(1, nx):
        index = (x + t) % nx
        sm_s[t - 1] = (pm_s[index, c].astype(F32) + rm_s[index].astype(F32)).astype(BF)
        to_x.append(wires.send(sm_s.at[t - 1], cm_s.at[t - 1], x=t))
    advance(pairs)
    for copy in later:
        copy.wait()
    step = min(256, width)
    for i, (left, right) in enumerate(((h_s, dq_s), (m_s, dk_s), (m_s, dv_s), (dc_s, o_s))):
        for col in range(0, width, step):
            cols = slice(col, col + step)
            gr_s[i, cols, :] = dot(left[:, cols], right[...], 0, 0).astype(BF)
        moves.store(gr_s.at[i], og.at[i])
    total = pm_s[x, c].astype(F32) + rm_s[x].astype(F32)
    for t in range(1, nx):
        to_x[t - 1].wait_recv()
        total = total + cm_s[t - 1].astype(F32)
    om_s[...] = total.astype(BF)
    moves.store(om_s, om)
    near.wait_recv()
    moves.store(db_s, odb)
    advance(len(queue))
    moves.close()
    wires.close()


def cross_back(reach, rows_grad, resid_grad, maps, saved, normed, frames, resid, params, ffn_grads):
    n = grid_sizes()
    nz, ny, nx = n["z"], n["y"], n["x"]
    queries, keys, values, mixed, logsum = saved
    chip_rows, width = rows_grad.shape
    own = chip_rows // 2
    slot, local = keys.shape
    hidden = ffn_grads.shape[2]
    rows = width // (nz * ny)
    deep = width // (2 * nx)
    copies = nz * (ny - 1) + (nz - 1) + 3 + (nx - 1)
    vmem = pl.BlockSpec(memory_space=pltpu.VMEM)
    smem = pl.BlockSpec(memory_space=pltpu.SMEM)
    hbm = pl.BlockSpec(memory_space=pl.ANY)
    half = lambda *shape: pltpu.VMEM(shape, BF)
    return pl.pallas_call(
        functools.partial(cross_back_kernel, n),
        out_shape=[
            jax.ShapeDtypeStruct((2, rows, hidden), F32),
            jax.ShapeDtypeStruct((4, width, local), BF),
            jax.ShapeDtypeStruct((own, width), F32),
            jax.ShapeDtypeStruct((chip_rows, width), BF),
            jax.ShapeDtypeStruct((slot, deep), BF),
            jax.ShapeDtypeStruct(params.shape, F32),
        ],
        in_specs=[smem, hbm, vmem, hbm, hbm, hbm, hbm, hbm, vmem, hbm, hbm, vmem, vmem, hbm],
        out_specs=[vmem, hbm, vmem, hbm, hbm, vmem],
        scratch_shapes=[
            half(chip_rows, width),
            half(4, width, local),
            half(chip_rows, local),
            half(slot, local),
            half(slot, local),
            half(chip_rows, local),
            half(chip_rows, width),
            half(slot, width),
            half(chip_rows, local),
            half(chip_rows, local),
            half(slot, local),
            half(slot, local),
            half(2, slot, chip_rows),
            half(4, width, local),
            half(chip_rows, width),
            half(own, width),
            half(chip_rows, width),
            half(nx, 2, slot, deep),
            half(nx, slot, deep),
            half(nx - 1, slot, deep),
            half(nx - 1, slot, deep),
            half(slot, deep),
            half(nz, 2, rows, hidden),
            half(ny - 1, nz, 2, rows, hidden),
            pltpu.VMEM((2, rows, hidden), F32),
            half(nz - 1, 2, rows, hidden),
            half(nz - 1, 2, rows, hidden),
            pltpu.SemaphoreType.DMA((copies,)),
            pltpu.SemaphoreType.DMA((copies,)),
            pltpu.SemaphoreType.DMA((16 + nz,)),
        ],
        compiler_params=pltpu.CompilerParams(
            collective_id=5, has_side_effects=True, vmem_limit_bytes=56 * 2**20
        ),
        name="cross_back",
    )(
        reach, rows_grad, resid_grad, maps, queries, keys, values, mixed, logsum, normed, frames,
        resid, params, ffn_grads,
    )


class Scatter:
    def __init__(self, wires, grads, ra1, rb1, sa2, sb2, ra2, rb2, acc, s3, r3):
        self.wires, self.grads = wires, grads
        self.n, self.at = wires.sizes, wires.place
        self.ra1, self.rb1, self.sa2, self.sb2 = ra1, rb1, sa2, sb2
        self.ra2, self.rb2, self.acc, self.s3, self.r3 = ra2, rb2, acc, s3, r3
        self.rows, self.wide = acc.shape[2], acc.shape[3]
        self.by_x, self.by_y, self.next_x, self.next_y, self.to_z = {}, {}, {}, {}, {}

    @staticmethod
    def copies(n):
        nz, ny, nx = n["z"], n["y"], n["x"]
        return nz * 2 * (nx - 1 + ny - 1) + nz * (ny - 1 + nx - 1) + nz - 1

    @staticmethod
    def scratch(n, rows, wide):
        nz, ny, nx = n["z"], n["y"], n["x"]
        return [
            pltpu.VMEM((nx - 1, nz, 2, ny * rows, wide), BF),
            pltpu.VMEM((ny - 1, nz, 2, rows, nx * wide), BF),
            pltpu.VMEM((ny - 1, nz, 2, rows, wide), BF),
            pltpu.VMEM((nx - 1, nz, 2, rows, wide), BF),
            pltpu.VMEM((ny - 1, nz, 2, rows, wide), BF),
            pltpu.VMEM((nx - 1, nz, 2, rows, wide), BF),
            pltpu.VMEM((nz, 4, rows, wide), F32),
            pltpu.VMEM((nz - 1, 4, rows, wide), BF),
            pltpu.VMEM((nz - 1, 4, rows, wide), BF),
        ]

    def bands(self, i, band, count, col):
        rows, wide = self.rows, self.wide
        return self.grads.at[
            i,
            pl.ds(pl.multiple_of(band * rows, rows), count * rows),
            pl.ds(pl.multiple_of(col * wide, wide), wide),
        ]

    def zone(self, s):
        return ((self.at["z"] + s) % self.n["z"]) * self.n["y"]

    def begin(self, mats=(0, 1, 2, 3)):
        nx, ny, rows = self.n["x"], self.n["y"], self.rows
        for s in zone_order(self.n):
            zone = self.zone(s)
            for i in mats:
                if i < 2:
                    for t in range(1, nx):
                        src = self.bands(i, zone, ny, (self.at["x"] + t) % nx)
                        self.by_x[s, t, i] = self.wires.send(src, self.ra1.at[t - 1, s, i], x=t)
                else:
                    for t in range(1, ny):
                        band = zone + (self.at["y"] + t) % ny
                        src = self.grads.at[i, pl.ds(pl.multiple_of(band * rows, rows), rows)]
                        self.by_y[s, t, i] = self.wires.send(src, self.rb1.at[t - 1, s, i - 2], y=t)

    def middle(self, s):
        nx, ny, rows, wide = self.n["x"], self.n["y"], self.rows, self.wide
        x, y = self.at["x"], self.at["y"]
        zone = self.zone(s)
        for i in range(2):
            for t in range(1, nx):
                self.by_x[s, t, i].wait_recv()
            for b in range(ny):
                band = (y + b) % ny
                total = self.bands(i, zone + band, 1, x)[...].astype(F32)
                for t in range(1, nx):
                    lines = pl.ds(pl.multiple_of(band * rows, rows), rows)
                    total = total + self.ra1[t - 1, s, i, lines, :].astype(F32)
                if b == 0:
                    self.acc[s, i] = total
                else:
                    self.sa2[b - 1, s, i] = total.astype(BF)
        for t in range(1, ny):
            self.next_y[s, t] = self.wires.send(self.sa2.at[t - 1, s], self.ra2.at[t - 1, s], y=t)
        for i in range(2, 4):
            for t in range(1, ny):
                self.by_y[s, t, i].wait_recv()
            for b in range(nx):
                column = (x + b) % nx
                total = self.bands(i, zone + y, 1, column)[...].astype(F32)
                for t in range(1, ny):
                    lanes = pl.ds(pl.multiple_of(column * wide, wide), wide)
                    total = total + self.rb1[t - 1, s, i - 2, :, lanes].astype(F32)
                if b == 0:
                    self.acc[s, i] = total
                else:
                    self.sb2[b - 1, s, i - 2] = total.astype(BF)
        for t in range(1, nx):
            self.next_x[s, t] = self.wires.send(self.sb2.at[t - 1, s], self.rb2.at[t - 1, s], x=t)

    def along_z(self, s):
        nx, ny = self.n["x"], self.n["y"]
        for t in range(1, ny):
            self.next_y[s, t].wait_recv()
        for t in range(1, nx):
            self.next_x[s, t].wait_recv()
        for i in range(4):
            total = self.acc[s, i]
            if i < 2:
                for t in range(1, ny):
                    total = total + self.ra2[t - 1, s, i].astype(F32)
            else:
                for t in range(1, nx):
                    total = total + self.rb2[t - 1, s, i - 2].astype(F32)
            if s:
                self.s3[s - 1, i] = total.astype(BF)
            else:
                self.acc[s, i] = total
        if s:
            self.to_z[s] = self.wires.send(self.s3.at[s - 1], self.r3.at[s - 1], z=s)

    def finish(self, out):
        nz = self.n["z"]
        for s in range(1, nz):
            self.to_z[s].wait_recv()
        for i in range(4):
            total = self.acc[0, i]
            for s in range(1, nz):
                total = total + self.r3[s - 1, i].astype(F32)
            out[i] = total


def self_back_kernel(
    n, length, db_hbm, dx_ref, w_hbm, q_hbm, k_hbm, v_hbm, o_hbm, l_ref, h_hbm, x_ref, p_ref,
    cg_hbm, m_hbm, np_ref, oc_ref, og_ref, os_ref, om_ref, on_ref, *scratch,
):
    (
        db_s, w_s, q_s, k_s, v_s, o_s, h_s, g_s, dq_s, dk_s, dv_s, ds_s, cg_s, gr_s, part_s, rc_s,
        sx_s, rx_s, out_s, np_s, nn_s, nf_s,
    ) = scratch[:22]
    send_sem, recv_sem, go_sem, come_sem, move_sem = scratch[-5:]
    at = grid_place()
    z, y, x, c = at["z"], at["y"], at["x"], at["c"]
    nz, ny, nx = n["z"], n["y"], n["x"]
    data, model = z * ny + y, x * 2 + c
    wires = Wires(n, at, send_sem, recv_sem)
    moves = Moves(move_sem)
    get_cross = moves.start(cg_hbm, cg_s)
    loads = [
        moves.start(a, b)
        for a, b in (
            (db_hbm, db_s), (w_hbm, w_s), (q_hbm, q_s), (k_hbm, k_s), (v_hbm, v_s), (o_hbm, o_s),
            (h_hbm, h_s),
        )
    ]
    wires.greet(
        [
            dict(z=sz, y=sy, x=sx, c=sc)
            for sz in range(nz)
            for sy in range(ny)
            for sx in range(nx)
            for sc in range(2)
            if sz or sy or sx or sc
        ]
    )
    cross = Scatter(wires, cg_s, *scratch[22:31])
    own_sum = Scatter(wires, gr_s, *scratch[31:40])
    get_cross.wait()
    cross.begin()
    order = zone_order(n)
    queue = [functools.partial(cross.middle, s) for s in order]
    queue += [functools.partial(cross.along_z, s) for s in order]
    done = [0]

    def advance(limit):
        while done[0] < min(limit, len(queue)):
            queue[done[0]]()
            done[0] += 1

    spread = []
    for i, shift in enumerate(dp_shifts(n)):
        target = wires.peer(**shift)[0]
        spread.append(wires.send(m_hbm.at[target], om_ref.at[data], **shift))
    keep = moves.start(m_hbm.at[data], om_ref.at[data])

    chip_rows, width = db_s.shape
    slot = h_s.shape[0]
    own = chip_rows // 2
    strip = min(STRIP, own)
    pairs = q_s.shape[1] // PAIR
    chip_start = x * chip_rows
    for copy in loads:
        copy.wait()
    mat_rows(g_s, db_s, w_s.at[3], chip_rows, strip)
    bound = lax.broadcasted_iota(jnp.int32, (1, chip_rows), 1) + chip_start + 1
    bound = jnp.minimum(bound, length[0])
    for p in range(pairs):
        attend_pair_back(
            p, 256, bound, q_s, k_s, v_s, o_s, l_ref, g_s, dq_s, dk_s, dv_s, ds_s
        )
        advance(p + 1)

    def input_part(rows_):
        sums = dot(dk_s[rows_, :], w_s[1], 1, 1) + dot(dv_s[rows_, :], w_s[2], 1, 1)
        part_s[rows_, :] = sums.astype(BF)

    loop_rows(slot, strip, input_part)

    def query_part(rows_):
        here = shifted(rows_, chip_start)
        sums = part_s[here, :].astype(F32) + dot(dq_s[rows_, :], w_s[0], 1, 1)
        part_s[here, :] = sums.astype(BF)

    loop_rows(chip_rows, strip, query_part)

    def block(chip, core):
        return pl.ds(pl.multiple_of((chip * 2 + core) * own, own), own)

    to_c = [
        wires.send(part_s.at[block(b, 1 - c)], rc_s.at[b], c=1) for b in range(nx)
    ]
    step = min(256, width)

    def weight_grad(i, left, right):
        for col in range(0, width, step):
            cols = slice(col, col + step)
            gr_s[i, cols, :] = dot(left[:, cols], right[...], 0, 0).astype(BF)
        own_sum.begin((i,))

    chip_lines = pl.ds(pl.multiple_of(chip_start, chip_rows), chip_rows)
    weight_grad(1, h_s, dk_s)
    for copy in to_c:
        copy.wait_recv()
    to_x = []
    for t in range(1, nx):
        index = (x + t) % nx
        sums = part_s[block(index, c), :].astype(F32) + rc_s[index].astype(F32)
        sx_s[t - 1] = sums.astype(BF)
        to_x.append(wires.send(sx_s.at[t - 1], rx_s.at[t - 1], x=t))
    weight_grad(2, h_s, dv_s)
    weight_grad(3, db_s, o_s)
    weight_grad(0, h_s.at[chip_lines], dq_s)
    advance(2 * nz)

    upstream = part_s[block(x, c), :].astype(F32) + rc_s[x].astype(F32)
    for t in range(1, nx):
        to_x[t - 1].wait_recv()
        upstream = upstream + rx_s[t - 1].astype(F32)
    grad, normed = norm_back_rows(x_ref[...].astype(F32), upstream, p_ref[0:1, :])
    out_s[...] = (dx_ref[...] + grad).astype(BF)
    lines, deep = os_ref.shape[1], os_ref.shape[2]
    blocks = own // lines

    def homeward():
        for b in range(blocks):
            for m in range(2 * nx):
                target = (model * blocks + b, m)
                src = out_s.at[b * lines : (b + 1) * lines, m * deep : (m + 1) * deep]
                mine = jnp.logical_and(target[0] == data, model == m)
                remote = pltpu.make_async_remote_copy(
                    src_ref=src,
                    dst_ref=os_ref.at[data],
                    send_sem=go_sem.at[b * 2 * nx + m],
                    recv_sem=come_sem.at[data],
                    device_id=target,
                    device_id_type=pl.DeviceIdType.MESH,
                )
                yield mine, remote, pltpu.make_async_copy(src, os_ref.at[data], come_sem.at[data])

    for mine, remote, here in homeward():
        pl.when(mine)(lambda: here.start())
        pl.when(jnp.logical_not(mine))(lambda: remote.start())

    line = lax.broadcasted_iota(jnp.int32, np_ref.shape, 0)
    params = (
        np_ref[...]
        + jnp.where(line == 0, row_sum(upstream * normed), 0.0)
        + jnp.where(line == 4, row_sum(upstream), 0.0)
    )
    columns = on_ref.shape[1]
    for k in range(nz * ny):
        np_s[0, k] = params[:, k * columns : (k + 1) * columns]
    norm_near = [wires.send(np_s.at[0], nn_s.at[i], **s) for i, s in enumerate(mp_shifts(n))]

    for s in order:
        own_sum.middle(s)
    total = np_s[0]
    for i, copy in enumerate(norm_near):
        copy.wait_recv()
        total = total + nn_s[i]
    np_s[1] = total
    norm_far = []
    for i, shift in enumerate(dp_shifts(n)):
        target = wires.peer(**shift)[0]
        norm_far.append(wires.send(np_s.at[1, target], nf_s.at[i], **shift))
    for s in order:
        own_sum.along_z(s)
    cross.finish(oc_ref)
    total = np_s[1, data]
    for i, copy in enumerate(norm_far):
        copy.wait_recv()
        total = total + nf_s[i]
    on_ref[...] = total
    own_sum.finish(og_ref)
    for copy in spread:
        copy.wait_recv()
    keep.wait()
    for mine, remote, here in homeward():
        pl.when(jnp.logical_not(mine))(lambda: remote.wait_send())
    for r in range(nz * ny):
        pltpu.make_async_copy(os_ref.at[r], os_ref.at[r], come_sem.at[r]).wait()
    wires.close()


def self_back(
    length, rows_grad, resid_grad, maps, saved, normed, inputs, params, cross_grads, memory, norm_part
):
    n = grid_sizes()
    nz, ny, nx = n["z"], n["y"], n["x"]
    data, model = nz * ny, 2 * nx
    queries, keys, values, mixed, logsum = saved
    chip_rows, width = rows_grad.shape
    own = chip_rows // 2
    slot, local = keys.shape
    rows, wide = width // data, local // nx
    utterances, lines, deep = memory.shape
    columns = width // data
    copies = 2 * Scatter.copies(n) + 2 * (data - 1) + nx + (nx - 1) + (model - 1)
    vmem = pl.BlockSpec(memory_space=pltpu.VMEM)
    smem = pl.BlockSpec(memory_space=pltpu.SMEM)
    hbm = pl.BlockSpec(memory_space=pl.ANY)
    half = lambda *shape: pltpu.VMEM(shape, BF)
    return pl.pallas_call(
        functools.partial(self_back_kernel, n),
        out_shape=[
            jax.ShapeDtypeStruct((4, rows, wide), F32),
            jax.ShapeDtypeStruct((4, rows, wide), F32),
            jax.ShapeDtypeStruct((data, lines, deep), BF),
            jax.ShapeDtypeStruct((data, lines, deep), BF),
            jax.ShapeDtypeStruct((params.shape[0], columns), F32),
        ],
        in_specs=[smem, hbm, vmem] + [hbm] * 5 + [vmem, hbm, vmem, vmem, hbm, hbm, vmem],
        out_specs=[vmem, vmem, hbm, hbm, vmem],
        scratch_shapes=[
            half(chip_rows, width),
            half(4, width, local),
            half(chip_rows, local),
            half(slot, local),
            half(slot, local),
            half(chip_rows, local),
            half(slot, width),
            half(chip_rows, local),
            half(chip_rows, local),
            half(slot, local),
            half(slot, local),
            half(2, slot, chip_rows),
            half(4, width, local),
            half(4, width, local),
            half(slot, width),
            half(nx, own, width),
            half(nx - 1, own, width),
            half(nx - 1, own, width),
            half(own, width),
            pltpu.VMEM((2, data, params.shape[0], columns), F32),
            pltpu.VMEM((model - 1, data, params.shape[0], columns), F32),
            pltpu.VMEM((data - 1, params.shape[0], columns), F32),
        ]
        + Scatter.scratch(n, rows, wide)
        + Scatter.scratch(n, rows, wide)
        + [
            pltpu.SemaphoreType.DMA((copies,)),
            pltpu.SemaphoreType.DMA((copies,)),
            pltpu.SemaphoreType.DMA((data,)),
            pltpu.SemaphoreType.DMA((data,)),
            pltpu.SemaphoreType.DMA((12,)),
        ],
        compiler_params=pltpu.CompilerParams(
            collective_id=1, has_side_effects=True, vmem_limit_bytes=58 * 2**20
        ),
        name="self_back",
    )(
        length, rows_grad, resid_grad, maps, queries, keys, values, mixed, logsum, normed, inputs,
        params, cross_grads, memory, norm_part,
    )


def square_sum_kernel(n, g_ref, o_ref, near_ref, sum_ref, far_ref, send_sem, recv_sem):
    wires = Wires(n, grid_place(), send_sem, recv_sem)
    wires.greet(dp_shifts(n) + mp_shifts(n))
    copies = [wires.send(g_ref, near_ref.at[i], **shift) for i, shift in enumerate(mp_shifts(n))]
    total = g_ref[...]
    for i, copy in enumerate(copies):
        copy.wait_recv()
        total = total + near_ref[i]
    sum_ref[...] = total
    copies = [wires.send(sum_ref, far_ref.at[i], **shift) for i, shift in enumerate(dp_shifts(n))]
    for i, copy in enumerate(copies):
        copy.wait_recv()
        total = total + far_ref[i]
    o_ref[...] = total
    wires.close()


def square_sum(partial):
    n = grid_sizes()
    data = n["z"] * n["y"]
    model = 2 * n["x"]
    vmem = pl.BlockSpec(memory_space=pltpu.VMEM)
    copies = data - 1 + model - 1
    return pl.pallas_call(
        functools.partial(square_sum_kernel, n),
        out_shape=jax.ShapeDtypeStruct(partial.shape, F32),
        in_specs=[vmem],
        out_specs=vmem,
        scratch_shapes=[
            pltpu.VMEM((model - 1,) + partial.shape, F32),
            pltpu.VMEM(partial.shape, F32),
            pltpu.VMEM((data - 1,) + partial.shape, F32),
            pltpu.SemaphoreType.DMA((copies,)),
            pltpu.SemaphoreType.DMA((copies,)),
        ],
        compiler_params=pltpu.CompilerParams(collective_id=2, has_side_effects=True),
        name="square_sum",
    )(partial)


def adam_step(weight, moment, square, gradient, step_rate, weight_decay):
    moment_new = BETA_FIRST * moment + (1.0 - BETA_FIRST) * gradient
    square_new = BETA_SECOND * square + (1.0 - BETA_SECOND) * gradient * gradient
    moment_hat = moment_new / (1.0 - BETA_FIRST**STEP)
    square_hat = square_new / (1.0 - BETA_SECOND**STEP)
    updated = weight - step_rate * (
        moment_hat / (jnp.sqrt(square_hat) + ADAM_EPSILON) + weight_decay * weight
    )
    return (updated, moment_new, square_new)


def per_device(
    states,
    memory,
    cotangent,
    lengths,
    memory_lengths,
    regroup_order,
    attn_weights,
    ffn_weights,
    norm_params,
    attn_mean,
    ffn_mean,
    norm_mean,
    attn_square,
    ffn_square,
    norm_square,
    attn_average,
    ffn_average,
    norm_average,
):
    n = grid_sizes()
    at = grid_place()
    nz, ny, nx = n["z"], n["y"], n["x"]
    data_index = lax.axis_index("dp")
    model_index = lax.axis_index("mp")
    data_size = lax.axis_size("dp")
    width = states.shape[2] * lax.axis_size("mp")
    slot = states.shape[1] * data_size
    own_rows = cotangent.shape[1]
    chip_rows = 2 * own_rows
    chip_start = at["x"] * chip_rows

    attn_low = attn_weights.astype(BF)
    ffn_low = ffn_weights.astype(BF)

    weights_self, norm_values, inputs, frames = entry(
        attn_low[0:4],
        norm_params.astype(BF).astype(F32),
        jnp.take(states, regroup_order, axis=0),
        jnp.take(memory, regroup_order, axis=0),
    )
    norm_values = jnp.swapaxes(norm_values, 0, 1).reshape(norm_params.shape[0], width)
    length = lengths[regroup_order[data_index]]
    reach = memory_lengths[regroup_order[data_index]]

    (
        weights_cross,
        ffn_maps,
        normed_first,
        query_self,
        key_self,
        value_self,
        mixed_self,
        logsum_self,
        resid_one_own,
        normed_second,
        query_cross,
        key_cross,
        value_cross,
        mixed_cross,
        logsum_cross,
        resid_two_own,
        normed_third,
    ) = forward(
        length[None],
        reach[None],
        inputs,
        frames,
        weights_self,
        norm_values,
        attn_low[4:8],
        ffn_low,
        own_rows,
    )
    layer_output, grad_two, cross_rows, ffn_grads, norm_ffn = feed_forward(
        length[None], normed_third, resid_two_own, ffn_maps, cotangent[0], norm_values
    )
    ffn_shard, cross_grads, grad_one, self_rows, memory_part, norm_cross = cross_back(
        reach[None],
        cross_rows,
        grad_two,
        weights_cross,
        (query_cross, key_cross, value_cross, mixed_cross, logsum_cross),
        normed_second,
        frames,
        resid_one_own,
        norm_values,
        ffn_grads,
    )
    shard_cross, shard_self, back_states, back_memory, norm_shard = self_back(
        length[None],
        self_rows,
        grad_one,
        weights_self,
        (query_self, key_self, value_self, mixed_self, logsum_self),
        normed_first,
        lax.dynamic_slice_in_dim(inputs, model_index * own_rows, own_rows, 0),
        norm_values,
        cross_grads,
        memory_part.reshape(data_size, -1, memory_part.shape[1]),
        norm_ffn + norm_cross,
    )
    attn_shard = jnp.concatenate([shard_self, shard_cross], axis=0)

    inverse = jnp.argsort(regroup_order)
    states_grad = jnp.take(back_states, inverse, axis=0).astype(F32)
    memory_grad = jnp.take(back_memory, inverse, axis=0).astype(F32)
    def squares(value):
        return jnp.sum((value * value).reshape(-1, 8, 128), axis=0)

    norm_squares = jnp.sum(norm_shard * norm_shard) / lax.axis_size("mp")
    local_squares = squares(attn_shard) + squares(ffn_shard) + norm_squares / 1024.0
    grad_norm = jnp.sqrt(jnp.sum(square_sum(local_squares)))
    clip_scale = jnp.minimum(1.0, THRESHOLD / (grad_norm + 1e-06))
    attn_updated, mean_attn, square_attn = adam_step(
        attn_weights, attn_mean, attn_square, clip_scale * attn_shard, MATRIX_RATE, MATRIX_DECAY
    )
    ffn_updated, mean_ffn, square_ffn = adam_step(
        ffn_weights, ffn_mean, ffn_square, clip_scale * ffn_shard, MATRIX_RATE, MATRIX_DECAY
    )
    norm_updated, mean_norm, square_norm = adam_step(
        norm_params, norm_mean, norm_square, clip_scale * norm_shard, NORM_RATE, 0.0
    )
    average_attn = AVERAGING * attn_average + (1.0 - AVERAGING) * attn_updated
    average_ffn = AVERAGING * ffn_average + (1.0 - AVERAGING) * ffn_updated
    average_norm = AVERAGING * norm_average + (1.0 - AVERAGING) * norm_updated
    return (
        layer_output[None],
        states_grad,
        memory_grad,
        attn_updated,
        ffn_updated,
        norm_updated,
        mean_attn,
        mean_ffn,
        mean_norm,
        square_attn,
        square_ffn,
        square_norm,
        average_attn,
        average_ffn,
        average_norm,
        grad_norm,
    )


def solution(mesh):
    rows = P(None, "dp", "mp")
    line = P(None, "dp")
    return jax.shard_map(
        per_device,
        mesh=mesh,
        in_specs=(rows, rows, P("dp", "mp", None), P(), P(), P())
        + (rows, rows, line) * 4,
        out_specs=(P("dp", "mp", None), rows, rows) + (rows, rows, line) * 4 + (P(),),
        check_vma=False,
    )
```

time: 717 us -> 488 us (0.68)
  Pallas kernels: 229 us -> 430 us
  waiting for transfers between devices: 200 us -> 0 us
  matrix products: 79.4 us -> 0 us
  local copies, waits for them, and re-layouts: 96.8 us -> 19.4 us
  other arithmetic: 69.3 us -> 23 us
  starting transfers between devices: 29.2 us -> 0 us
    ppermute x41 -> x0, waiting for transfers between devices: 200 us -> none  [hop(): return lax.ppermute(value, ('dp', 'mp'), pairs)]
    pallas_call x7 -> x4, Pallas kernels: 141 us -> 340 us  [the longest x1 115 us: self_back(): pl.pallas_call(functools.partial(self_back_kernel, n), out_shape=[jax.Sha...]
    dot_general x44 -> x0, matrix products: 79.4 us -> none  [dot(): lax.dot_general(left, right, (((left_dim,), (right_dim,)), ((), ())), pre...]
    unnamed x215 -> x46, local copies, waits for them, and re-layouts: 36.9 us -> 5.35 us
    ppermute x41 -> x0, starting transfers between devices: 29.2 us -> none  [hop(): return lax.ppermute(value, ('dp', 'mp'), pairs)]
    dynamic_slice x11 -> x1, local copies, waits for them, and re-layouts: 25.1 us -> 0.93 us  [per_device(): lax.dynamic_slice_in_dim(inputs, model_index * own_rows, own_rows, 0)]
    reduce_sum x17 -> x0, other arithmetic: 15.2 us -> none  [the longest x9 9.58 us: layer_norm(): centered = values - jnp.mean(values, axis=-1, keepdims=True)]
    concatenate x8 -> x1, local copies, waits for them, and re-layouts: 14.1 us -> 0.04 us  [per_device(): attn_shard = jnp.concatenate([shard_self, shard_cross], axis=0)]
  transfers between devices with their start and end apart: 41 -> 0, of which waited for: 15 -> 0; matrix products, arithmetic and copies ran while one was open for 26% -> 0% of each run, Pallas kernels for 18% -> 0%
where the time goes in v2:
time: 488 us; the launch traced here: 478 us
  Pallas kernels  430 us (88%)
  other arithmetic  23 us (5%)
  local copies, waits for them, and re-layouts  19.4 us (4%)
  between operations  5.61 us (1%)
    pallas_call x1, Pallas kernels, self_back(): pl.pallas_call(functools.partial(self_back_kernel, n), out_shape=[jax.Sha...  115 us
    pallas_call x1, Pallas kernels, forward(): pl.pallas_call(functools.partial(forward_kernel, n, own_rows), out_shape=...  104 us
    pallas_call x1, Pallas kernels, entry(): pl.pallas_call(functools.partial(entry_kernel, n), out_shape=[jax.ShapeDt...  76.8 us
    pallas_call x1, Pallas kernels, cross_back(): pl.pallas_call(functools.partial(cross_back_kernel, n), out_shape=[jax.Sh...  67.1 us
    pallas_call x1, Pallas kernels, feed_forward(): pl.pallas_call(functools.partial(ffn_kernel, n), out_shape=[jax.ShapeDtyp...  55 us
    pallas_call x1, Pallas kernels, square_sum(): pl.pallas_call(functools.partial(square_sum_kernel, n), out_shape=jax.Sha...  13.1 us

profile of v2, /device:TPU:0, one launch (start us, length us, event | category | flops | bytes accessed | tf_op | source)
XLA Modules:
  0.0 478.3 jit_solution(11187498981021567448)
XLA Ops:
  0.6 0.0 copy-start
  0.7 0.0 copy-start.6
  0.7 0.0 copy-start.7
  0.7 1.4 dynamic_slice.13
  4.0 1.2 dynamic_slice.15.reach
  5.3 1.2 dynamic_slice.14.length
  6.5 0.7 compare_and_fusion.1
  7.2 0.7 compare_select_fusion.1
  7.8 1.6 sort.17
  9.5 0.7 convert_convert_fusion.p_ref
  10.2 0.6 gather_fusion.1
  10.7 2.4 gather_fusion
  13.2 1.2 broadcast_select_fusion
  14.4 0.1 convert_element_type.18
  14.4 0.7 fusion.7
  15.2 0.9 convert_element_type.21.wf_ref
  16.0 76.8 %entry.1 = (bf16[4,1024,512]{2,1,0:T(8,128)(2,1)S(1)}, f32[8,8,128]{2,1,0:T(8,128)S(1)}, bf16[1024,1024]{1,0:T(8,128)(2,1)S(1)}, bf16[1024,1024]{1,0:T(8,128)(2,1)S(1)}) custom-call(bf16[4,128,256]{2,1,0:T(8,128)(2,1)S(1)} %get-tuple-element.106.w_ref, f32[8,128]{1,0:T(8,128)S(1)} %convert_convert_fusion.p_ref, ...), custom_call_target="tpu_custom_call" | custom-call | tf_op jit(solution)/shard_map/entry/pallas_call | solution.py:286
  92.8 1.9 copy-done.2
  94.8 1.3 copy-done.3
  96.1 0.6 copy-done.5
  96.7 0.9 constant_dynamic-slice_fusion.x_ref
  97.6 0.6 copy-done.4
  98.2 103.5 %forward.1 = (bf16[4,1024,512]{2,1,0:T(8,128)(2,1)}, bf16[2,1024,1024]{2,1,0:T(8,128)(2,1)}, bf16[1024,1024]{1,0:T(8,128)(2,1)}, bf16[512,512]{1,0:T(8,128)(2,1)...) custom-call(s32[1]{0:T(128)} %dynamic_slice.14.length, ...), custom_call_target="tpu_custom_call" | custom-call | tf_op jit(solution)/shard_map/forward/pallas_call | solution.py:618
  201.7 55.0 %feed_forward.1 = (bf16[256,1024]{1,0:T(8,128)(2,1)}, f32[256,1024]{1,0:T(8,128)}, bf16[512,1024]{1,0:T(8,128)(2,1)}, bf16[2,1024,1024]{2,1,0:T(8,128)(2,1)}, f32[8,1024]{1,0:T(8,128)}) custom-call(s32[1]{0:T(128)} %dynamic_slice.14.length, bf16[512,1024]{1,0:T(8,128)(2,1)} %get-tuple-element.59.h_hbm, f32[256,1024]{1,0:T(8,128)} %get-tuple-element.60.x_ref, ...), custom_call_target="tpu_custom_call" | custom-call | tf_op jit(solution)/shard_map/feed_forward/pallas_call | solution.py:823
  256.7 0.0 copy-start.16
  256.7 67.1 %cross_back.1 = (f32[2,128,1024]{2,1,0:T(8,128)}, bf16[4,1024,512]{2,1,0:T(8,128)(2,1)}, f32[256,1024]{1,0:T(8,128)}, bf16[512,1024]{1,0:T(8,128)(2,1)}, bf16[1024,256]{1,0:T(8,128)(2,1)}, /*index=5*/f32[8,1024]{1,0:T(8,128)}) custom-call(s32[1]{0:T(128)} %dynamic_slice.15.reach, bf16[512,1024]{1,0:T(8,128)(2,1)} %get-tuple-element.63.dc_hbm, ...), custom_call_target="tpu_custom_call" | custom-call | tf_op jit(solution)/shard_map/cross_back/pallas_call | solution.py:1030
  323.9 1.4 add.86.np_ref
  325.2 114.8 %self_back.1 = (f32[4,128,256]{2,1,0:T(8,128)}, f32[4,128,256]{2,1,0:T(8,128)}, bf16[8,128,256]{2,1,0:T(8,128)(2,1)}, bf16[8,128,256]{2,1,0:T(8,128)(2,1)}, f32[8,128]{1,0:T(8,128)}) custom-call(s32[1]{0:T(128)} %dynamic_slice.14.length, bf16[512,1024]{1,0:T(8,128)(2,1)} %get-tuple-element.74.db_hbm, f32[256,1024]{1,0:T(8,128)} %get-tuple-element.75.dx_ref, ...), custom_call_target="tpu_custom_call" | custom-call | tf_op jit(solution)/shard_map/self_back/pallas_call | solution.py:1406
  440.0 1.3 multiply_reduce_fusion.1
  441.9 1.6 gather_fusion.2
  443.6 1.6 gather_fusion.3
  445.2 0.0 copy-done.9
  445.2 0.0 copy-start.15
  445.2 0.1 multiply_reduce_fusion
  445.3 1.5 select_convert_fusion
  446.9 0.0 copy-start.20
  446.9 0.0 copy-start.21
  447.0 1.1 mul.172
  448.1 2.3 mul.173
  450.4 1.5 reduce_sum.38
  451.9 0.6 fusion.3.g_ref
  452.5 13.1 %square_sum.1 = f32[8,128]{1,0:T(8,128)} custom-call(f32[8,128]{1,0:T(8,128)} %fusion.3.g_ref), custom_call_target="tpu_custom_call" | custom-call | tf_op jit(solution)/shard_map/square_sum/pallas_call | solution.py:1483
  465.6 1.3 reduce_sum.42
  467.7 0.6 multiply_add_fusion.4
  468.3 0.0 copy-start.12
  468.4 5.2 %multiply_add_fusion = (f32[2,128,1024]{2,1,0:T(8,128)}, f32[2,128,1024]{2,1,0:T(8,128)}, f32[2,128,1024]{2,1,0:T(8,128)}, f32[2,128,1024]{2,1,0:T(8,128)}) fusion(f32[2,128,1024]{2,1,0:T(8,128)} %param.36, f32[2,128,1024]{2,1,0:T(8,128)S(1)} %copy-done.6, f32[2,128,1024]{2,1,0:T(8,128)} %get-tuple-element.91, f32[]{:T(128)S(6)} %min.3, ...), kind=kLoop, calls=%fused_computation.8 | loop fusion | flops 4980736 | bytes 9437188 | tf_op jit(solution)/shard_map/add | solution.py:1635
  473.5 2.6 multiply_add_fusion.1
  476.2 0.8 copy.36
  (37 shorter events, 0.2 us)
Async XLA Ops:
  0.6 9.5 %copy-start = (bf16[8,128,256]{2,1,0:T(8,128)(2,1)S(1)}, bf16[8,128,256]{2,1,0:T(8,128)(2,1)}, u32[]{:S(2)}) copy-start(bf16[8,128,256]{2,1,0:T(8,128)(2,1)} %param.21) | copy-start | bytes 1572868
  0.7 14.5 %copy-start.6 = (f32[2,128,1024]{2,1,0:T(8,128)S(1)}, f32[2,128,1024]{2,1,0:T(8,128)}, u32[]{:S(2)}) copy-start(f32[2,128,1024]{2,1,0:T(8,128)} %param.27) | copy-start | bytes 3145732
  0.7 13.7 %copy-start.7 = (f32[8,128,256]{2,1,0:T(8,128)S(1)}, f32[8,128,256]{2,1,0:T(8,128)}, u32[]{:S(2)}) copy-start(f32[8,128,256]{2,1,0:T(8,128)} %param.26) | copy-start | bytes 3145732
  92.8 1.9 copy-start.2
  94.8 1.3 copy-start.3
  96.1 0.6 copy-start.5
  96.7 1.5 copy-start.4
  256.7 67.1 %copy-start.16 = (f32[8,1024]{1,0:T(8,128)S(1)}, f32[8,1024]{1,0:T(8,128)}, u32[]{:S(2)}) copy-start(f32[8,1024]{1,0:T(8,128)} %get-tuple-element.84) | copy-start | bytes 98308
  325.2 120.0 %copy-start.9 = (f32[2,128,1024]{2,1,0:T(8,128)S(1)}, f32[2,128,1024]{2,1,0:T(8,128)}, u32[]{:S(2)}) copy-start(f32[2,128,1024]{2,1,0:T(8,128)} %get-tuple-element.91) | copy-start | bytes 3145732
  445.2 1.6 copy-start.15
  445.2 1.7 copy-start.14
  446.9 20.8 %copy-start.17 = (f32[8,128]{1,0:T(8,128)S(1)}, f32[8,128]{1,0:T(8,128)}, u32[]{:S(2)}) copy-start(f32[8,128]{1,0:T(8,128)} %param.28) | copy-start | bytes 12292
  446.9 20.8 %copy-start.18 = (f32[8,128]{1,0:T(8,128)S(1)}, f32[8,128]{1,0:T(8,128)}, u32[]{:S(2)}) copy-start(f32[8,128]{1,0:T(8,128)} %get-tuple-element.92) | copy-start | bytes 12292
  446.9 20.8 %copy-start.19 = (f32[8,128]{1,0:T(8,128)S(1)}, f32[8,128]{1,0:T(8,128)}, u32[]{:S(2)}) copy-start(f32[8,128]{1,0:T(8,128)} %param.37) | copy-start | bytes 12292
  446.9 20.8 %copy-start.20 = (f32[8,128]{1,0:T(8,128)S(1)}, f32[8,128]{1,0:T(8,128)}, u32[]{:S(2)}) copy-start(f32[8,128]{1,0:T(8,128)} %param.31) | copy-start | bytes 12292
  446.9 20.8 %copy-start.21 = (f32[8,128]{1,0:T(8,128)S(1)}, f32[8,128]{1,0:T(8,128)}, u32[]{:S(2)}) copy-start(f32[8,128]{1,0:T(8,128)} %param.34) | copy-start | bytes 12292
  468.3 5.2 %copy-start.8 = (f32[8,128,256]{2,1,0:T(8,128)S(1)}, f32[8,128,256]{2,1,0:T(8,128)}, u32[]{:S(2)}) copy-start(f32[8,128,256]{2,1,0:T(8,128)} %param.26) | copy-start | bytes 3145732
  468.3 5.2 %copy-start.10 = (f32[8,128,256]{2,1,0:T(8,128)S(1)}, f32[8,128,256]{2,1,0:T(8,128)}, u32[]{:S(2)}) copy-start(f32[8,128,256]{2,1,0:T(8,128)} %param.35) | copy-start | bytes 3145732
  468.3 5.2 %copy-start.11 = (f32[8,128,256]{2,1,0:T(8,128)S(1)}, f32[8,128,256]{2,1,0:T(8,128)}, u32[]{:S(2)}) copy-start(f32[8,128,256]{2,1,0:T(8,128)} %param.29) | copy-start | bytes 3145732
  468.3 5.2 %copy-start.12 = (f32[8,128,256]{2,1,0:T(8,128)S(1)}, f32[8,128,256]{2,1,0:T(8,128)}, u32[]{:S(2)}) copy-start(f32[8,128,256]{2,1,0:T(8,128)} %param.32) | copy-start | bytes 3145732
  473.5 3.5 copy-start.1
  473.5 2.7 copy-start.13
